TPU v7x, 32 devices: a whole 2x2x4 slice. The times are simulated.
32 devices in a mesh: groups: 2 (over x), dp: 8 (over z, y), tensor: 2 (over core).
Axes of the slice: x: 2, y: 2, z: 4, core: 2. Of those that a mesh axis runs over, the one named last changes fastest.
Arguments:
- hidden_in: bfloat16 [256, 4096], P(('groups', 'dp')), parts along dimension 0, may hold values from -6 to 6
- grad_out: bfloat16 [256, 4096], P(('groups', 'dp')), parts along dimension 0, may hold values from -6 to 6
- norm_gain: float32 [4096], replicated, may hold values from 0.5 to 1.5
- gate_weight: bfloat16 [4096, 16384], P(None, ('dp', 'tensor')), may hold values from -0.09375 to 0.09375
- up_weight: bfloat16 [4096, 16384], P(None, ('dp', 'tensor')), may hold values from -0.09375 to 0.09375
- down_weight: bfloat16 [16384, 4096], P(('dp', 'tensor')), may hold values from -0.046875 to 0.046875
- tenant_basis: bfloat16 [16, 8, 4096], P(('groups', 'dp')), parts along dimension 0, may hold values from -0.09375 to 0.09375
- tenant_learned: bfloat16 [16, 8, 4096], P(('groups', 'dp')), parts along dimension 0, may hold values from -0.09375 to 0.09375
- tenant_bias: bfloat16 [16, 8], P(('groups', 'dp')), parts along dimension 0, may hold values from -4 to 4
- row_counts: int32 [16], P('groups'), parts along dimension 0, may hold values from 0 to 80, as said below
- segment_starts: int32 [16], P('groups'), parts along dimension 0, may hold values from 0 to 128, as said below
- owner_slot: int32 [16], P('groups'), parts along dimension 0, may hold values from 0 to 7, each once
Outputs:
- grad_hidden: bfloat16 [256, 4096], P(('groups', 'dp')), parts along dimension 0
- grad_basis: float32 [16, 8, 4096], P(('groups', 'dp')), parts along dimension 0
- grad_learned: float32 [16, 8, 4096], P(('groups', 'dp')), parts along dimension 0
- grad_bias: float32 [16, 8], P(('groups', 'dp')), parts along dimension 0
There are 2 independent parts, one for each index of `groups`. A program takes and returns all parts, laid end to end along the dimension named above; an argument that names none is the same for every part. Nothing has to cross between parts.
Inputs may be any that keep to these rules, and one draw needn't show every extreme that they name: Tenant segments lie in tenant order end to end over all 128 rows; tenant t covers ceil(row_counts[t] / 16) blocks of 16 rows; 4 tenants have rows, the others none; one tenant covers exactly 5 blocks and holds 80 rows. segment_starts[t] is 16 times the blocks of all tenants before t; the last tenant has no rows.
All inputs are finite; a program needn't handle non-finite values.
Results may differ from a plain program's by a relative error of at most 0.0059.
Values may be sent and summed in bfloat16 or wider, within the bound.
No kernel may reach another device: no remote copies, remote signals or barrier semaphores. Data moves between devices by JAX's collectives and lax.ppermute only.
A program may use at most 128 MiB of HBM per device.

v0:
```python
import jax
import jax.numpy as jnp
from jax import lax
from jax.sharding import PartitionSpec as P

SEG = 16


def block_plan(row_counts, segment_starts, owner_slot, first_block, block_total):
    tenant_total = segment_starts.shape[0]
    starts = (first_block + jnp.arange(block_total, dtype=jnp.int32)) * SEG
    below = (segment_starts[None, :] <= starts[:, None]).astype(jnp.int32)
    tenant_of = jnp.sum(below, axis=1) - 1
    match = tenant_of[:, None] == jnp.arange(tenant_total, dtype=jnp.int32)[None, :]
    block_start = jnp.sum(jnp.where(match, segment_starts[None, :], 0), axis=1)
    block_count = jnp.sum(jnp.where(match, row_counts[None, :], 0), axis=1)
    slots = jnp.sum(jnp.where(match, owner_slot[None, :], 0), axis=1)
    position = starts[:, None] + jnp.arange(SEG, dtype=jnp.int32)[None, :] - block_start[:, None]
    live = (position < block_count[:, None]).astype(jnp.float32)
    return (slots, live)


def intervene(rows, basis_f, learned_f, bias_f, live):
    rows_f = rows.astype(jnp.float32)
    coeffs = jnp.einsum(
        "bsd,brd->bsr", rows_f, learned_f - basis_f, precision=lax.Precision.HIGHEST
    )
    coeffs = (coeffs + bias_f[:, None, :]) * live[:, :, None]
    middle = rows_f + jnp.einsum("bsr,brd->bsd", coeffs, basis_f, precision=lax.Precision.HIGHEST)
    return (coeffs, middle.astype(jnp.bfloat16))


def hidden_terms(middle, upstream, norm_gain, gate_weight, up_weight, down_weight):
    middle_f = middle.astype(jnp.float32)
    inverse = lax.rsqrt(jnp.mean(middle_f * middle_f, axis=-1, keepdims=True) + 1e-05)
    normed = (middle_f * inverse * norm_gain).astype(jnp.bfloat16)
    gate = jnp.dot(normed, gate_weight, preferred_element_type=jnp.float32)
    upward = jnp.dot(normed, up_weight, preferred_element_type=jnp.float32)
    sigma = jax.nn.sigmoid(gate)
    back = jnp.dot(upstream, down_weight.T, preferred_element_type=jnp.float32)
    gate_grad = (back * upward * sigma * (1.0 + gate * (1.0 - sigma))).astype(jnp.bfloat16)
    up_grad = (back * gate * sigma).astype(jnp.bfloat16)
    first = jnp.dot(gate_grad, gate_weight.T, preferred_element_type=jnp.float32)
    return first + jnp.dot(up_grad, up_weight.T, preferred_element_type=jnp.float32)


def norm_back(middle, upstream, normal_grad, norm_gain):
    middle_f = middle.astype(jnp.float32)
    inverse = lax.rsqrt(jnp.mean(middle_f * middle_f, axis=-1, keepdims=True) + 1e-05)
    scaled = normal_grad * norm_gain
    inner = jnp.mean(scaled * middle_f, axis=-1, keepdims=True)
    return upstream.astype(jnp.float32) + inverse * (scaled - middle_f * inverse * inverse * inner)


def intervene_back(rows, total, coeffs, basis_f, learned_f, live):
    rows_f = rows.astype(jnp.float32)
    pulled = (
        jnp.einsum("bsd,brd->bsr", total, basis_f, precision=lax.Precision.HIGHEST)
        * live[:, :, None]
    )
    grad_rows = total + jnp.einsum(
        "bsr,brd->bsd", pulled, learned_f - basis_f, precision=lax.Precision.HIGHEST
    )
    grad_learn = jnp.einsum("bsr,bsd->brd", pulled, rows_f, precision=lax.Precision.HIGHEST)
    grad_base = (
        jnp.einsum("bsr,bsd->brd", coeffs, total, precision=lax.Precision.HIGHEST) - grad_learn
    )
    return (grad_rows.astype(jnp.bfloat16), grad_base, grad_learn, jnp.sum(pulled, axis=1))


def on_device(
    hidden_in,
    grad_out,
    norm_gain,
    gate_weight,
    up_weight,
    down_weight,
    tenant_basis,
    tenant_learned,
    tenant_bias,
    row_counts,
    segment_starts,
    owner_slot,
):
    row_total, width = hidden_in.shape
    per_device = row_total // SEG
    tenant_total = row_counts.shape[0]
    device_index = lax.axis_index("dp")
    slots, live = block_plan(
        row_counts, segment_starts, owner_slot, device_index * per_device, per_device
    )
    tables = (
        lax.all_gather(tenant_basis, "dp", axis=0, tiled=True),
        lax.all_gather(tenant_learned, "dp", axis=0, tiled=True),
        lax.all_gather(tenant_bias, "dp", axis=0, tiled=True),
    )
    pick = (slots[:, None] == jnp.arange(tenant_total, dtype=jnp.int32)[None, :]).astype(
        jnp.bfloat16
    )
    basis_f = jnp.einsum("bs,srd->brd", pick, tables[0], preferred_element_type=jnp.float32)
    learned_f = jnp.einsum("bs,srd->brd", pick, tables[1], preferred_element_type=jnp.float32)
    bias_f = jnp.dot(pick, tables[2], preferred_element_type=jnp.float32)
    rows = hidden_in.reshape(per_device, SEG, width)
    coeffs, middle = intervene(rows, basis_f, learned_f, bias_f, live)
    middle_rows = middle.reshape(row_total, width)
    all_middle, all_upstream = (
        lax.all_gather(middle_rows, "dp", axis=0, tiled=True),
        lax.all_gather(grad_out, "dp", axis=0, tiled=True),
    )
    share = lax.psum_scatter(
        hidden_terms(all_middle, all_upstream, norm_gain, gate_weight, up_weight, down_weight),
        "dp",
        scatter_dimension=0,
        tiled=True,
    )
    normal_grad = lax.psum(share, "tensor")
    total = norm_back(middle_rows, grad_out, normal_grad, norm_gain).reshape(per_device, SEG, width)
    grad_rows, grad_base, grad_learn, grad_offset = intervene_back(
        rows, total, coeffs, basis_f, learned_f, live
    )
    tenant_hot = (slots[:, None] == jnp.arange(tenant_total, dtype=jnp.int32)[None, :]).astype(
        jnp.float32
    )
    table_basis = jnp.einsum("bs,brd->srd", tenant_hot, grad_base, precision=lax.Precision.HIGHEST)
    table_learned = jnp.einsum(
        "bs,brd->srd", tenant_hot, grad_learn, precision=lax.Precision.HIGHEST
    )
    table_bias = jnp.dot(tenant_hot.T, grad_offset, precision=lax.Precision.HIGHEST)
    owned = (
        lax.psum_scatter(table_basis, "dp", scatter_dimension=0, tiled=True),
        lax.psum_scatter(table_learned, "dp", scatter_dimension=0, tiled=True),
        lax.psum_scatter(table_bias, "dp", scatter_dimension=0, tiled=True),
    )
    return (grad_rows.reshape(row_total, width), owned[0], owned[1], owned[2])


def solution(mesh):
    return jax.shard_map(
        on_device,
        mesh=mesh,
        in_specs=(
            P(("groups", "dp"), None),
            P(("groups", "dp"), None),
            P(),
            P(None, ("dp", "tensor")),
            P(None, ("dp", "tensor")),
            P(("dp", "tensor"), None),
            P(("groups", "dp"), None, None),
            P(("groups", "dp"), None, None),
            P(("groups", "dp"), None),
            P("groups"),
            P("groups"),
            P("groups"),
        ),
        out_specs=(
            P(("groups", "dp"), None),
            P(("groups", "dp"), None, None),
            P(("groups", "dp"), None, None),
            P(("groups", "dp"), None),
        ),
        check_vma=False,
    )
```

profile of v0, /device:TPU:1, one launch (start us, length us, event | category | flops | bytes accessed | tf_op | source)
XLA Modules:
  0.0 439.8 jit_solution(10643459185361765234)
XLA Ops:
  7.2 27.2 %all_gather.16 = bf16[8,8,4096]{2,1,0:T(8,128)(2,1)S(1)} all-gather(bf16[1,8,4096]{2,1,0:T(8,128)(2,1)} %param.18), channel_id=1, replica_groups=mesh['groups'=2,'dp'=8,'tensor'=2] {'dp'}, dimensions={0}, use_global_device_ids=true | all-gather | bytes 589824 | tf_op jit(solution)/shard_map/all_gather | solution.py:93
  34.4 1.3 fusion.39
  36.3 1.3 select_reduce_fusion.2
  37.6 1.3 select_reduce_fusion
  38.9 25.5 %all_gather.15 = bf16[8,8,4096]{2,1,0:T(8,128)(2,1)S(1)} all-gather(bf16[1,8,4096]{2,1,0:T(8,128)(2,1)} %param.19), channel_id=1, replica_groups=mesh['groups'=2,'dp'=8,'tensor'=2] {'dp'}, dimensions={0}, use_global_device_ids=true | all-gather | bytes 589824 | tf_op jit(solution)/shard_map/all_gather | solution.py:94
  64.4 1.3 fusion.10
  65.7 1.3 fusion.12
  67.1 15.9 %all-gather = bf16[8,1,8]{2,1,0:T(2,128)(2,1)S(1)} all-gather(bf16[1,1,8]{2,1,0:T(2,128)(2,1)} %bitcast.44), channel_id=1, replica_groups=mesh['groups'=2,'dp'=8,'tensor'=2] {'dp'}, dimensions={0}, use_global_device_ids=true | all-gather | bytes 144 | tf_op jit(solution)/shard_map/all_gather | solution.py:95
  82.9 0.8 convolution_bitcast_fusion
  83.7 1.3 compare_convert_fusion
  85.0 1.3 fusion.8
  86.3 2.0 fusion
  88.4 0.7 all-gather.4.cloned.1.call-update
  89.1 52.2 %all-gather.6.cloned.1.call-done = bf16[128,4096]{1,0:T(8,128)(2,1)} async-done(((bf16[16,4096]{1,0:T(8,128)(2,1)}), bf16[128,4096]{1,0:T(8,128)(2,1)}) %all-gather.6.cloned.1.call-update) | async-done | bytes 1048592 | tf_op jit(solution)/shard_map/all_gather | solution.py:107
  141.3 1.6 fusion.2
  142.9 39.4 %all-gather.4.cloned.1.call-done = bf16[128,4096]{1,0:T(8,128)(2,1)} async-done(((bf16[16,4096]{1,0:T(8,128)(2,1)}), bf16[128,4096]{1,0:T(8,128)(2,1)}) %all-gather.4.cloned.1.call-update) | async-done | bytes 1048592 | tf_op jit(solution)/shard_map/all_gather | solution.py:108
  182.4 7.5 %fusion.47 = f32[128,1024]{1,0:T(8,128)} fusion(bf16[128,4096]{1,0:T(8,128)(2,1)} %all-gather.4.cloned.1.call-done, bf16[1024,4096]{1,0:T(8,128)(2,1)} %param.17), kind=kOutput, calls=%fused_computation.74 | convolution fusion | flops 1073741824 | bytes 9961472 | tf_op jit(solution)/shard_map/dot_general | solution.py:40
  189.9 2.2 fusion.17
  192.2 10.3 %fusion.9 = f32[128,4096]{1,0:T(8,128)S(1)} fusion(bf16[4096,1024]{1,0:T(8,128)(2,1)} %param.15, f32[128,1024]{1,0:T(8,128)} %fusion.47, bf16[4096,1024]{1,0:T(8,128)(2,1)} %param.16, f32[128,1024]{1,0:T(8,128)} %fusion.17, bf16[128,4096]{1,0:T(8,128)(2,1)S(1)} %copy-done.1, f32[4096]{0:T(1024)S(1)} %copy-done.5, f32[128]{0:T(128)S(1)} %add_rsqrt_fusion), kind=kOutput, calls=%fused_computation.19 | convolution fusion | flops 2150891520 | bytes 20988416 | tf_op jit(solution)/shard_map/dot_general | solution.py:43
  202.5 8.0 %convolution_add_fusion = f32[128,4096]{1,0:T(8,128)} fusion(f32[128,4096]{1,0:T(8,128)S(1)} %fusion.9, bf16[4096,1024]{1,0:T(8,128)(2,1)} %param.16, f32[128,1024]{1,0:T(8,128)} %fusion.47, f32[128,1024]{1,0:T(8,128)} %fusion.17), kind=kOutput, calls=%fused_computation | convolution fusion | flops 1075052544 | bytes 13631488 | tf_op jit(solution)/shard_map/dot_general | solution.py:44
  210.6 66.3 %reduce-scatter.4.cloned.1.call-done = f32[16,4096]{1,0:T(8,128)} async-done(((f32[128,4096]{1,0:T(8,128)}), f32[16,4096]{1,0:T(8,128)}) %reduce-scatter.4.cloned.1.call-update) | async-done | bytes 262160 | tf_op jit(solution)/shard_map/reduce_scatter | solution.py:110
  276.9 0.7 fusion.40
  277.6 21.0 %all-reduce.3.cloned.1.call-done = f32[16,4096]{1,0:T(8,128)} async-done(((f32[16,4096]{1,0:T(8,128)}), f32[16,4096]{1,0:T(8,128)}) %all-reduce.3.cloned.1.call-update) | async-done | bytes 262160 | tf_op jit(solution)/shard_map/psum | solution.py:116
  298.6 1.1 fusion.21
  299.7 1.1 fusion.26
  301.8 1.6 broadcast_multiply_fusion
  304.1 0.6 dynamic-slice
  304.7 18.0 %all-reduce = f32[8,8]{1,0:T(8,128)S(1)} all-reduce(f32[8,8]{1,0:T(8,128)S(1)} %broadcast_multiply_fusion.2), channel_id=5, replica_groups=mesh['groups'=2,'dp'=8,'tensor'=2] {'dp'}, use_global_device_ids=true, to_apply=%region_12.13.clone | all-reduce | flops 64 | bytes 512
  322.8 1.2 constant_dynamic-slice_fusion
  323.9 1.1 fusion.1
  325.0 41.2 %reduce-scatter.6.cloned.1.call-done = f32[1,8,4096]{2,1,0:T(8,128)} async-done(((f32[8,8,4096]{2,1,0:T(8,128)}), f32[1,8,4096]{2,1,0:T(8,128)}) %reduce-scatter.6.cloned.1.call-update) | async-done | bytes 131088 | tf_op jit(solution)/shard_map/reduce_scatter | solution.py:130
  366.3 66.7 %reduce-scatter.8.cloned.1.call-done = f32[1,8,4096]{2,1,0:T(8,128)} async-done(((f32[8,8,4096]{2,1,0:T(8,128)}), f32[1,8,4096]{2,1,0:T(8,128)}) %reduce-scatter.8.cloned.1.call-update) | async-done | bytes 131088 | tf_op jit(solution)/shard_map/reduce_scatter | solution.py:131
  (32 shorter events, 1.9 us)
Async XLA Ops:
  7.2 182.8 %copy-start.5 = (f32[4096]{0:T(1024)S(1)}, f32[4096]{0:T(1024)}, u32[]{:S(2)}) copy-start(f32[4096]{0:T(1024)} %param.14) | copy-start | bytes 49156
  7.2 134.1 %all-gather.6.cloned.1.call-start = ((), (), s32[]{:S(2)}) async-start(), calls=%async_computation.4 | async-start | bytes 1179648 | tf_op jit(solution)/shard_map/all_gather | solution.py:107
  88.3 94.1 %all-gather.4.cloned.1.call-start = ((), (), s32[]{:S(2)}) async-start(), calls=%async_computation.3 | async-start | bytes 1179648 | tf_op jit(solution)/shard_map/all_gather | solution.py:108
  89.1 187.8 %reduce-scatter.4.cloned.1.call-start = ((), (), s32[]{:S(2)}) async-start(), calls=%async_computation.5 | async-start | bytes 2359296 | tf_op jit(solution)/shard_map/reduce_scatter | solution.py:110
  141.3 48.6 %copy-start.1 = (bf16[128,4096]{1,0:T(8,128)(2,1)S(1)}, bf16[128,4096]{1,0:T(8,128)(2,1)}, u32[]{:S(2)}) copy-start(bf16[128,4096]{1,0:T(8,128)(2,1)} %all-gather.6.cloned.1.call-done) | copy-start | bytes 3145732
  182.4 7.6 %copy-start = (bf16[4096,1024]{1,0:T(8,128)(2,1)S(1)}, bf16[4096,1024]{1,0:T(8,128)(2,1)}, u32[]{:S(2)}) copy-start(bf16[4096,1024]{1,0:T(8,128)(2,1)} %param.15) | copy-start | bytes 25165828
  202.4 96.1 %copy-start.2 = (bf16[16,4096]{1,0:T(8,128)(2,1)S(1)}, bf16[16,4096]{1,0:T(8,128)(2,1)}, u32[]{:S(2)}) copy-start(bf16[16,4096]{1,0:T(8,128)(2,1)} %fusion) | copy-start | bytes 393220
  202.4 97.3 %copy-start.4 = (bf16[16,4096]{1,0:T(8,128)(2,1)S(1)}, bf16[16,4096]{1,0:T(8,128)(2,1)}, u32[]{:S(2)}) copy-start(bf16[16,4096]{1,0:T(8,128)(2,1)} %param.13) | copy-start | bytes 393220
  202.4 98.9 %copy-start.3 = (bf16[16,4096]{1,0:T(8,128)(2,1)S(1)}, bf16[16,4096]{1,0:T(8,128)(2,1)}, u32[]{:S(2)}) copy-start(bf16[16,4096]{1,0:T(8,128)(2,1)} %param.12) | copy-start | bytes 393220
  202.5 101.6 %copy-start.6 = (u32[32]{0:T(128)S(1)}, u32[32]{0:T(128)}, u32[]{:S(2)}) copy-start(u32[32]{0:T(128)} %constant.33) | copy-start | bytes 388
  210.5 88.1 %all-reduce.3.cloned.1.call-start = ((), (), s32[]{:S(2)}) async-start(), calls=%async_computation.6 | async-start | bytes 524288 | tf_op jit(solution)/shard_map/psum | solution.py:116
  276.9 89.4 %reduce-scatter.6.cloned.1.call-start = ((), (), s32[]{:S(2)}) async-start(), calls=%async_computation.7 | async-start | bytes 1179648 | tf_op jit(solution)/shard_map/reduce_scatter | solution.py:130
  303.5 129.5 %reduce-scatter.8.cloned.1.call-start = ((), (), s32[]{:S(2)}) async-start(), calls=%async_computation.8 | async-start | bytes 1179648 | tf_op jit(solution)/shard_map/reduce_scatter | solution.py:131
Sparse Core Ops, SparseCore 0:
  88.4 52.8 all-gather.5
  143.4 38.8 all-gather.3
  210.6 66.1 reduce-scatter.3
  279.0 19.4 all-reduce.2
  303.6 62.6 reduce-scatter.5
  370.1 62.7 reduce-scatter.7
where the time goes:
time: 442 us; the launch traced here: 440 us
  waiting for transfers between devices  288 us (65%)
  blocking collectives  86.6 us (20%)
  matrix products  36.8 us (8%)
  between operations  14.9 us (3%)
  other arithmetic  11.4 us (3%)
    reduce_scatter x1, waiting for transfers between devices, on_device(): lax.psum_scatter(table_learned, 'dp', scatter_dimension=0, tiled=True)  66.7 us
    reduce_scatter x1, waiting for transfers between devices, on_device(): lax.psum_scatter(hidden_terms(all_middle, all_upstream, norm_gain, gate_w...  66.3 us
    all_gather x1, waiting for transfers between devices, on_device(): lax.all_gather(middle_rows, 'dp', axis=0, tiled=True)  52.2 us
    reduce_scatter x1, waiting for transfers between devices, on_device(): lax.psum_scatter(table_basis, 'dp', scatter_dimension=0, tiled=True)  41.2 us
    all_gather x1, waiting for transfers between devices, on_device(): lax.all_gather(grad_out, 'dp', axis=0, tiled=True)  39.4 us
    all_gather x1, blocking collectives, on_device(): lax.all_gather(tenant_basis, 'dp', axis=0, tiled=True)  27.2 us
    all_gather x1, blocking collectives, on_device(): lax.all_gather(tenant_learned, 'dp', axis=0, tiled=True)  25.5 us
    psum x1, waiting for transfers between devices, on_device(): normal_grad = lax.psum(share, 'tensor')  21 us
  transfers between devices with their start and end apart: 6, of which 6 were waited for; matrix products, arithmetic and copies ran while one was open for 1% of the time, Pallas kernels for 0%

commit v1 on v0

v1 whole, which is shorter than its diff:
```python
import functools

import jax
import jax.numpy as jnp
from jax import lax
from jax.experimental import pallas as pl
from jax.experimental.pallas import tpu as pltpu
from jax.sharding import PartitionSpec as P

SEG = 16
RANK = 8
PAD = 128
EPS = 1e-05
BF = jnp.bfloat16
F32 = jnp.float32


def dot_nn(a, b):
    return jnp.dot(a, b, preferred_element_type=F32)


def dot_nt(a, b):
    return lax.dot_general(a, b, (((1,), (1,)), ((), ())), preferred_element_type=F32)


def split(x):
    high = x.astype(BF)
    low = (x - high.astype(F32)).astype(BF)
    return high, low


def ring_order(n):
    if n == 8:
        return [0, 2, 4, 6, 7, 5, 3, 1]
    return list(range(n))


def block_kernel(
    tile,
    step,
    mask_ref,
    rows_ref,
    tables_ref,
    upstream_ref,
    gain_ref,
    gate_hbm,
    up_hbm,
    down_hbm,
    own_ref,
    own_slot_ref,
    total_ref,
    slot_ref,
    gate_ref,
    up_ref,
    down_ref,
    middle_ref,
    normed_ref,
    scaled_ref,
    gate_grad_ref,
    up_grad_ref,
    sems,
):
    row_total, width = middle_ref.shape
    hidden = gate_ref.shape[1]
    tiles = hidden // tile
    chunks = width // step
    columns = tables_ref.shape[0]

    def weight_copies(j):
        cols = pl.ds(j * tile, tile)
        return (
            pltpu.make_async_copy(gate_hbm.at[:, cols], gate_ref.at[:, cols], sems.at[0, j]),
            pltpu.make_async_copy(up_hbm.at[:, cols], up_ref.at[:, cols], sems.at[1, j]),
            pltpu.make_async_copy(down_hbm.at[cols, :], down_ref.at[cols, :], sems.at[2, j]),
        )

    for j in range(tiles):
        for copy in weight_copies(j):
            copy.start()

    mask = mask_ref[...]
    lane = lax.broadcasted_iota(jnp.int32, (row_total, columns), 1)
    products = dot_nt(rows_ref[...], tables_ref[...])
    coeffs = mask * (pltpu.roll(products, columns - RANK, 1) - products)
    coeff_high, coeff_low = split(coeffs)
    pulled_up = dot_nt(upstream_ref[...], tables_ref[:, :width])
    first_slot = jnp.where(lane < RANK, 0.5, 0.0)

    def middle_step(c, squares):
        cols = pl.ds(pl.multiple_of(c * step, step), step)
        table = tables_ref[:, cols]
        value = rows_ref[:, cols].astype(F32) + (
            dot_nn(coeff_high, table) + dot_nn(coeff_low, table)
        )
        value = value.astype(BF)
        middle_ref[:, cols] = value
        value = value.astype(F32)
        return squares + jnp.sum(value * value, axis=1, keepdims=True)

    squares = lax.fori_loop(0, chunks, middle_step, jnp.zeros((row_total, 1), F32))
    inverse = lax.rsqrt(squares / width + EPS)

    def normed_step(c, carry):
        cols = pl.ds(pl.multiple_of(c * step, step), step)
        value = middle_ref[:, cols].astype(F32) * inverse * gain_ref[:, cols]
        normed_ref[:, cols] = value.astype(BF)
        return carry

    lax.fori_loop(0, chunks, normed_step, 0)

    for j in range(tiles):
        for copy in weight_copies(j):
            copy.wait()
        cols = pl.ds(j * tile, tile)
        gate = dot_nn(normed_ref[...], gate_ref[:, cols])
        upward = dot_nn(normed_ref[...], up_ref[:, cols])
        back = dot_nt(upstream_ref[...], down_ref[cols, :])
        sigma = jax.nn.sigmoid(gate)
        gate_grad_ref[:, cols] = (back * upward * sigma * (1.0 + gate * (1.0 - sigma))).astype(BF)
        up_grad_ref[:, cols] = (back * gate * sigma).astype(BF)

    def scaled_step(c, inner):
        cols = pl.ds(pl.multiple_of(c * step, step), step)
        value = dot_nt(gate_grad_ref[...], gate_ref[cols, :])
        value = value + dot_nt(up_grad_ref[...], up_ref[cols, :])
        value = value * gain_ref[:, cols]
        scaled_ref[:, cols] = value
        return inner + jnp.sum(value * middle_ref[:, cols].astype(F32), axis=1, keepdims=True)

    inner = lax.fori_loop(0, chunks, scaled_step, jnp.zeros((row_total, 1), F32))
    shrink = inverse * inverse * (inner / width)

    def total_step(c, pulled):
        cols = pl.ds(pl.multiple_of(c * step, step), step)
        value = inverse * (scaled_ref[:, cols] - middle_ref[:, cols].astype(F32) * shrink)
        scaled_ref[:, cols] = value
        high, low = split(value)
        total_ref[:, cols] = high
        own_ref[:, cols] = value[:SEG] + 0.5 * upstream_ref[:SEG, cols].astype(F32)
        table = tables_ref[:, cols]
        return pulled + (dot_nt(high, table) + dot_nt(low, table))

    pulled = lax.fori_loop(0, chunks, total_step, jnp.zeros((row_total, columns), F32))
    pulled = mask * (pulled + first_slot * pulled_up)
    pulled = pltpu.roll(pulled, RANK, 1) - pulled
    coeff_t = coeffs.T
    first_t = (coeffs * first_slot).T
    pulled_t = pulled.T
    coeff_high, coeff_low = split(coeff_t)
    first_high, first_low = split(first_t[:SEG])
    pulled_high, pulled_low = split(pulled_t)

    def slot_step(c, carry):
        cols = pl.ds(pl.multiple_of(c * step, step), step)
        high, low = split(scaled_ref[:, cols])
        rows = rows_ref[:, cols]
        value = dot_nn(coeff_high, high) + dot_nn(coeff_high, low) + dot_nn(coeff_low, high)
        value = value + dot_nn(pulled_high, rows) + dot_nn(pulled_low, rows)
        slot_ref[:, cols] = value.astype(BF)
        upstream = upstream_ref[:, cols]
        own_slot_ref[:, cols] = value[:SEG] + (
            dot_nn(first_high, upstream) + dot_nn(first_low, upstream)
        )
        return carry

    lax.fori_loop(0, chunks, slot_step, 0)
    extra = rows_ref[:, width:]
    value = dot_nn(pulled_high, extra) + dot_nn(pulled_low, extra)
    slot_ref[:, width:] = value.astype(BF)
    own_slot_ref[:, width:] = value[:SEG]


def block(mask, rows, tables, upstream, gain, gate_weight, up_weight, down_weight):
    row_total, width = upstream.shape
    wide = rows.shape[1]
    hidden = gate_weight.shape[1]
    tile = min(256, hidden)
    tiles = hidden // tile
    vmem = pl.BlockSpec(memory_space=pltpu.VMEM)
    hbm = pl.BlockSpec(memory_space=pl.ANY)
    return pl.pallas_call(
        functools.partial(block_kernel, tile, 512),
        out_shape=(
            jax.ShapeDtypeStruct((SEG, width), F32),
            jax.ShapeDtypeStruct((SEG, wide), F32),
            jax.ShapeDtypeStruct((row_total, width), BF),
            jax.ShapeDtypeStruct((row_total, wide), BF),
        ),
        in_specs=[vmem, vmem, vmem, vmem, vmem, hbm, hbm, hbm],
        out_specs=(vmem, vmem, vmem, vmem),
        scratch_shapes=[
            pltpu.VMEM((width, hidden), BF),
            pltpu.VMEM((width, hidden), BF),
            pltpu.VMEM((hidden, width), BF),
            pltpu.VMEM((row_total, width), BF),
            pltpu.VMEM((row_total, width), BF),
            pltpu.VMEM((row_total, width), F32),
            pltpu.VMEM((row_total, hidden), BF),
            pltpu.VMEM((row_total, hidden), BF),
            pltpu.SemaphoreType.DMA((3, tiles)),
        ],
        compiler_params=pltpu.CompilerParams(vmem_limit_bytes=58 * 1024 * 1024),
        cost_estimate=pl.CostEstimate(
            flops=10 * row_total * width * hidden,
            bytes_accessed=6 * width * hidden,
            transcendentals=row_total * hidden,
        ),
    )(mask, rows, tables, upstream, gain, gate_weight, up_weight, down_weight)


def plan(row_counts, segment_starts, owner_slot, blocks, own_slots):
    starts = blocks * SEG
    tenant_total = segment_starts.shape[0]
    tenant_of = jnp.sum((segment_starts[None, :] <= starts[:, None]).astype(jnp.int32), axis=1) - 1
    match = tenant_of[:, None] == jnp.arange(tenant_total, dtype=jnp.int32)[None, :]
    block_start = jnp.sum(jnp.where(match, segment_starts[None, :], 0), axis=1)
    block_count = jnp.sum(jnp.where(match, row_counts[None, :], 0), axis=1)
    slots = jnp.sum(jnp.where(match, owner_slot[None, :], 0), axis=1)
    position = starts[:, None] + jnp.arange(SEG, dtype=jnp.int32)[None, :] - block_start[:, None]
    live = (position < block_count[:, None]).astype(F32)
    pick = slots[:, None] == own_slots[None, :]
    mask = live[:, :, None] * pick[:, None, :].astype(F32)
    return live, pick, mask.reshape(-1, own_slots.shape[0])


def make_device_function(n):
    order = ring_order(n)
    place = {d: k for k, d in enumerate(order)}
    half = n // 2 - 1
    pairs = []
    for d in range(n):
        pairs.append((d * 2, order[(place[d] + 1) % n] * 2))
        pairs.append((d * 2 + 1, order[(place[d] - 1) % n] * 2 + 1))

    def hop(x):
        return lax.ppermute(x, ("dp", "tensor"), pairs)

    def swap(x):
        return lax.ppermute(x, "tensor", [(0, 1), (1, 0)])

    def on_device(
        hidden_in,
        grad_out,
        norm_gain,
        gate_weight,
        up_weight,
        down_weight,
        tenant_basis,
        tenant_learned,
        tenant_bias,
        row_counts,
        segment_starts,
        owner_slot,
    ):
        width = hidden_in.shape[1]
        ones = jnp.zeros((SEG, PAD), BF).at[:, 0].set(1)
        bias = jnp.pad(
            tenant_bias.reshape(RANK, 1), ((RANK, 0), (0, PAD - 1))
        )
        packed = jnp.concatenate(
            [
                jnp.concatenate([hidden_in, tenant_basis[0], tenant_learned[0]], axis=0),
                jnp.concatenate([ones, bias], axis=0),
            ],
            axis=1,
        )
        first, second = packed, grad_out
        ahead, behind = [], []
        for _ in range(half):
            first, second = hop(first), hop(second)
            ahead.append((first, second))
            behind.append((swap(first), swap(second)))
        pieces = [(packed, grad_out)] + ahead + behind + [(hop(first), hop(second))]
        rows = jnp.concatenate([a[:SEG] for a, _ in pieces], axis=0)
        tables = jnp.concatenate([a[SEG:] for a, _ in pieces], axis=0)
        upstream = jnp.concatenate([b for _, b in pieces], axis=0)

        core = lax.axis_index("tensor")
        me = jnp.array([place[d] for d in range(n)], jnp.int32)[lax.axis_index("dp")]
        away = jnp.array(
            [0] + [-t for t in range(1, half + 1)] + [t for t in range(1, half + 1)] + [n // 2],
            jnp.int32,
        )
        away = jnp.where(core == 0, away, -away)
        index = jnp.array(order, jnp.int32)[(me + away + n) % n]
        live, pick, mask = plan(row_counts, segment_starts, owner_slot, index, index)
        mask = jnp.repeat(mask, 2 * RANK, axis=1)
        column = jnp.arange(mask.shape[1], dtype=jnp.int32)
        mask = jnp.where(column[None, :] % (2 * RANK) < RANK, mask, 0.0)

        own, own_slot, total, slot = block(
            mask,
            rows,
            tables,
            upstream,
            norm_gain.reshape(1, width),
            gate_weight,
            up_weight,
            down_weight,
        )

        sent = slice(SEG, SEG * (1 + half))
        kept = SEG * (1 + half)
        far = SEG * (1 + 2 * half)
        results = []
        parts = []
        for value in (slot, total):
            parts.append((value, hop(value[far:]), swap(value[sent])))
        state = [p[1] for p in parts]
        for t in range(half - 1, -1, -1):
            for k, (value, _, other) in enumerate(parts):
                mine = value[kept + t * SEG : kept + (t + 1) * SEG].astype(F32)
                partner = other[t * SEG : (t + 1) * SEG].astype(F32)
                state[k] = hop((state[k].astype(F32) + (mine + partner)).astype(BF))
        for local, value in ((own_slot, state[0]), (own, state[1])):
            value = local + value.astype(F32)
            results.append(value + swap(value))
        slots, total = results

        which = jnp.sum(jnp.where(pick[0], jnp.arange(n, dtype=jnp.int32), 0))
        table = lax.dynamic_slice_in_dim(tables, which * SEG, SEG, 0)[:, :width].astype(F32)
        basis, learned = table[:RANK], table[RANK:]
        pulled = (
            lax.dot_general(
                total, basis, (((1,), (1,)), ((), ())), precision=lax.Precision.HIGHEST
            )
            * live[0][:, None]
        )
        grad_rows = total + jnp.dot(pulled, learned - basis, precision=lax.Precision.HIGHEST)
        return (
            grad_rows.astype(BF),
            slots[None, :RANK, :width],
            slots[None, RANK:, :width],
            slots[None, RANK:, width],
        )

    return on_device


def solution(mesh):
    return jax.shard_map(
        make_device_function(mesh.shape["dp"]),
        mesh=mesh,
        in_specs=(
            P(("groups", "dp"), None),
            P(("groups", "dp"), None),
            P(),
            P(None, ("dp", "tensor")),
            P(None, ("dp", "tensor")),
            P(("dp", "tensor"), None),
            P(("groups", "dp"), None, None),
            P(("groups", "dp"), None, None),
            P(("groups", "dp"), None),
            P("groups"),
            P("groups"),
            P("groups"),
        ),
        out_specs=(
            P(("groups", "dp"), None),
            P(("groups", "dp"), None, None),
            P(("groups", "dp"), None, None),
            P(("groups", "dp"), None),
        ),
        check_vma=False,
    )
```

time: 442 us -> 105 us (0.24)
  waiting for transfers between devices: 288 us -> 23.2 us
  blocking collectives: 86.6 us -> 0 us
  matrix products: 36.8 us -> 2.21 us
  starting transfers between devices: 0.24 us -> 29.9 us
  Pallas kernels: 0 us -> 25.8 us
  between operations: 14.9 us -> 2.34 us
  local copies, waits for them, and re-layouts: 1.78 us -> 11.7 us
    reduce_scatter x3 -> x0, waiting for transfers between devices: 174 us -> none  [the longest x1 66.7 us: on_device(): lax.psum_scatter(table_learned, 'dp', scatter_dimension=0, tiled=True)]
    all_gather x2 -> x0, waiting for transfers between devices: 91.6 us -> none  [the longest x1 52.2 us: on_device(): lax.all_gather(middle_rows, 'dp', axis=0, tiled=True)]
    all_gather x3 -> x0, blocking collectives: 68.5 us -> none  [the longest x1 27.2 us: on_device(): lax.all_gather(tenant_basis, 'dp', axis=0, tiled=True)]
    dot_general x13 -> x2, matrix products: 36.8 us -> 2.21 us  [the longest x1 1.12 us: on_device(): jnp.dot(pulled, learned - basis, precision=lax.Precision.HIGHEST)]
    ppermute x0 -> x26, starting transfers between devices: none -> 29.9 us  [the longest x10 21 us: swap(): return lax.ppermute(x, 'tensor', [(0, 1), (1, 0)])]
    pallas_call x0 -> x1, Pallas kernels: none -> 25.8 us  [block(): pl.pallas_call(functools.partial(block_kernel, tile, 512), out_shape=(jax...]
    ppermute x0 -> x26, waiting for transfers between devices: none -> 23.2 us  [the longest x16 21.6 us: hop(): return lax.ppermute(x, ('dp', 'tensor'), pairs)]
    psum x1 -> x0, waiting for transfers between devices: 21 us -> none  [on_device(): normal_grad = lax.psum(share, 'tensor')]
  transfers between devices with their start and end apart: 6 -> 26, of which waited for: 6 -> 12; matrix products, arithmetic and copies ran while one was open for 1% -> 15% of each run, Pallas kernels for 0% -> 0%
where the time goes in v1:
time: 105 us
  starting transfers between devices  29.9 us (28%)
  Pallas kernels  25.8 us (25%)
  waiting for transfers between devices  23.2 us (22%)
  local copies, waits for them, and re-layouts  11.7 us (11%)
  other arithmetic  9.38 us (9%)
  between operations  2.34 us (2%)
  matrix products  2.21 us (2%)
    pallas_call x1, Pallas kernels, block(): pl.pallas_call(functools.partial(block_kernel, tile, 512), out_shape=(jax...  25.8 us
    ppermute x16, waiting for transfers between devices, hop(): return lax.ppermute(x, ('dp', 'tensor'), pairs)  21.6 us
    ppermute x10, starting transfers between devices, swap(): return lax.ppermute(x, 'tensor', [(0, 1), (1, 0)])  21 us
    ppermute x16, starting transfers between devices, hop(): return lax.ppermute(x, ('dp', 'tensor'), pairs)  8.84 us
    unnamed x40, local copies, waits for them, and re-layouts  4.43 us
    convert_element_type x6, other arithmetic, on_device(): state[k] = hop((state[k].astype(F32) + (mine + partner)).astype(BF))  3.04 us
  transfers between devices with their start and end apart: 26, of which 12 were waited for; matrix products, arithmetic and copies ran while one was open for 15% of the time, Pallas kernels for 0%

profile of v1, /device:TPU:1, one launch (start us, length us, event | category | flops | bytes accessed | tf_op | source)
XLA Modules:
  0.0 104.6 jit_solution(8070377866354306506)
XLA Ops:
  2.8 1.0 fusion.5
  3.8 2.1 %collective-permute-start = (bf16[32,4224]{1,0:T(8,128)(2,1)S(1)}, bf16[32,4224]{1,0:T(8,128)(2,1)}, u32[]{:S(2)}, u32[]{:S(2)}) collective-permute-start(bf16[32,4224]{1,0:T(8,128)(2,1)S(1)} %fusion.5), channel_id=1, source_target_pairs={{0,4},{1,3},{2,0},{3,7},{4,8},{5,1},{6,2},{7,11},{8,12},{9,5},{10,... | collective-permute-start | bytes 811016 | tf_op jit(solution)/shard_map/ppermute | solution.py:236
  5.9 1.3 %collective-permute-start.7 = (bf16[16,4096]{1,0:T(8,128)(2,1)}, bf16[16,4096]{1,0:T(8,128)(2,1)}, u32[]{:S(2)}, u32[]{:S(2)}) collective-permute-start(bf16[16,4096]{1,0:T(8,128)(2,1)} %param.18), channel_id=1, source_target_pairs={{0,4},{1,3},{2,0},{3,7},{4,8},{5,1},{6,2},{7,11},{8,12},{9,5},{10,... | collective-permute-start | bytes 393224 | tf_op jit(solution)/shard_map/ppermute | solution.py:236
  12.1 0.9 copy.24
  14.4 1.3 %broadcast_select_fusion.mask_ref = f32[128,128]{1,0:T(8,128)} fusion(f32[128,128]{1,0:T(8,128)S(1)} %copy.24, pred[128]{0:T(512)(128)(4,1)} %fusion.11), kind=kLoop, calls=%fused_computation.50 | loop fusion | flops 16384 | bytes 131200 | tf_op jit(solution)/shard_map/jit(_where)/select_n | solution.py:289
  15.7 1.3 %collective-permute-start.8 = (bf16[16,4096]{1,0:T(8,128)(2,1)}, bf16[16,4096]{1,0:T(8,128)(2,1)S(1)}, u32[]{:S(2)}, u32[]{:S(2)}) collective-permute-start(bf16[16,4096]{1,0:T(8,128)(2,1)} %collective-permute-done.7), channel_id=1, source_target_pairs={{0,4},{1,3},{2,0},{3,7},{4,8},{5,1},{6,2},{7,11},{8,12},{9,5},{10,... | collective-permute-start | bytes 393224 | tf_op jit(solution)/shard_map/ppermute | solution.py:236
  17.0 1.6 %collective-permute-start.10 = (bf16[16,4096]{1,0:T(8,128)(2,1)}, bf16[16,4096]{1,0:T(8,128)(2,1)S(1)}, u32[]{:S(2)}, u32[]{:S(2)}) collective-permute-start(bf16[16,4096]{1,0:T(8,128)(2,1)} %collective-permute-done.7), channel_id=1, source_target_pairs={{0,1},{1,0},{2,3},{3,2},{4,5},{5,4},{6,7},{7,6},{8,9},{9,8},{10,11... | collective-permute-start | bytes 393224 | tf_op jit(solution)/shard_map/ppermute | solution.py:239
  19.7 1.6 %collective-permute-start.9 = (bf16[16,4096]{1,0:T(8,128)(2,1)S(1)}, bf16[16,4096]{1,0:T(8,128)(2,1)S(1)}, u32[]{:S(2)}, u32[]{:S(2)}) collective-permute-start(bf16[16,4096]{1,0:T(8,128)(2,1)S(1)} %collective-permute-done.8), channel_id=1, source_target_pairs={{0,4},{1,3},{2,0},{3,7},{4,8},{5,1},{6,2},{7,11},{8,12},{9,5},{10,... | collective-permute-start | bytes 393224 | tf_op jit(solution)/shard_map/ppermute | solution.py:236
  21.3 2.4 %collective-permute-start.11 = (bf16[16,4096]{1,0:T(8,128)(2,1)S(1)}, bf16[16,4096]{1,0:T(8,128)(2,1)S(1)}, u32[]{:S(2)}, u32[]{:S(2)}) collective-permute-start(bf16[16,4096]{1,0:T(8,128)(2,1)S(1)} %collective-permute-done.8), channel_id=1, source_target_pairs={{0,1},{1,0},{2,3},{3,2},{4,5},{5,4},{6,7},{7,6},{8,9},{9,8},{10,11... | collective-permute-start | bytes 393224 | tf_op jit(solution)/shard_map/ppermute | solution.py:239
  24.0 1.4 %collective-permute-start.3 = (bf16[32,4224]{1,0:T(8,128)(2,1)}, bf16[32,4224]{1,0:T(8,128)(2,1)S(1)}, u32[]{:S(2)}, u32[]{:S(2)}) collective-permute-start(bf16[32,4224]{1,0:T(8,128)(2,1)} %collective-permute-done), channel_id=1, source_target_pairs={{0,1},{1,0},{2,3},{3,2},{4,5},{5,4},{6,7},{7,6},{8,9},{9,8},{10,11... | collective-permute-start | bytes 811016 | tf_op jit(solution)/shard_map/ppermute | solution.py:239
  25.3 1.0 slice_dynamic-update-slice_fusion.6
  28.1 3.2 %collective-permute-done.13 = bf16[16,4096]{1,0:T(8,128)(2,1)S(1)} collective-permute-done((bf16[16,4096]{1,0:T(8,128)(2,1)S(1)}, bf16[16,4096]{1,0:T(8,128)(2,1)S(1)}, u32[]{:S(2)}, u32[]{:S(2)}) %collective-permute-start.13) | collective-permute-done | bytes 131104 | tf_op jit(solution)/shard_map/ppermute | solution.py:236
  31.6 2.3 %collective-permute-start.4 = (bf16[32,4224]{1,0:T(8,128)(2,1)S(1)}, bf16[32,4224]{1,0:T(8,128)(2,1)S(1)}, u32[]{:S(2)}, u32[]{:S(2)}) collective-permute-start(bf16[32,4224]{1,0:T(8,128)(2,1)S(1)} %collective-permute-done.1), channel_id=1, source_target_pairs={{0,1},{1,0},{2,3},{3,2},{4,5},{5,4},{6,7},{7,6},{8,9},{9,8},{10,11... | collective-permute-start | bytes 811016 | tf_op jit(solution)/shard_map/ppermute | solution.py:239
  33.8 3.1 %collective-permute-done.2 = bf16[32,4224]{1,0:T(8,128)(2,1)S(1)} collective-permute-done((bf16[32,4224]{1,0:T(8,128)(2,1)S(1)}, bf16[32,4224]{1,0:T(8,128)(2,1)S(1)}, u32[]{:S(2)}, u32[]{:S(2)}) %collective-permute-start.2) | collective-permute-done | bytes 270368 | tf_op jit(solution)/shard_map/ppermute | solution.py:236
  37.0 1.7 %collective-permute-start.5 = (bf16[32,4224]{1,0:T(8,128)(2,1)S(1)}, bf16[32,4224]{1,0:T(8,128)(2,1)S(1)}, u32[]{:S(2)}, u32[]{:S(2)}) collective-permute-start(bf16[32,4224]{1,0:T(8,128)(2,1)S(1)} %collective-permute-done.2), channel_id=1, source_target_pairs={{0,1},{1,0},{2,3},{3,2},{4,5},{5,4},{6,7},{7,6},{8,9},{9,8},{10,11... | collective-permute-start | bytes 811016 | tf_op jit(solution)/shard_map/ppermute | solution.py:239
  39.9 4.4 %collective-permute-done.6 = bf16[32,4224]{1,0:T(8,128)(2,1)S(1)} collective-permute-done((bf16[32,4224]{1,0:T(8,128)(2,1)S(1)}, bf16[32,4224]{1,0:T(8,128)(2,1)S(1)}, u32[]{:S(2)}, u32[]{:S(2)}) %collective-permute-start.6) | collective-permute-done | bytes 270368 | tf_op jit(solution)/shard_map/ppermute | solution.py:236
  44.4 1.0 copy-done.1
  45.7 25.8 %shard_map.174 = (f32[16,4096]{1,0:T(8,128)}, f32[16,4224]{1,0:T(8,128)}, bf16[128,4096]{1,0:T(8,128)(2,1)}, bf16[128,4224]{1,0:T(8,128)(2,1)}) custom-call(f32[128,128]{1,0:T(8,128)} %broadcast_select_fusion.mask_ref, bf16[128,4224]{1,0:T(8,128)(2,1)} %copy-done.2, bf16[128,4224]{1,0:T(8,128)(2,1)} %copy-done.1, bf16[128,4096]{1,0:T(8,128)(2,1)} %copy-done.3, ...), custom_call_target="tpu_custom_call" | custom-call | flops 5368709120 | bytes 25165824 | tf_op jit(solution)/shard_map/pallas_call | solution.py:181
  71.5 1.1 %slice.170 = bf16[48,4224]{1,0:T(8,128)(2,1)S(1)} slice(bf16[128,4224]{1,0:T(8,128)(2,1)} %get-tuple-element.23), slice={[16:64], [0:4224]} | slice | bytes 811008 | tf_op jit(solution)/shard_map/slice | solution.py:308
  74.7 1.5 %collective-permute-start.15 = (bf16[48,4096]{1,0:T(8,128)(2,1)S(1)}, bf16[48,4096]{1,0:T(8,128)(2,1)S(1)}, u32[]{:S(2)}, u32[]{:S(2)}) collective-permute-start(bf16[48,4096]{1,0:T(8,128)(2,1)S(1)} %slice.156), channel_id=1, source_target_pairs={{0,1},{1,0},{2,3},{3,2},{4,5},{5,4},{6,7},{7,6},{8,9},{9,8},{10,11... | collective-permute-start | bytes 1179656 | tf_op jit(solution)/shard_map/ppermute | solution.py:239
  77.3 3.0 %collective-permute-done.14 = bf16[16,4096]{1,0:T(8,128)(2,1)S(1)} collective-permute-done((bf16[16,4096]{1,0:T(8,128)(2,1)S(1)}, bf16[16,4096]{1,0:T(8,128)(2,1)S(1)}, u32[]{:S(2)}, u32[]{:S(2)}) %collective-permute-start.14) | collective-permute-done | bytes 131104 | tf_op jit(solution)/shard_map/ppermute | solution.py:236
  80.6 1.0 add_convert_fusion.2
  81.8 2.7 %collective-permute-done.16 = bf16[16,4096]{1,0:T(8,128)(2,1)S(1)} collective-permute-done((bf16[16,4096]{1,0:T(8,128)(2,1)S(1)}, bf16[16,4096]{1,0:T(8,128)(2,1)S(1)}, u32[]{:S(2)}, u32[]{:S(2)}) %collective-permute-start.16) | collective-permute-done | bytes 131104 | tf_op jit(solution)/shard_map/ppermute | solution.py:236
  84.8 1.0 collective-permute-done.22
  85.8 1.0 add_convert_fusion.1
  87.0 1.4 %collective-permute-done.17 = bf16[16,4096]{1,0:T(8,128)(2,1)S(1)} collective-permute-done((bf16[16,4096]{1,0:T(8,128)(2,1)S(1)}, bf16[16,4096]{1,0:T(8,128)(2,1)S(1)}, u32[]{:S(2)}, u32[]{:S(2)}) %collective-permute-start.17) | collective-permute-done | bytes 131104 | tf_op jit(solution)/shard_map/ppermute | solution.py:236
  88.8 2.1 %collective-permute-done.23 = bf16[16,4224]{1,0:T(8,128)(2,1)S(1)} collective-permute-done((bf16[16,4224]{1,0:T(8,128)(2,1)S(1)}, bf16[16,4224]{1,0:T(8,128)(2,1)S(1)}, u32[]{:S(2)}, u32[]{:S(2)}) %collective-permute-start.23) | collective-permute-done | bytes 135200 | tf_op jit(solution)/shard_map/ppermute | solution.py:236
  90.9 1.0 add_convert_fusion
  92.4 5.0 %collective-permute-start.19 = (f32[16,4096]{1,0:T(8,128)S(1)}, f32[16,4096]{1,0:T(8,128)S(1)}, u32[]{:S(2)}, u32[]{:S(2)}) collective-permute-start(f32[16,4096]{1,0:T(8,128)S(1)} %convert_add_fusion.1), channel_id=1, source_target_pairs={{0,1},{1,0},{2,3},{3,2},{4,5},{5,4},{6,7},{7,6},{8,9},{9,8},{10,11... | collective-permute-start | bytes 786440 | tf_op jit(solution)/shard_map/ppermute | solution.py:239
  97.5 3.5 %collective-permute-start.25 = (f32[16,4224]{1,0:T(8,128)S(1)}, f32[16,4224]{1,0:T(8,128)S(1)}, u32[]{:S(2)}, u32[]{:S(2)}) collective-permute-start(f32[16,4224]{1,0:T(8,128)S(1)} %convert_add_fusion), channel_id=1, source_target_pairs={{0,1},{1,0},{2,3},{3,2},{4,5},{5,4},{6,7},{7,6},{8,9},{9,8},{10,11... | collective-permute-start | bytes 811016 | tf_op jit(solution)/shard_map/ppermute | solution.py:239
  101.0 1.1 %convolution_multiply_fusion = f32[16,8]{0,1:T(8,128)S(1)} fusion(f32[16,4096]{1,0:T(8,128)S(1)} %convert_add_fusion.1, f32[16,4096]{1,0:T(8,128)S(1)} %collective-permute-done.19, bf16[128,4224]{1,0:T(8,128)(2,1)} %copy-done.1, s32[]{:T(128)S(6)} %select_n.64, f32[16]{0:T(128)S(1)} %fusion.12), kind=kOutput, calls=%fused_computation.3 | convolution fusion | flops 6357120 | bytes 590404 | tf_op jit(solution)/shard_map/dot_general | solution.py:324
  102.1 1.1 %fusion = bf16[16,4096]{1,0:T(8,128)(2,1)} fusion(f32[16,8]{0,1:T(8,128)S(1)} %convolution_multiply_fusion, f32[16,4096]{1,0:T(8,128)S(1)} %dynamic-slice_convert_fusion, f32[16,4096]{1,0:T(8,128)S(1)} %convert_add_fusion.1, f32[16,4096]{1,0:T(8,128)S(1)} %collective-permute-done.19), kind=kOutput, calls=%fused_computation.2 | convolution fusion | flops 6520832 | bytes 918016 | tf_op jit(solution)/shard_map/dot_general | solution.py:329
  (107 shorter events, 18.3 us)
Async XLA Ops:
  0.7 9.3 %copy-start = (s32[8]{0:T(128)S(1)}, s32[8]{0:T(128)}, u32[]{:S(2)}) copy-start(s32[8]{0:T(128)} %constant.91.clone) | copy-start | bytes 100
  0.7 9.9 %copy-start.7 = (s32[8]{0:T(128)S(1)}, s32[8]{0:T(128)}, u32[]{:S(2)}) copy-start(s32[8]{0:T(128)} %param.27) | copy-start | bytes 100
  0.7 10.1 %copy-start.9 = (s32[8]{0:T(128)S(1)}, s32[8]{0:T(128)}, u32[]{:S(2)}) copy-start(s32[8]{0:T(128)} %param.26) | copy-start | bytes 100
  0.7 10.1 %copy-start.8 = (s32[8]{0:T(128)S(1)}, s32[8]{0:T(128)}, u32[]{:S(2)}) copy-start(s32[8]{0:T(128)} %param.28) | copy-start | bytes 100
  3.8 20.0 %collective-permute-start = (bf16[32,4224]{1,0:T(8,128)(2,1)S(1)}, bf16[32,4224]{1,0:T(8,128)(2,1)}, u32[]{:S(2)}, u32[]{:S(2)}) collective-permute-start(bf16[32,4224]{1,0:T(8,128)(2,1)S(1)} %fusion.5), channel_id=1, source_target_pairs={{0,4},{1,3},{2,0},{3,7},{4,8},{5,1},{6,2},{7,11},{8,12},{9,5},{10,... | collective-permute-start | bytes 811016 | tf_op jit(solution)/shard_map/ppermute | solution.py:236
  5.9 9.8 %collective-permute-start.7 = (bf16[16,4096]{1,0:T(8,128)(2,1)}, bf16[16,4096]{1,0:T(8,128)(2,1)}, u32[]{:S(2)}, u32[]{:S(2)}) collective-permute-start(bf16[16,4096]{1,0:T(8,128)(2,1)} %param.18), channel_id=1, source_target_pairs={{0,4},{1,3},{2,0},{3,7},{4,8},{5,1},{6,2},{7,11},{8,12},{9,5},{10,... | collective-permute-start | bytes 393224 | tf_op jit(solution)/shard_map/ppermute | solution.py:236
  15.7 4.0 %collective-permute-start.8 = (bf16[16,4096]{1,0:T(8,128)(2,1)}, bf16[16,4096]{1,0:T(8,128)(2,1)S(1)}, u32[]{:S(2)}, u32[]{:S(2)}) collective-permute-start(bf16[16,4096]{1,0:T(8,128)(2,1)} %collective-permute-done.7), channel_id=1, source_target_pairs={{0,4},{1,3},{2,0},{3,7},{4,8},{5,1},{6,2},{7,11},{8,12},{9,5},{10,... | collective-permute-start | bytes 393224 | tf_op jit(solution)/shard_map/ppermute | solution.py:236
  17.0 10.2 %collective-permute-start.10 = (bf16[16,4096]{1,0:T(8,128)(2,1)}, bf16[16,4096]{1,0:T(8,128)(2,1)S(1)}, u32[]{:S(2)}, u32[]{:S(2)}) collective-permute-start(bf16[16,4096]{1,0:T(8,128)(2,1)} %collective-permute-done.7), channel_id=1, source_target_pairs={{0,1},{1,0},{2,3},{3,2},{4,5},{5,4},{6,7},{7,6},{8,9},{9,8},{10,11... | collective-permute-start | bytes 393224 | tf_op jit(solution)/shard_map/ppermute | solution.py:239
  19.7 6.6 %collective-permute-start.9 = (bf16[16,4096]{1,0:T(8,128)(2,1)S(1)}, bf16[16,4096]{1,0:T(8,128)(2,1)S(1)}, u32[]{:S(2)}, u32[]{:S(2)}) collective-permute-start(bf16[16,4096]{1,0:T(8,128)(2,1)S(1)} %collective-permute-done.8), channel_id=1, source_target_pairs={{0,4},{1,3},{2,0},{3,7},{4,8},{5,1},{6,2},{7,11},{8,12},{9,5},{10,... | collective-permute-start | bytes 393224 | tf_op jit(solution)/shard_map/ppermute | solution.py:236
  21.3 6.1 %collective-permute-start.11 = (bf16[16,4096]{1,0:T(8,128)(2,1)S(1)}, bf16[16,4096]{1,0:T(8,128)(2,1)S(1)}, u32[]{:S(2)}, u32[]{:S(2)}) collective-permute-start(bf16[16,4096]{1,0:T(8,128)(2,1)S(1)} %collective-permute-done.8), channel_id=1, source_target_pairs={{0,1},{1,0},{2,3},{3,2},{4,5},{5,4},{6,7},{7,6},{8,9},{9,8},{10,11... | collective-permute-start | bytes 393224 | tf_op jit(solution)/shard_map/ppermute | solution.py:239
  23.7 7.6 %collective-permute-start.1 = (bf16[32,4224]{1,0:T(8,128)(2,1)}, bf16[32,4224]{1,0:T(8,128)(2,1)S(1)}, u32[]{:S(2)}, u32[]{:S(2)}) collective-permute-start(bf16[32,4224]{1,0:T(8,128)(2,1)} %collective-permute-done), channel_id=1, source_target_pairs={{0,4},{1,3},{2,0},{3,7},{4,8},{5,1},{6,2},{7,11},{8,12},{9,5},{10,... | collective-permute-start | bytes 811016 | tf_op jit(solution)/shard_map/ppermute | solution.py:236
  24.0 14.9 %collective-permute-start.3 = (bf16[32,4224]{1,0:T(8,128)(2,1)}, bf16[32,4224]{1,0:T(8,128)(2,1)S(1)}, u32[]{:S(2)}, u32[]{:S(2)}) collective-permute-start(bf16[32,4224]{1,0:T(8,128)(2,1)} %collective-permute-done), channel_id=1, source_target_pairs={{0,1},{1,0},{2,3},{3,2},{4,5},{5,4},{6,7},{7,6},{8,9},{9,8},{10,11... | collective-permute-start | bytes 811016 | tf_op jit(solution)/shard_map/ppermute | solution.py:239
  26.3 1.8 %collective-permute-start.12 = (bf16[16,4096]{1,0:T(8,128)(2,1)S(1)}, bf16[16,4096]{1,0:T(8,128)(2,1)S(1)}, u32[]{:S(2)}, u32[]{:S(2)}) collective-permute-start(bf16[16,4096]{1,0:T(8,128)(2,1)S(1)} %collective-permute-done.9), channel_id=1, source_target_pairs={{0,1},{1,0},{2,3},{3,2},{4,5},{5,4},{6,7},{7,6},{8,9},{9,8},{10,11... | collective-permute-start | bytes 393224 | tf_op jit(solution)/shard_map/ppermute | solution.py:239
  27.1 4.2 %collective-permute-start.13 = (bf16[16,4096]{1,0:T(8,128)(2,1)S(1)}, bf16[16,4096]{1,0:T(8,128)(2,1)S(1)}, u32[]{:S(2)}, u32[]{:S(2)}) collective-permute-start(bf16[16,4096]{1,0:T(8,128)(2,1)S(1)} %collective-permute-done.9), channel_id=1, source_target_pairs={{0,4},{1,3},{2,0},{3,7},{4,8},{5,1},{6,2},{7,11},{8,12},{9,5},{10,... | collective-permute-start | bytes 393224 | tf_op jit(solution)/shard_map/ppermute | solution.py:236
  31.3 5.7 %collective-permute-start.2 = (bf16[32,4224]{1,0:T(8,128)(2,1)S(1)}, bf16[32,4224]{1,0:T(8,128)(2,1)S(1)}, u32[]{:S(2)}, u32[]{:S(2)}) collective-permute-start(bf16[32,4224]{1,0:T(8,128)(2,1)S(1)} %collective-permute-done.1), channel_id=1, source_target_pairs={{0,4},{1,3},{2,0},{3,7},{4,8},{5,1},{6,2},{7,11},{8,12},{9,5},{10,... | collective-permute-start | bytes 811016 | tf_op jit(solution)/shard_map/ppermute | solution.py:236
  31.6 7.4 %collective-permute-start.4 = (bf16[32,4224]{1,0:T(8,128)(2,1)S(1)}, bf16[32,4224]{1,0:T(8,128)(2,1)S(1)}, u32[]{:S(2)}, u32[]{:S(2)}) collective-permute-start(bf16[32,4224]{1,0:T(8,128)(2,1)S(1)} %collective-permute-done.1), channel_id=1, source_target_pairs={{0,1},{1,0},{2,3},{3,2},{4,5},{5,4},{6,7},{7,6},{8,9},{9,8},{10,11... | collective-permute-start | bytes 811016 | tf_op jit(solution)/shard_map/ppermute | solution.py:239
  37.0 2.9 %collective-permute-start.5 = (bf16[32,4224]{1,0:T(8,128)(2,1)S(1)}, bf16[32,4224]{1,0:T(8,128)(2,1)S(1)}, u32[]{:S(2)}, u32[]{:S(2)}) collective-permute-start(bf16[32,4224]{1,0:T(8,128)(2,1)S(1)} %collective-permute-done.2), channel_id=1, source_target_pairs={{0,1},{1,0},{2,3},{3,2},{4,5},{5,4},{6,7},{7,6},{8,9},{9,8},{10,11... | collective-permute-start | bytes 811016 | tf_op jit(solution)/shard_map/ppermute | solution.py:239
  38.7 5.6 %collective-permute-start.6 = (bf16[32,4224]{1,0:T(8,128)(2,1)S(1)}, bf16[32,4224]{1,0:T(8,128)(2,1)S(1)}, u32[]{:S(2)}, u32[]{:S(2)}) collective-permute-start(bf16[32,4224]{1,0:T(8,128)(2,1)S(1)} %collective-permute-done.2), channel_id=1, source_target_pairs={{0,4},{1,3},{2,0},{3,7},{4,8},{5,1},{6,2},{7,11},{8,12},{9,5},{10,... | collective-permute-start | bytes 811016 | tf_op jit(solution)/shard_map/ppermute | solution.py:236
  73.6 7.0 %collective-permute-start.21 = (bf16[48,4224]{1,0:T(8,128)(2,1)S(1)}, bf16[48,4224]{1,0:T(8,128)(2,1)S(1)}, u32[]{:S(2)}, u32[]{:S(2)}) collective-permute-start(bf16[48,4224]{1,0:T(8,128)(2,1)S(1)} %slice.170), channel_id=1, source_target_pairs={{0,1},{1,0},{2,3},{3,2},{4,5},{5,4},{6,7},{7,6},{8,9},{9,8},{10,11... | collective-permute-start | bytes 1216520 | tf_op jit(solution)/shard_map/ppermute | solution.py:239
  74.5 6.0 %collective-permute-start.20 = (bf16[16,4224]{1,0:T(8,128)(2,1)S(1)}, bf16[16,4224]{1,0:T(8,128)(2,1)S(1)}, u32[]{:S(2)}, u32[]{:S(2)}) collective-permute-start(bf16[16,4224]{1,0:T(8,128)(2,1)S(1)} %slice.168), channel_id=1, source_target_pairs={{0,4},{1,3},{2,0},{3,7},{4,8},{5,1},{6,2},{7,11},{8,12},{9,5},{10,... | collective-permute-start | bytes 405512 | tf_op jit(solution)/shard_map/ppermute | solution.py:236
  74.7 5.6 %collective-permute-start.15 = (bf16[48,4096]{1,0:T(8,128)(2,1)S(1)}, bf16[48,4096]{1,0:T(8,128)(2,1)S(1)}, u32[]{:S(2)}, u32[]{:S(2)}) collective-permute-start(bf16[48,4096]{1,0:T(8,128)(2,1)S(1)} %slice.156), channel_id=1, source_target_pairs={{0,1},{1,0},{2,3},{3,2},{4,5},{5,4},{6,7},{7,6},{8,9},{9,8},{10,11... | collective-permute-start | bytes 1179656 | tf_op jit(solution)/shard_map/ppermute | solution.py:239
  76.2 4.1 %collective-permute-start.14 = (bf16[16,4096]{1,0:T(8,128)(2,1)S(1)}, bf16[16,4096]{1,0:T(8,128)(2,1)S(1)}, u32[]{:S(2)}, u32[]{:S(2)}) collective-permute-start(bf16[16,4096]{1,0:T(8,128)(2,1)S(1)} %slice.154), channel_id=1, source_target_pairs={{0,4},{1,3},{2,0},{3,7},{4,8},{5,1},{6,2},{7,11},{8,12},{9,5},{10,... | collective-permute-start | bytes 393224 | tf_op jit(solution)/shard_map/ppermute | solution.py:236
  80.3 4.2 %collective-permute-start.16 = (bf16[16,4096]{1,0:T(8,128)(2,1)S(1)}, bf16[16,4096]{1,0:T(8,128)(2,1)S(1)}, u32[]{:S(2)}, u32[]{:S(2)}) collective-permute-start(bf16[16,4096]{1,0:T(8,128)(2,1)S(1)} %add_convert_fusion.5), channel_id=1, source_target_pairs={{0,4},{1,3},{2,0},{3,7},{4,8},{5,1},{6,2},{7,11},{8,12},{9,5},{10,... | collective-permute-start | bytes 393224 | tf_op jit(solution)/shard_map/ppermute | solution.py:236
  81.5 10.8 %copy-start.6 = (f32[16,4096]{1,0:T(8,128)S(1)}, f32[16,4096]{1,0:T(8,128)}, u32[]{:S(2)}) copy-start(f32[16,4096]{1,0:T(8,128)} %get-tuple-element.20) | copy-start | bytes 786436
  81.5 4.3 %collective-permute-start.22 = (bf16[16,4224]{1,0:T(8,128)(2,1)S(1)}, bf16[16,4224]{1,0:T(8,128)(2,1)S(1)}, u32[]{:S(2)}, u32[]{:S(2)}) collective-permute-start(bf16[16,4224]{1,0:T(8,128)(2,1)S(1)} %add_convert_fusion.2), channel_id=1, source_target_pairs={{0,4},{1,3},{2,0},{3,7},{4,8},{5,1},{6,2},{7,11},{8,12},{9,5},{10,... | collective-permute-start | bytes 405512 | tf_op jit(solution)/shard_map/ppermute | solution.py:236
  84.6 12.9 %copy-start.5 = (f32[16,4224]{1,0:T(8,128)S(1)}, f32[16,4224]{1,0:T(8,128)}, u32[]{:S(2)}) copy-start(f32[16,4224]{1,0:T(8,128)} %get-tuple-element.22) | copy-start | bytes 811012
  84.6 3.9 %collective-permute-start.17 = (bf16[16,4096]{1,0:T(8,128)(2,1)S(1)}, bf16[16,4096]{1,0:T(8,128)(2,1)S(1)}, u32[]{:S(2)}, u32[]{:S(2)}) collective-permute-start(bf16[16,4096]{1,0:T(8,128)(2,1)S(1)} %add_convert_fusion.4), channel_id=1, source_target_pairs={{0,4},{1,3},{2,0},{3,7},{4,8},{5,1},{6,2},{7,11},{8,12},{9,5},{10,... | collective-permute-start | bytes 393224 | tf_op jit(solution)/shard_map/ppermute | solution.py:236
  86.8 4.1 %collective-permute-start.23 = (bf16[16,4224]{1,0:T(8,128)(2,1)S(1)}, bf16[16,4224]{1,0:T(8,128)(2,1)S(1)}, u32[]{:S(2)}, u32[]{:S(2)}) collective-permute-start(bf16[16,4224]{1,0:T(8,128)(2,1)S(1)} %add_convert_fusion.1), channel_id=1, source_target_pairs={{0,4},{1,3},{2,0},{3,7},{4,8},{5,1},{6,2},{7,11},{8,12},{9,5},{10,... | collective-permute-start | bytes 405512 | tf_op jit(solution)/shard_map/ppermute | solution.py:236
  88.5 3.9 %collective-permute-start.18 = (bf16[16,4096]{1,0:T(8,128)(2,1)S(1)}, bf16[16,4096]{1,0:T(8,128)(2,1)S(1)}, u32[]{:S(2)}, u32[]{:S(2)}) collective-permute-start(bf16[16,4096]{1,0:T(8,128)(2,1)S(1)} %add_convert_fusion.3), channel_id=1, source_target_pairs={{0,4},{1,3},{2,0},{3,7},{4,8},{5,1},{6,2},{7,11},{8,12},{9,5},{10,... | collective-permute-start | bytes 393224 | tf_op jit(solution)/shard_map/ppermute | solution.py:236
  91.9 5.5 %collective-permute-start.24 = (bf16[16,4224]{1,0:T(8,128)(2,1)S(1)}, bf16[16,4224]{1,0:T(8,128)(2,1)S(1)}, u32[]{:S(2)}, u32[]{:S(2)}) collective-permute-start(bf16[16,4224]{1,0:T(8,128)(2,1)S(1)} %add_convert_fusion), channel_id=1, source_target_pairs={{0,4},{1,3},{2,0},{3,7},{4,8},{5,1},{6,2},{7,11},{8,12},{9,5},{10,... | collective-permute-start | bytes 405512 | tf_op jit(solution)/shard_map/ppermute | solution.py:236
  92.4 8.6 %collective-permute-start.19 = (f32[16,4096]{1,0:T(8,128)S(1)}, f32[16,4096]{1,0:T(8,128)S(1)}, u32[]{:S(2)}, u32[]{:S(2)}) collective-permute-start(f32[16,4096]{1,0:T(8,128)S(1)} %convert_add_fusion.1), channel_id=1, source_target_pairs={{0,1},{1,0},{2,3},{3,2},{4,5},{5,4},{6,7},{7,6},{8,9},{9,8},{10,11... | collective-permute-start | bytes 786440 | tf_op jit(solution)/shard_map/ppermute | solution.py:239
  97.5 5.7 %collective-permute-start.25 = (f32[16,4224]{1,0:T(8,128)S(1)}, f32[16,4224]{1,0:T(8,128)S(1)}, u32[]{:S(2)}, u32[]{:S(2)}) collective-permute-start(f32[16,4224]{1,0:T(8,128)S(1)} %convert_add_fusion), channel_id=1, source_target_pairs={{0,1},{1,0},{2,3},{3,2},{4,5},{5,4},{6,7},{7,6},{8,9},{9,8},{10,11... | collective-permute-start | bytes 811016 | tf_op jit(solution)/shard_map/ppermute | solution.py:239
  (7 other events, 37.3 us)

commit v2 on v1

v2 whole, which is shorter than its diff:
```python
import functools

import jax
import jax.numpy as jnp
from jax import lax
from jax.experimental import pallas as pl
from jax.experimental.pallas import tpu as pltpu
from jax.sharding import PartitionSpec as P

SEG = 16
RANK = 8
PAD = 128
EPS = 1e-05
BF = jnp.bfloat16
F32 = jnp.float32


def dot_nn(a, b):
    return jnp.dot(a, b, preferred_element_type=F32)


def dot_nt(a, b):
    return lax.dot_general(a, b, (((1,), (1,)), ((), ())), preferred_element_type=F32)


def split(x):
    high = x.astype(BF)
    low = (x - high.astype(F32)).astype(BF)
    return high, low


def ring_order(n):
    if n == 8:
        return [0, 2, 4, 6, 7, 5, 3, 1]
    return list(range(n))


def place_of(n, d):
    if n == 8:
        return jnp.where(d % 2 == 0, d // 2, n - 1 - d // 2)
    return d


def device_at(n, p):
    if n == 8:
        return jnp.where(p < n // 2, 2 * p, 2 * (n - 1 - p) + 1)
    return p


def piece_devices(n, where_ref):
    half = n // 2 - 1
    steps = [0] + [-t for t in range(1, half + 1)] + [t for t in range(1, half + 1)] + [n // 2]
    me = place_of(n, where_ref[0])
    sign = 1 - 2 * where_ref[1]
    return [device_at(n, lax.rem(me + sign * step + n, n)) for step in steps]


def block_tenant(device, counts_ref, starts_ref, slots_ref):
    first = device * SEG
    begin, count, slot = starts_ref[0], counts_ref[0], slots_ref[0]
    for t in range(1, starts_ref.shape[0]):
        reached = starts_ref[t] <= first
        begin = jnp.where(reached, starts_ref[t], begin)
        count = jnp.where(reached, counts_ref[t], count)
        slot = jnp.where(reached, slots_ref[t], slot)
    return slot, count - (first - begin)


def tenant_mask(n, where_ref, counts_ref, starts_ref, slots_ref):
    shape = (n * SEG, n * SEG)
    row = lax.broadcasted_iota(jnp.int32, shape, 0)
    column = lax.broadcasted_iota(jnp.int32, shape, 1)
    devices = piece_devices(n, where_ref)
    row_slot = jnp.zeros(shape, jnp.int32)
    row_limit = jnp.zeros(shape, jnp.int32)
    column_slot = jnp.zeros(shape, jnp.int32)
    for k, device in enumerate(devices):
        slot, limit = block_tenant(device, counts_ref, starts_ref, slots_ref)
        here = row // SEG == k
        row_slot = jnp.where(here, slot, row_slot)
        row_limit = jnp.where(here, limit, row_limit)
        column_slot = jnp.where(column // SEG == k, device, column_slot)
    keep = (row_slot == column_slot) & (row % SEG < row_limit) & (column % SEG < RANK)
    return jnp.where(keep, 1.0, 0.0)


def columns_at(c, step):
    return pl.ds(pl.multiple_of(c * step, step), step)


def pack_kernel(
    hidden_hbm, basis_hbm, learned_hbm, bias_hbm, packed_ref, basis_ref, learned_ref, bias_ref, sems
):
    width = hidden_hbm.shape[1]
    copies = (
        pltpu.make_async_copy(hidden_hbm, packed_ref.at[:SEG, :width], sems.at[0]),
        pltpu.make_async_copy(basis_hbm, basis_ref, sems.at[1]),
        pltpu.make_async_copy(learned_hbm, learned_ref, sems.at[2]),
        pltpu.make_async_copy(bias_hbm, bias_ref, sems.at[3]),
    )
    for copy in copies:
        copy.start()
    for copy in copies:
        copy.wait()
    packed_ref[SEG:, :width] = jnp.concatenate(
        [basis_ref[0].astype(F32), learned_ref[0].astype(F32)], axis=0
    ).astype(BF)
    shape = (SEG, PAD)
    row = lax.broadcasted_iota(jnp.int32, shape, 0)
    lane = lax.broadcasted_iota(jnp.int32, shape, 1)
    packed_ref[:SEG, width:] = jnp.where(lane == 0, 1.0, 0.0).astype(BF)
    bias = jnp.zeros(shape, F32)
    wide = bias_ref[...].astype(F32)
    for r in range(RANK):
        bias = jnp.where((row == RANK + r) & (lane == 0), wide[:, r : r + 1], bias)
    packed_ref[SEG:, width:] = bias.astype(BF)


def mark_kernel(after, out_ref):
    del after
    out_ref[...] = jnp.zeros_like(out_ref)


def back_kernel(n, *refs):
    pieces, (down_ref, upstream_ref, back_ref) = refs[:n], refs[-3:]
    for k, piece in enumerate(pieces):
        upstream_ref[k * SEG : (k + 1) * SEG, :] = piece[...]
    back_ref[...] = dot_nt(upstream_ref[...], down_ref[...])


def hidden_kernel(n, step, *refs):
    where_ref, counts_ref, starts_ref, slots_ref = refs[:4]
    pieces = refs[4 : 4 + n]
    (
        gain_ref,
        back_ref,
        gate_ref,
        up_ref,
        own_ref,
        sent_ref,
        scaled_ref,
        rows_ref,
        tables_ref,
        middle_ref,
        coeffs_ref,
        stats_ref,
        normed_ref,
        gate_grad_ref,
        up_grad_ref,
    ) = refs[4 + n :]
    row_total, width = middle_ref.shape
    chunks = width // step
    for k, piece in enumerate(pieces):
        rows_ref[k * SEG : (k + 1) * SEG, :] = piece[:SEG, :]
        tables_ref[k * SEG : (k + 1) * SEG, :] = piece[SEG:, :]

    columns = tables_ref.shape[0]
    products = dot_nt(rows_ref[...], tables_ref[...])
    mask = tenant_mask(n, where_ref, counts_ref, starts_ref, slots_ref)
    coeffs = mask * (pltpu.roll(products, columns - RANK, 1) - products)
    coeffs_ref[...] = coeffs
    coeff_high, coeff_low = split(coeffs)

    def middle_step(c, squares):
        cols = columns_at(c, step)
        table = tables_ref[:, cols]
        value = rows_ref[:, cols].astype(F32) + (
            dot_nn(coeff_high, table) + dot_nn(coeff_low, table)
        )
        value = value.astype(BF)
        middle_ref[:, cols] = value
        value = value.astype(F32)
        return squares + jnp.sum(value * value, axis=1, keepdims=True)

    squares = lax.fori_loop(0, chunks, middle_step, jnp.zeros((row_total, 1), F32))
    inverse = lax.rsqrt(squares / width + EPS)

    def normed_step(c, carry):
        cols = columns_at(c, step)
        value = middle_ref[:, cols].astype(F32) * inverse * gain_ref[:, cols]
        normed_ref[:, cols] = value.astype(BF)
        return carry

    lax.fori_loop(0, chunks, normed_step, 0)

    hidden = gate_ref.shape[1]
    tile = min(256, hidden)
    for j in range(hidden // tile):
        cols = slice(j * tile, (j + 1) * tile)
        gate = dot_nn(normed_ref[...], gate_ref[:, cols])
        upward = dot_nn(normed_ref[...], up_ref[:, cols])
        back = back_ref[:, cols]
        sigma = jax.nn.sigmoid(gate)
        gate_grad_ref[:, cols] = (back * upward * sigma * (1.0 + gate * (1.0 - sigma))).astype(BF)
        up_grad_ref[:, cols] = (back * gate * sigma).astype(BF)

    def scaled_step(c, inner):
        cols = columns_at(c, step)
        value = dot_nt(gate_grad_ref[...], gate_ref[cols, :])
        value = value + dot_nt(up_grad_ref[...], up_ref[cols, :])
        value = value * gain_ref[:, cols]
        scaled_ref[:, cols] = value
        own_ref[:, cols] = value[:SEG]
        sent_ref[:, cols] = value[SEG:].astype(BF)
        return inner + jnp.sum(value * middle_ref[:, cols].astype(F32), axis=1, keepdims=True)

    inner = lax.fori_loop(0, chunks, scaled_step, jnp.zeros((row_total, 1), F32))
    lane = lax.broadcasted_iota(jnp.int32, stats_ref.shape, 1)
    stats_ref[...] = jnp.where(lane == 0, inverse, inverse * inverse * (inner / width))


def slot_kernel(
    n,
    step,
    where_ref,
    counts_ref,
    starts_ref,
    slots_ref,
    scaled_ref,
    rows_ref,
    tables_ref,
    upstream_ref,
    middle_ref,
    coeffs_ref,
    stats_ref,
    own_ref,
    sent_ref,
    total_ref,
):
    row_total, width = middle_ref.shape
    columns = tables_ref.shape[0]
    chunks = width // step
    inverse, shrink = stats_ref[:, 0:1], stats_ref[:, 1:2]

    def total_step(c, carry):
        pulled, pulled_up = carry
        cols = columns_at(c, step)
        value = inverse * (scaled_ref[:, cols] - middle_ref[:, cols].astype(F32) * shrink)
        high, low = split(value)
        total_ref[0, :, cols] = high
        total_ref[1, :, cols] = low
        table = tables_ref[:, cols]
        pulled = pulled + (dot_nt(high, table) + dot_nt(low, table))
        return pulled, pulled_up + dot_nt(upstream_ref[:, cols], table)

    zero = jnp.zeros((row_total, columns), F32)
    pulled, pulled_up = lax.fori_loop(0, chunks, total_step, (zero, zero))
    mask = tenant_mask(n, where_ref, counts_ref, starts_ref, slots_ref)
    lane = lax.broadcasted_iota(jnp.int32, (row_total, columns), 1)
    first_slot = jnp.where(lane < RANK, 0.5, 0.0)
    pulled = mask * (pulled + first_slot * pulled_up)
    pulled = pltpu.roll(pulled, RANK, 1) - pulled
    coeffs = coeffs_ref[...]
    coeff_high, coeff_low = split(coeffs.T)
    first_high, first_low = split((coeffs * first_slot).T[:SEG])
    pulled_high, pulled_low = split(pulled.T)

    def slot_step(c, carry):
        cols = columns_at(c, step)
        high, low = total_ref[0, :, cols], total_ref[1, :, cols]
        rows = rows_ref[:, cols]
        value = dot_nn(coeff_high, high) + dot_nn(coeff_high, low) + dot_nn(coeff_low, high)
        value = value + dot_nn(pulled_high, rows) + dot_nn(pulled_low, rows)
        sent_ref[:, cols] = value[SEG:].astype(BF)
        upstream = upstream_ref[:, cols]
        own_ref[:, cols] = value[:SEG] + (
            dot_nn(first_high, upstream) + dot_nn(first_low, upstream)
        )
        return carry

    lax.fori_loop(0, chunks, slot_step, 0)
    extra = rows_ref[:, width:]
    value = dot_nn(pulled_high, extra) + dot_nn(pulled_low, extra)
    sent_ref[:, width:] = value[SEG:].astype(BF)
    own_ref[:, width:] = value[:SEG]


def rows_kernel(
    n,
    where_ref,
    counts_ref,
    starts_ref,
    slots_ref,
    mine_ref,
    other_ref,
    upstream_ref,
    middle_ref,
    stats_ref,
    tables_ref,
    out_ref,
):
    width = out_ref.shape[1]
    devices = piece_devices(n, where_ref)
    slot, limit = block_tenant(devices[0], counts_ref, starts_ref, slots_ref)
    which = 0
    for k, device in enumerate(devices):
        which = jnp.where(device == slot, k, which)
    table = tables_ref[pl.ds(pl.multiple_of(which * SEG, SEG), SEG), :width]
    middle = middle_ref[:SEG, :].astype(F32)
    inverse = stats_ref[:SEG, 0:1]
    scaled = mine_ref[...] + other_ref[...]
    inner = jnp.sum(scaled * middle, axis=1, keepdims=True) / width
    total = upstream_ref[...].astype(F32) + inverse * (
        scaled - middle * (inverse * inverse * inner)
    )
    high, low = split(total)
    pulled = dot_nt(high, table) + dot_nt(low, table)
    row = lax.broadcasted_iota(jnp.int32, (SEG, RANK), 0)
    pulled = jnp.where(row < limit, pulled[:, :RANK], 0.0)
    pulled = jnp.concatenate([-pulled, pulled], axis=1)
    high, low = split(pulled)
    out_ref[...] = (total + dot_nn(high, table) + dot_nn(low, table)).astype(BF)


LOAD_FLOPS = 4 * 10**9
LONG_FLOPS = 40 * 10**9
SMEM_SPEC = pl.BlockSpec(memory_space=pltpu.SMEM)
VMEM_SPEC = pl.BlockSpec(memory_space=pltpu.VMEM)


def call(kernel, outs, scalars, arrays, scratch=(), flops=0, moved=0, limit=4, spec=None):
    return pl.pallas_call(
        kernel,
        out_shape=tuple(jax.ShapeDtypeStruct(s, d) for s, d in outs),
        in_specs=[SMEM_SPEC] * len(scalars) + [spec or VMEM_SPEC] * len(arrays),
        out_specs=tuple(VMEM_SPEC for _ in outs),
        scratch_shapes=list(scratch),
        compiler_params=pltpu.CompilerParams(vmem_limit_bytes=limit * 1024 * 1024),
        cost_estimate=pl.CostEstimate(flops=flops, bytes_accessed=moved, transcendentals=0),
    )(*scalars, *arrays)


def resident(x):
    return pltpu.with_memory_space_constraint(x, pltpu.VMEM)


def remote(x):
    return pltpu.with_memory_space_constraint(x, pltpu.HBM)


def mark(after):
    (out,) = call(
        mark_kernel, [((8, 128), F32)], (), (after,), flops=LOAD_FLOPS, spec=pl.BlockSpec(memory_space=pl.ANY)
    )
    return out


def make_device_function(n):
    order = ring_order(n)
    place = {d: k for k, d in enumerate(order)}
    half = n // 2 - 1
    pairs = []
    for d in range(n):
        pairs.append((d * 2, order[(place[d] + 1) % n] * 2))
        pairs.append((d * 2 + 1, order[(place[d] - 1) % n] * 2 + 1))

    def hop(x):
        return lax.ppermute(x, ("dp", "tensor"), pairs)

    def swap(x):
        return lax.ppermute(x, "tensor", [(0, 1), (1, 0)])

    def gather(x):
        ahead, behind = [], []
        state = x
        for _ in range(half):
            state = hop(state)
            ahead.append(state)
            behind.append(swap(state))
        return [x] + ahead + behind + [hop(state)]

    def reduce(own, sent):
        other = swap(sent[: half * SEG])
        state = hop(sent[2 * half * SEG :])
        for t in range(half - 1, -1, -1):
            mine = sent[(half + t) * SEG : (half + t + 1) * SEG].astype(F32)
            partner = other[t * SEG : (t + 1) * SEG].astype(F32)
            state = hop((state.astype(F32) + (mine + partner)).astype(BF))
        return own + state.astype(F32)

    def on_device(
        hidden_in,
        grad_out,
        norm_gain,
        gate_weight,
        up_weight,
        down_weight,
        tenant_basis,
        tenant_learned,
        tenant_bias,
        row_counts,
        segment_starts,
        owner_slot,
    ):
        width = hidden_in.shape[1]
        hidden = gate_weight.shape[1]
        wide = width + PAD
        rows_total = n * SEG
        work = 2 * rows_total * width * hidden
        where = jnp.stack([lax.axis_index("dp"), lax.axis_index("tensor")]).astype(jnp.int32)
        scalars = (where, row_counts, segment_starts, owner_slot)
        (packed,) = call(
            pack_kernel,
            [((2 * SEG, wide), BF)],
            (),
            tuple(remote(x) for x in (hidden_in, tenant_basis, tenant_learned, tenant_bias)),
            scratch=[
                pltpu.VMEM(tenant_basis.shape, BF),
                pltpu.VMEM(tenant_learned.shape, BF),
                pltpu.VMEM(tenant_bias.shape, BF),
                pltpu.SemaphoreType.DMA((4,)),
            ],
            moved=4 * SEG * wide * 2,
            spec=pl.BlockSpec(memory_space=pl.ANY),
        )
        upstream_pieces = gather(grad_out)
        packed_pieces = gather(packed)
        marks = tuple(mark(x) for x in (packed, upstream_pieces[1], upstream_pieces[2]))
        upstream, back = call(
            functools.partial(back_kernel, n),
            [((rows_total, width), BF), ((rows_total, hidden), F32)],
            (),
            (*upstream_pieces, *marks, resident(down_weight)),
            flops=LONG_FLOPS,
            moved=2 * width * hidden,
            limit=n,
        )
        own, sent, scaled, rows, tables, middle, coeffs, stats = call(
            functools.partial(hidden_kernel, n, 1024),
            [
                ((SEG, width), F32),
                ((rows_total - SEG, width), BF),
                ((rows_total, width), F32),
                ((rows_total, wide), BF),
                ((rows_total, wide), BF),
                ((rows_total, width), BF),
                ((rows_total, rows_total), F32),
                ((rows_total, 128), F32),
            ],
            scalars,
            (
                *packed_pieces,
                norm_gain.reshape(1, width),
                back,
                resident(gate_weight),
                resident(up_weight),
            ),
            scratch=[
                pltpu.VMEM((rows_total, width), BF),
                pltpu.VMEM((rows_total, hidden), BF),
                pltpu.VMEM((rows_total, hidden), BF),
            ],
            flops=4 * work,
            moved=4 * width * hidden,
            limit=n + n // 2,
        )
        own_slot, sent_slot = call(
            functools.partial(slot_kernel, n, 512),
            [((SEG, wide), F32), ((rows_total - SEG, wide), BF)],
            scalars,
            (scaled, rows, tables, upstream, middle, coeffs, stats),
            scratch=[pltpu.VMEM((2, rows_total, width), BF)],
            flops=work,
            moved=10 * rows_total * width,
            limit=n + n // 2,
        )
        mine = reduce(own, sent)
        other = swap(mine)
        slots = reduce(own_slot, sent_slot)
        (grad_rows,) = call(
            functools.partial(rows_kernel, n),
            [((SEG, width), BF)],
            scalars,
            (mine, other, grad_out, middle, stats, tables),
            flops=LONG_FLOPS,
            moved=14 * SEG * width,
        )
        slots = slots + swap(slots)
        return (
            grad_rows,
            slots[None, :RANK, :width],
            slots[None, RANK:, :width],
            slots[None, RANK:, width],
        )

    return on_device


def solution(mesh):
    return jax.shard_map(
        make_device_function(mesh.shape["dp"]),
        mesh=mesh,
        in_specs=(
            P(("groups", "dp"), None),
            P(("groups", "dp"), None),
            P(),
            P(None, ("dp", "tensor")),
            P(None, ("dp", "tensor")),
            P(("dp", "tensor"), None),
            P(("groups", "dp"), None, None),
            P(("groups", "dp"), None, None),
            P(("groups", "dp"), None),
            P("groups"),
            P("groups"),
            P("groups"),
        ),
        out_specs=(
            P(("groups", "dp"), None),
            P(("groups", "dp"), None, None),
            P(("groups", "dp"), None, None),
            P(("groups", "dp"), None),
        ),
        check_vma=False,
    )
```

time: 105 us -> 78.5 us (0.75)
  local copies, waits for them, and re-layouts: 11.7 us -> 1.47 us
  waiting for transfers between devices: 23.2 us -> 13.8 us
  other arithmetic: 9.38 us -> 0.5 us
  starting transfers between devices: 29.9 us -> 36.9 us
  matrix products: 2.21 us -> 0 us
  between operations: 2.34 us -> 0.94 us
  Pallas kernels: 25.8 us -> 24.7 us
    ppermute x16, waiting for transfers between devices: 21.6 us -> 13.8 us  [hop(): return lax.ppermute(x, ('dp', 'tensor'), pairs)]
    ppermute x16, starting transfers between devices: 8.84 us -> 15 us  [hop(): return lax.ppermute(x, ('dp', 'tensor'), pairs)]
    unnamed x40 -> x22, local copies, waits for them, and re-layouts: 4.43 us -> 0.06 us
    convert_element_type x8 -> x6, other arithmetic: 4.04 us -> 0.33 us  [reduce(): state = hop((state.astype(F32) + (mine + partner)).astype(BF))]
    dot_general x2 -> x0, matrix products: 2.21 us -> none  [the longest x1 1.12 us: on_device(): jnp.dot(pulled, learned - basis, precision=lax.Precision.HIGHEST)]
    slice x4, local copies, waits for them, and re-layouts: 2.07 us -> 0.08 us  [the longest x2 0.06 us: reduce(): other = swap(sent[:half * SEG])]
    select_n x2 -> x0, other arithmetic: 1.95 us -> none  [the longest x1 1.29 us: on_device(): mask = jnp.where(column[None, :] % (2 * RANK) < RANK, mask, 0.0)]
    reshape x2 -> x0, local copies, waits for them, and re-layouts: 1.67 us -> none  [the longest x1 0.93 us: on_device(): mask = jnp.repeat(mask, 2 * RANK, axis=1)]
  transfers between devices with their start and end apart: 26 -> 26, of which waited for: 12 -> 9; matrix products, arithmetic and copies ran while one was open for 15% -> 1% of each run, Pallas kernels for 0% -> 16%
where the time goes in v2:
time: 78.5 us; the launch traced here: 78.3 us
  starting transfers between devices  36.9 us (47%)
  Pallas kernels  24.7 us (31%)
  waiting for transfers between devices  13.8 us (18%)
  local copies, waits for them, and re-layouts  1.47 us (2%)
  between operations  0.94 us (1%)
    pallas_call x8, Pallas kernels, call(): pl.pallas_call(kernel, out_shape=tuple((jax.ShapeDtypeStruct(s, d) for s,...  24.7 us
    ppermute x10, starting transfers between devices, swap(): return lax.ppermute(x, 'tensor', [(0, 1), (1, 0)])  21.9 us
    ppermute x16, starting transfers between devices, hop(): return lax.ppermute(x, ('dp', 'tensor'), pairs)  15 us
    ppermute x16, waiting for transfers between devices, hop(): return lax.ppermute(x, ('dp', 'tensor'), pairs)  13.8 us
  transfers between devices with their start and end apart: 26, of which 9 were waited for; matrix products, arithmetic and copies ran while one was open for 1% of the time, Pallas kernels for 16%

profile of v2, /device:TPU:1, one launch (start us, length us, event | category | flops | bytes accessed | tf_op | source)
XLA Modules:
  0.0 78.3 jit_solution(16603536401309065757)
XLA Ops:
  0.6 2.1 %collective-permute-start.7 = (bf16[16,4096]{1,0:T(8,128)(2,1)}, bf16[16,4096]{1,0:T(8,128)(2,1)S(1)}, u32[]{:S(2)}, u32[]{:S(2)}) collective-permute-start(bf16[16,4096]{1,0:T(8,128)(2,1)} %upstream_ref.1), channel_id=1, source_target_pairs={{0,4},{1,3},{2,0},{3,7},{4,8},{5,1},{6,2},{7,11},{8,12},{9,5},{10,... | collective-permute-start | bytes 393224 | tf_op jit(solution)/shard_map/ppermute | solution.py:358
  2.8 1.1 %shard_map.147.after.refs_4_ = bf16[32,4224]{1,0:T(8,128)(2,1)S(1)} custom-call(bf16[16,4096]{1,0:T(8,128)(2,1)} %hidden_hbm.1, bf16[1,8,4096]{2,1,0:T(8,128)(2,1)} %basis_hbm.1, bf16[1,8,4096]{2,1,0:T(8,128)(2,1)} %learned_hbm.1, bf16[1,8]{1,0:T(2,128)(2,1)} %bias_hbm.1), custom_call_target="tpu_custom_call" | custom-call | bytes 540672 | tf_op jit(solution)/shard_map/pallas_call | solution.py:322
  3.9 1.3 %collective-permute-start = (bf16[32,4224]{1,0:T(8,128)(2,1)S(1)}, bf16[32,4224]{1,0:T(8,128)(2,1)S(1)}, u32[]{:S(2)}, u32[]{:S(2)}) collective-permute-start(bf16[32,4224]{1,0:T(8,128)(2,1)S(1)} %shard_map.147.after.refs_4_), channel_id=1, source_target_pairs={{0,4},{1,3},{2,0},{3,7},{4,8},{5,1},{6,2},{7,11},{8,12},{9,5},{10,... | collective-permute-start | bytes 811016 | tf_op jit(solution)/shard_map/ppermute | solution.py:358
  5.7 1.4 %collective-permute-start.8 = (bf16[16,4096]{1,0:T(8,128)(2,1)S(1)}, bf16[16,4096]{1,0:T(8,128)(2,1)S(1)}, u32[]{:S(2)}, u32[]{:S(2)}) collective-permute-start(bf16[16,4096]{1,0:T(8,128)(2,1)S(1)} %collective-permute-done.7.after.refs_1_), channel_id=1, source_target_pairs={{0,4},{1,3},{2,0},{3,7},{4,8},{5,1},{6,2},{7,11},{8,12},{9,5},{10,... | collective-permute-start | bytes 393224 | tf_op jit(solution)/shard_map/ppermute | solution.py:358
  7.2 3.8 %collective-permute-done.8.after.refs_2_ = bf16[16,4096]{1,0:T(8,128)(2,1)S(1)} collective-permute-done((bf16[16,4096]{1,0:T(8,128)(2,1)S(1)}, bf16[16,4096]{1,0:T(8,128)(2,1)S(1)}, u32[]{:S(2)}, u32[]{:S(2)}) %collective-permute-start.8) | collective-permute-done | bytes 131104 | tf_op jit(solution)/shard_map/ppermute | solution.py:358
  10.9 1.3 %collective-permute-start.9 = (bf16[16,4096]{1,0:T(8,128)(2,1)S(1)}, bf16[16,4096]{1,0:T(8,128)(2,1)S(1)}, u32[]{:S(2)}, u32[]{:S(2)}) collective-permute-start(bf16[16,4096]{1,0:T(8,128)(2,1)S(1)} %collective-permute-done.8.after.refs_2_), channel_id=1, source_target_pairs={{0,4},{1,3},{2,0},{3,7},{4,8},{5,1},{6,2},{7,11},{8,12},{9,5},{10,... | collective-permute-start | bytes 393224 | tf_op jit(solution)/shard_map/ppermute | solution.py:358
  12.2 1.3 %collective-permute-start.1 = (bf16[32,4224]{1,0:T(8,128)(2,1)S(1)}, bf16[32,4224]{1,0:T(8,128)(2,1)S(1)}, u32[]{:S(2)}, u32[]{:S(2)}) collective-permute-start(bf16[32,4224]{1,0:T(8,128)(2,1)S(1)} %collective-permute-done.refs_5_), channel_id=1, source_target_pairs={{0,4},{1,3},{2,0},{3,7},{4,8},{5,1},{6,2},{7,11},{8,12},{9,5},{10,... | collective-permute-start | bytes 811016 | tf_op jit(solution)/shard_map/ppermute | solution.py:358
  13.5 2.5 %collective-permute-start.10 = (bf16[16,4096]{1,0:T(8,128)(2,1)S(1)}, bf16[16,4096]{1,0:T(8,128)(2,1)S(1)}, u32[]{:S(2)}, u32[]{:S(2)}) collective-permute-start(bf16[16,4096]{1,0:T(8,128)(2,1)S(1)} %collective-permute-done.7.after.refs_1_), channel_id=1, source_target_pairs={{0,1},{1,0},{2,3},{3,2},{4,5},{5,4},{6,7},{7,6},{8,9},{9,8},{10,11... | collective-permute-start | bytes 393224 | tf_op jit(solution)/shard_map/ppermute | solution.py:361
  16.3 3.1 %collective-permute-start.12 = (bf16[16,4096]{1,0:T(8,128)(2,1)S(1)}, bf16[16,4096]{1,0:T(8,128)(2,1)S(1)}, u32[]{:S(2)}, u32[]{:S(2)}) collective-permute-start(bf16[16,4096]{1,0:T(8,128)(2,1)S(1)} %collective-permute-done.9.refs_3_), channel_id=1, source_target_pairs={{0,1},{1,0},{2,3},{3,2},{4,5},{5,4},{6,7},{7,6},{8,9},{9,8},{10,11... | collective-permute-start | bytes 393224 | tf_op jit(solution)/shard_map/ppermute | solution.py:361
  19.6 3.0 %collective-permute-start.3 = (bf16[32,4224]{1,0:T(8,128)(2,1)S(1)}, bf16[32,4224]{1,0:T(8,128)(2,1)S(1)}, u32[]{:S(2)}, u32[]{:S(2)}) collective-permute-start(bf16[32,4224]{1,0:T(8,128)(2,1)S(1)} %collective-permute-done.refs_5_), channel_id=1, source_target_pairs={{0,1},{1,0},{2,3},{3,2},{4,5},{5,4},{6,7},{7,6},{8,9},{9,8},{10,11... | collective-permute-start | bytes 811016 | tf_op jit(solution)/shard_map/ppermute | solution.py:361
  22.6 2.3 %collective-permute-done.2.refs_7_ = bf16[32,4224]{1,0:T(8,128)(2,1)S(1)} collective-permute-done((bf16[32,4224]{1,0:T(8,128)(2,1)S(1)}, bf16[32,4224]{1,0:T(8,128)(2,1)S(1)}, u32[]{:S(2)}, u32[]{:S(2)}) %collective-permute-start.2) | collective-permute-done | bytes 270368 | tf_op jit(solution)/shard_map/ppermute | solution.py:358
  25.1 3.8 %collective-permute-start.5 = (bf16[32,4224]{1,0:T(8,128)(2,1)S(1)}, bf16[32,4224]{1,0:T(8,128)(2,1)S(1)}, u32[]{:S(2)}, u32[]{:S(2)}) collective-permute-start(bf16[32,4224]{1,0:T(8,128)(2,1)S(1)} %collective-permute-done.2.refs_7_), channel_id=1, source_target_pairs={{0,1},{1,0},{2,3},{3,2},{4,5},{5,4},{6,7},{7,6},{8,9},{9,8},{10,11... | collective-permute-start | bytes 811016 | tf_op jit(solution)/shard_map/ppermute | solution.py:361
  28.9 2.9 %shard_map.151 = (bf16[128,4096]{1,0:T(8,128)(2,1)S(1)}, f32[128,1024]{1,0:T(8,128)S(1)}) custom-call(bf16[16,4096]{1,0:T(8,128)(2,1)S(1)} %copy-done.4, bf16[16,4096]{1,0:T(8,128)(2,1)S(1)} %collective-permute-done.7.after.refs_1_, bf16[16,4096]{1,0:T(8,128)(2,1)S(1)} %collective-permute-done.8.after.refs_2_, ...), custom_call_target="tpu_custom_call" | custom-call | flops 40000000000 | bytes 8388608 | tf_op jit(solution)/shard_map/pallas_call | solution.py:322
  31.9 12.1 %shard_map.152 = (f32[16,4096]{1,0:T(8,128)S(1)}, bf16[112,4096]{1,0:T(8,128)(2,1)S(1)}, f32[128,4096]{1,0:T(8,128)S(1)}, bf16[128,4224]{1,0:T(8,128)(2,1)S(1)},...) custom-call(s32[2]{0:T(128)S(1)} %pad_add_fusion.refs_0_.where_ref, ...), custom_call_target="tpu_custom_call" | custom-call | flops 4294967296 | bytes 16777216 | tf_op jit(solution)/shard_map/pallas_call | solution.py:322
  44.1 2.0 %collective-permute-start.15 = (bf16[48,4096]{1,0:T(8,128)(2,1)S(1)}, bf16[48,4096]{1,0:T(8,128)(2,1)S(1)}, u32[]{:S(2)}, u32[]{:S(2)}) collective-permute-start(bf16[48,4096]{1,0:T(8,128)(2,1)S(1)} %slice.59), channel_id=1, source_target_pairs={{0,1},{1,0},{2,3},{3,2},{4,5},{5,4},{6,7},{7,6},{8,9},{9,8},{10,11... | collective-permute-start | bytes 1179656 | tf_op jit(solution)/shard_map/ppermute | solution.py:361
  46.1 0.7 collective-permute-start.14
  46.8 6.5 %shard_map.154 = (f32[16,4224]{1,0:T(8,128)S(1)}, bf16[112,4224]{1,0:T(8,128)(2,1)S(1)}) custom-call(s32[2]{0:T(128)S(1)} %pad_add_fusion.refs_0_.where_ref, s32[8]{0:T(128)S(1)} %copy-done.1, s32[8]{0:T(128)S(1)} %copy-done.2, s32[8]{0:T(128)S(1)} %copy-done.3, f32[128,4096]{1,0:T(8,128)S(1)} %get-tuple-element.22.scaled_ref, ...), custom_call_target="tpu_custom_call" | custom-call | flops 1073741824 | bytes 5242880 | tf_op jit(solution)/shard_map/pallas_call | solution.py:322
  53.3 1.3 %collective-permute-start.20 = (bf16[16,4224]{1,0:T(8,128)(2,1)S(1)}, bf16[16,4224]{1,0:T(8,128)(2,1)S(1)}, u32[]{:S(2)}, u32[]{:S(2)}) collective-permute-start(bf16[16,4224]{1,0:T(8,128)(2,1)S(1)} %slice.65), channel_id=1, source_target_pairs={{0,4},{1,3},{2,0},{3,7},{4,8},{5,1},{6,2},{7,11},{8,12},{9,5},{10,... | collective-permute-start | bytes 405512 | tf_op jit(solution)/shard_map/ppermute | solution.py:358
  54.7 1.2 %collective-permute-start.21 = (bf16[48,4224]{1,0:T(8,128)(2,1)S(1)}, bf16[48,4224]{1,0:T(8,128)(2,1)S(1)}, u32[]{:S(2)}, u32[]{:S(2)}) collective-permute-start(bf16[48,4224]{1,0:T(8,128)(2,1)S(1)} %slice.67), channel_id=1, source_target_pairs={{0,1},{1,0},{2,3},{3,2},{4,5},{5,4},{6,7},{7,6},{8,9},{9,8},{10,11... | collective-permute-start | bytes 1216520 | tf_op jit(solution)/shard_map/ppermute | solution.py:361
  56.2 1.3 %collective-permute-done.20 = bf16[16,4224]{1,0:T(8,128)(2,1)S(1)} collective-permute-done((bf16[16,4224]{1,0:T(8,128)(2,1)S(1)}, bf16[16,4224]{1,0:T(8,128)(2,1)S(1)}, u32[]{:S(2)}, u32[]{:S(2)}) %collective-permute-start.20) | collective-permute-done | bytes 135200 | tf_op jit(solution)/shard_map/ppermute | solution.py:358
  57.6 1.3 %collective-permute-start.22 = (bf16[16,4224]{1,0:T(8,128)(2,1)S(1)}, bf16[16,4224]{1,0:T(8,128)(2,1)S(1)}, u32[]{:S(2)}, u32[]{:S(2)}) collective-permute-start(bf16[16,4224]{1,0:T(8,128)(2,1)S(1)} %add_convert_fusion.2), channel_id=1, source_target_pairs={{0,4},{1,3},{2,0},{3,7},{4,8},{5,1},{6,2},{7,11},{8,12},{9,5},{10,... | collective-permute-start | bytes 405512 | tf_op jit(solution)/shard_map/ppermute | solution.py:358
  58.9 1.1 %collective-permute-done.16 = bf16[16,4096]{1,0:T(8,128)(2,1)S(1)} collective-permute-done((bf16[16,4096]{1,0:T(8,128)(2,1)S(1)}, bf16[16,4096]{1,0:T(8,128)(2,1)S(1)}, u32[]{:S(2)}, u32[]{:S(2)}) %collective-permute-start.16) | collective-permute-done | bytes 131104 | tf_op jit(solution)/shard_map/ppermute | solution.py:358
  60.4 1.1 %collective-permute-done.22 = bf16[16,4224]{1,0:T(8,128)(2,1)S(1)} collective-permute-done((bf16[16,4224]{1,0:T(8,128)(2,1)S(1)}, bf16[16,4224]{1,0:T(8,128)(2,1)S(1)}, u32[]{:S(2)}, u32[]{:S(2)}) %collective-permute-start.22) | collective-permute-done | bytes 135200 | tf_op jit(solution)/shard_map/ppermute | solution.py:358
  61.6 1.6 %collective-permute-start.23 = (bf16[16,4224]{1,0:T(8,128)(2,1)S(1)}, bf16[16,4224]{1,0:T(8,128)(2,1)S(1)}, u32[]{:S(2)}, u32[]{:S(2)}) collective-permute-start(bf16[16,4224]{1,0:T(8,128)(2,1)S(1)} %add_convert_fusion.1), channel_id=1, source_target_pairs={{0,4},{1,3},{2,0},{3,7},{4,8},{5,1},{6,2},{7,11},{8,12},{9,5},{10,... | collective-permute-start | bytes 405512 | tf_op jit(solution)/shard_map/ppermute | solution.py:358
  63.2 1.1 %collective-permute-done.17 = bf16[16,4096]{1,0:T(8,128)(2,1)S(1)} collective-permute-done((bf16[16,4096]{1,0:T(8,128)(2,1)S(1)}, bf16[16,4096]{1,0:T(8,128)(2,1)S(1)}, u32[]{:S(2)}, u32[]{:S(2)}) %collective-permute-start.17) | collective-permute-done | bytes 131104 | tf_op jit(solution)/shard_map/ppermute | solution.py:358
  64.4 1.2 %collective-permute-done.23 = bf16[16,4224]{1,0:T(8,128)(2,1)S(1)} collective-permute-done((bf16[16,4224]{1,0:T(8,128)(2,1)S(1)}, bf16[16,4224]{1,0:T(8,128)(2,1)S(1)}, u32[]{:S(2)}, u32[]{:S(2)}) %collective-permute-start.23) | collective-permute-done | bytes 135200 | tf_op jit(solution)/shard_map/ppermute | solution.py:358
  65.8 1.4 %collective-permute-start.24 = (bf16[16,4224]{1,0:T(8,128)(2,1)S(1)}, bf16[16,4224]{1,0:T(8,128)(2,1)S(1)}, u32[]{:S(2)}, u32[]{:S(2)}) collective-permute-start(bf16[16,4224]{1,0:T(8,128)(2,1)S(1)} %add_convert_fusion), channel_id=1, source_target_pairs={{0,4},{1,3},{2,0},{3,7},{4,8},{5,1},{6,2},{7,11},{8,12},{9,5},{10,... | collective-permute-start | bytes 405512 | tf_op jit(solution)/shard_map/ppermute | solution.py:358
  67.2 1.3 %collective-permute-done.18 = bf16[16,4096]{1,0:T(8,128)(2,1)S(1)} collective-permute-done((bf16[16,4096]{1,0:T(8,128)(2,1)S(1)}, bf16[16,4096]{1,0:T(8,128)(2,1)S(1)}, u32[]{:S(2)}, u32[]{:S(2)}) %collective-permute-start.18) | collective-permute-done | bytes 131104 | tf_op jit(solution)/shard_map/ppermute | solution.py:358
  68.6 2.8 %collective-permute-start.19 = (f32[16,4096]{1,0:T(8,128)S(1)}, f32[16,4096]{1,0:T(8,128)S(1)}, u32[]{:S(2)}, u32[]{:S(2)}) collective-permute-start(f32[16,4096]{1,0:T(8,128)S(1)} %convert_add_fusion.1.mine_ref), channel_id=1, source_target_pairs={{0,1},{1,0},{2,3},{3,2},{4,5},{5,4},{6,7},{7,6},{8,9},{9,8},{10,11... | collective-permute-start | bytes 786440 | tf_op jit(solution)/shard_map/ppermute | solution.py:361
  71.4 3.4 %collective-permute-start.25 = (f32[16,4224]{1,0:T(8,128)S(1)}, f32[16,4224]{1,0:T(8,128)S(1)}, u32[]{:S(2)}, u32[]{:S(2)}) collective-permute-start(f32[16,4224]{1,0:T(8,128)S(1)} %convert_add_fusion), channel_id=1, source_target_pairs={{0,1},{1,0},{2,3},{3,2},{4,5},{5,4},{6,7},{7,6},{8,9},{9,8},{10,11... | collective-permute-start | bytes 811016 | tf_op jit(solution)/shard_map/ppermute | solution.py:361
  74.8 2.1 %shard_map.153 = bf16[16,4096]{1,0:T(8,128)(2,1)} custom-call(s32[2]{0:T(128)S(1)} %pad_add_fusion.refs_0_.where_ref, s32[8]{0:T(128)S(1)} %copy-done.1, s32[8]{0:T(128)S(1)} %copy-done.2, s32[8]{0:T(128)S(1)} %copy-done.3, f32[16,4096]{1,0:T(8,128)S(1)} %convert_add_fusion.1.mine_ref, f32[16,4096]{1,0:T(8,128)S(1)} %collective-permute-done.19.other_ref, ...), custom_call_target="tpu_custom_call" | custom-call | flops 40000000000 | bytes 917504 | tf_op jit(solution)/shard_map/pallas_call | solution.py:322
  77.6 0.7 slice_bitcast_fusion
  (69 shorter events, 3.1 us)
Async XLA Ops:
  0.6 5.0 %collective-permute-start.7 = (bf16[16,4096]{1,0:T(8,128)(2,1)}, bf16[16,4096]{1,0:T(8,128)(2,1)S(1)}, u32[]{:S(2)}, u32[]{:S(2)}) collective-permute-start(bf16[16,4096]{1,0:T(8,128)(2,1)} %upstream_ref.1), channel_id=1, source_target_pairs={{0,4},{1,3},{2,0},{3,7},{4,8},{5,1},{6,2},{7,11},{8,12},{9,5},{10,... | collective-permute-start | bytes 393224 | tf_op jit(solution)/shard_map/ppermute | solution.py:358
  3.9 8.4 %collective-permute-start = (bf16[32,4224]{1,0:T(8,128)(2,1)S(1)}, bf16[32,4224]{1,0:T(8,128)(2,1)S(1)}, u32[]{:S(2)}, u32[]{:S(2)}) collective-permute-start(bf16[32,4224]{1,0:T(8,128)(2,1)S(1)} %shard_map.147.after.refs_4_), channel_id=1, source_target_pairs={{0,4},{1,3},{2,0},{3,7},{4,8},{5,1},{6,2},{7,11},{8,12},{9,5},{10,... | collective-permute-start | bytes 811016 | tf_op jit(solution)/shard_map/ppermute | solution.py:358
  5.7 5.2 %collective-permute-start.8 = (bf16[16,4096]{1,0:T(8,128)(2,1)S(1)}, bf16[16,4096]{1,0:T(8,128)(2,1)S(1)}, u32[]{:S(2)}, u32[]{:S(2)}) collective-permute-start(bf16[16,4096]{1,0:T(8,128)(2,1)S(1)} %collective-permute-done.7.after.refs_1_), channel_id=1, source_target_pairs={{0,4},{1,3},{2,0},{3,7},{4,8},{5,1},{6,2},{7,11},{8,12},{9,5},{10,... | collective-permute-start | bytes 393224 | tf_op jit(solution)/shard_map/ppermute | solution.py:358
  10.9 5.2 %collective-permute-start.9 = (bf16[16,4096]{1,0:T(8,128)(2,1)S(1)}, bf16[16,4096]{1,0:T(8,128)(2,1)S(1)}, u32[]{:S(2)}, u32[]{:S(2)}) collective-permute-start(bf16[16,4096]{1,0:T(8,128)(2,1)S(1)} %collective-permute-done.8.after.refs_2_), channel_id=1, source_target_pairs={{0,4},{1,3},{2,0},{3,7},{4,8},{5,1},{6,2},{7,11},{8,12},{9,5},{10,... | collective-permute-start | bytes 393224 | tf_op jit(solution)/shard_map/ppermute | solution.py:358
  12.2 7.1 %collective-permute-start.1 = (bf16[32,4224]{1,0:T(8,128)(2,1)S(1)}, bf16[32,4224]{1,0:T(8,128)(2,1)S(1)}, u32[]{:S(2)}, u32[]{:S(2)}) collective-permute-start(bf16[32,4224]{1,0:T(8,128)(2,1)S(1)} %collective-permute-done.refs_5_), channel_id=1, source_target_pairs={{0,4},{1,3},{2,0},{3,7},{4,8},{5,1},{6,2},{7,11},{8,12},{9,5},{10,... | collective-permute-start | bytes 811016 | tf_op jit(solution)/shard_map/ppermute | solution.py:358
  13.5 15.4 %slice-start.4 = ((s8[8388608]{0:T(1024)(128)(4,1)}), s8[4194304]{0:T(1024)(128)(4,1)S(1)}, s32[]{:S(2)}) async-start(s8[8388608]{0:T(1024)(128)(4,1)} %bitcast.13), calls=%async_computation.4 | async-start | bytes 8388608
  13.5 15.4 %slice-start.5 = ((s8[8388608]{0:T(1024)(128)(4,1)}), s8[4194304]{0:T(1024)(128)(4,1)S(1)}, s32[]{:S(2)}) async-start(s8[8388608]{0:T(1024)(128)(4,1)} %bitcast.13), calls=%async_computation.5 | async-start | bytes 8388608
  13.5 15.4 %copy-start.4 = (bf16[16,4096]{1,0:T(8,128)(2,1)S(1)}, bf16[16,4096]{1,0:T(8,128)(2,1)}, u32[]{:S(2)}) copy-start(bf16[16,4096]{1,0:T(8,128)(2,1)} %upstream_ref.1) | copy-start | bytes 393220
  13.5 6.1 %collective-permute-start.10 = (bf16[16,4096]{1,0:T(8,128)(2,1)S(1)}, bf16[16,4096]{1,0:T(8,128)(2,1)S(1)}, u32[]{:S(2)}, u32[]{:S(2)}) collective-permute-start(bf16[16,4096]{1,0:T(8,128)(2,1)S(1)} %collective-permute-done.7.after.refs_1_), channel_id=1, source_target_pairs={{0,1},{1,0},{2,3},{3,2},{4,5},{5,4},{6,7},{7,6},{8,9},{9,8},{10,11... | collective-permute-start | bytes 393224 | tf_op jit(solution)/shard_map/ppermute | solution.py:361
  16.0 6.5 %collective-permute-start.11 = (bf16[16,4096]{1,0:T(8,128)(2,1)S(1)}, bf16[16,4096]{1,0:T(8,128)(2,1)S(1)}, u32[]{:S(2)}, u32[]{:S(2)}) collective-permute-start(bf16[16,4096]{1,0:T(8,128)(2,1)S(1)} %collective-permute-done.8.after.refs_2_), channel_id=1, source_target_pairs={{0,1},{1,0},{2,3},{3,2},{4,5},{5,4},{6,7},{7,6},{8,9},{9,8},{10,11... | collective-permute-start | bytes 393224 | tf_op jit(solution)/shard_map/ppermute | solution.py:361
  16.1 9.0 %collective-permute-start.13 = (bf16[16,4096]{1,0:T(8,128)(2,1)S(1)}, bf16[16,4096]{1,0:T(8,128)(2,1)S(1)}, u32[]{:S(2)}, u32[]{:S(2)}) collective-permute-start(bf16[16,4096]{1,0:T(8,128)(2,1)S(1)} %collective-permute-done.9.refs_3_), channel_id=1, source_target_pairs={{0,4},{1,3},{2,0},{3,7},{4,8},{5,1},{6,2},{7,11},{8,12},{9,5},{10,... | collective-permute-start | bytes 393224 | tf_op jit(solution)/shard_map/ppermute | solution.py:358
  16.3 12.6 %collective-permute-start.12 = (bf16[16,4096]{1,0:T(8,128)(2,1)S(1)}, bf16[16,4096]{1,0:T(8,128)(2,1)S(1)}, u32[]{:S(2)}, u32[]{:S(2)}) collective-permute-start(bf16[16,4096]{1,0:T(8,128)(2,1)S(1)} %collective-permute-done.9.refs_3_), channel_id=1, source_target_pairs={{0,1},{1,0},{2,3},{3,2},{4,5},{5,4},{6,7},{7,6},{8,9},{9,8},{10,11... | collective-permute-start | bytes 393224 | tf_op jit(solution)/shard_map/ppermute | solution.py:361
  19.3 5.6 %collective-permute-start.2 = (bf16[32,4224]{1,0:T(8,128)(2,1)S(1)}, bf16[32,4224]{1,0:T(8,128)(2,1)S(1)}, u32[]{:S(2)}, u32[]{:S(2)}) collective-permute-start(bf16[32,4224]{1,0:T(8,128)(2,1)S(1)} %collective-permute-done.1.refs_6_), channel_id=1, source_target_pairs={{0,4},{1,3},{2,0},{3,7},{4,8},{5,1},{6,2},{7,11},{8,12},{9,5},{10,... | collective-permute-start | bytes 811016 | tf_op jit(solution)/shard_map/ppermute | solution.py:358
  19.5 12.3 %slice-start.1 = ((s8[8388608]{0:T(1024)(128)(4,1)}), s8[4194304]{0:T(1024)(128)(4,1)S(1)}, s32[]{:S(2)}) async-start(s8[8388608]{0:T(1024)(128)(4,1)} %bitcast.8), calls=%async_computation.1 | async-start | bytes 8388608
  19.5 12.3 %slice-start.3 = ((s8[8388608]{0:T(1024)(128)(4,1)}), s8[4194304]{0:T(1024)(128)(4,1)S(1)}, s32[]{:S(2)}) async-start(s8[8388608]{0:T(1024)(128)(4,1)} %bitcast.10), calls=%async_computation.3 | async-start | bytes 8388608
  19.5 12.3 %copy-start = (f32[4096]{0:T(1024)S(1)}, f32[4096]{0:T(1024)}, u32[]{:S(2)}) copy-start(f32[4096]{0:T(1024)} %param.14) | copy-start | bytes 49156
  19.6 12.2 %collective-permute-start.3 = (bf16[32,4224]{1,0:T(8,128)(2,1)S(1)}, bf16[32,4224]{1,0:T(8,128)(2,1)S(1)}, u32[]{:S(2)}, u32[]{:S(2)}) collective-permute-start(bf16[32,4224]{1,0:T(8,128)(2,1)S(1)} %collective-permute-done.refs_5_), channel_id=1, source_target_pairs={{0,1},{1,0},{2,3},{3,2},{4,5},{5,4},{6,7},{7,6},{8,9},{9,8},{10,11... | collective-permute-start | bytes 811016 | tf_op jit(solution)/shard_map/ppermute | solution.py:361
  22.6 9.2 %collective-permute-start.4 = (bf16[32,4224]{1,0:T(8,128)(2,1)S(1)}, bf16[32,4224]{1,0:T(8,128)(2,1)S(1)}, u32[]{:S(2)}, u32[]{:S(2)}) collective-permute-start(bf16[32,4224]{1,0:T(8,128)(2,1)S(1)} %collective-permute-done.1.refs_6_), channel_id=1, source_target_pairs={{0,1},{1,0},{2,3},{3,2},{4,5},{5,4},{6,7},{7,6},{8,9},{9,8},{10,11... | collective-permute-start | bytes 811016 | tf_op jit(solution)/shard_map/ppermute | solution.py:361
  24.9 6.9 %collective-permute-start.6 = (bf16[32,4224]{1,0:T(8,128)(2,1)S(1)}, bf16[32,4224]{1,0:T(8,128)(2,1)S(1)}, u32[]{:S(2)}, u32[]{:S(2)}) collective-permute-start(bf16[32,4224]{1,0:T(8,128)(2,1)S(1)} %collective-permute-done.2.refs_7_), channel_id=1, source_target_pairs={{0,4},{1,3},{2,0},{3,7},{4,8},{5,1},{6,2},{7,11},{8,12},{9,5},{10,... | collective-permute-start | bytes 811016 | tf_op jit(solution)/shard_map/ppermute | solution.py:358
  25.1 6.7 %collective-permute-start.5 = (bf16[32,4224]{1,0:T(8,128)(2,1)S(1)}, bf16[32,4224]{1,0:T(8,128)(2,1)S(1)}, u32[]{:S(2)}, u32[]{:S(2)}) collective-permute-start(bf16[32,4224]{1,0:T(8,128)(2,1)S(1)} %collective-permute-done.2.refs_7_), channel_id=1, source_target_pairs={{0,1},{1,0},{2,3},{3,2},{4,5},{5,4},{6,7},{7,6},{8,9},{9,8},{10,11... | collective-permute-start | bytes 811016 | tf_op jit(solution)/shard_map/ppermute | solution.py:361
  44.1 11.8 %collective-permute-start.15 = (bf16[48,4096]{1,0:T(8,128)(2,1)S(1)}, bf16[48,4096]{1,0:T(8,128)(2,1)S(1)}, u32[]{:S(2)}, u32[]{:S(2)}) collective-permute-start(bf16[48,4096]{1,0:T(8,128)(2,1)S(1)} %slice.59), channel_id=1, source_target_pairs={{0,1},{1,0},{2,3},{3,2},{4,5},{5,4},{6,7},{7,6},{8,9},{9,8},{10,11... | collective-permute-start | bytes 1179656 | tf_op jit(solution)/shard_map/ppermute | solution.py:361
  46.1 9.8 %collective-permute-start.14 = (bf16[16,4096]{1,0:T(8,128)(2,1)S(1)}, bf16[16,4096]{1,0:T(8,128)(2,1)S(1)}, u32[]{:S(2)}, u32[]{:S(2)}) collective-permute-start(bf16[16,4096]{1,0:T(8,128)(2,1)S(1)} %slice.57), channel_id=1, source_target_pairs={{0,4},{1,3},{2,0},{3,7},{4,8},{5,1},{6,2},{7,11},{8,12},{9,5},{10,... | collective-permute-start | bytes 393224 | tf_op jit(solution)/shard_map/ppermute | solution.py:358
  53.3 4.2 %collective-permute-start.20 = (bf16[16,4224]{1,0:T(8,128)(2,1)S(1)}, bf16[16,4224]{1,0:T(8,128)(2,1)S(1)}, u32[]{:S(2)}, u32[]{:S(2)}) collective-permute-start(bf16[16,4224]{1,0:T(8,128)(2,1)S(1)} %slice.65), channel_id=1, source_target_pairs={{0,4},{1,3},{2,0},{3,7},{4,8},{5,1},{6,2},{7,11},{8,12},{9,5},{10,... | collective-permute-start | bytes 405512 | tf_op jit(solution)/shard_map/ppermute | solution.py:358
  54.7 2.9 %collective-permute-start.21 = (bf16[48,4224]{1,0:T(8,128)(2,1)S(1)}, bf16[48,4224]{1,0:T(8,128)(2,1)S(1)}, u32[]{:S(2)}, u32[]{:S(2)}) collective-permute-start(bf16[48,4224]{1,0:T(8,128)(2,1)S(1)} %slice.67), channel_id=1, source_target_pairs={{0,1},{1,0},{2,3},{3,2},{4,5},{5,4},{6,7},{7,6},{8,9},{9,8},{10,11... | collective-permute-start | bytes 1216520 | tf_op jit(solution)/shard_map/ppermute | solution.py:361
  55.9 4.2 %collective-permute-start.16 = (bf16[16,4096]{1,0:T(8,128)(2,1)S(1)}, bf16[16,4096]{1,0:T(8,128)(2,1)S(1)}, u32[]{:S(2)}, u32[]{:S(2)}) collective-permute-start(bf16[16,4096]{1,0:T(8,128)(2,1)S(1)} %add_convert_fusion.5), channel_id=1, source_target_pairs={{0,4},{1,3},{2,0},{3,7},{4,8},{5,1},{6,2},{7,11},{8,12},{9,5},{10,... | collective-permute-start | bytes 393224 | tf_op jit(solution)/shard_map/ppermute | solution.py:358
  57.6 3.9 %collective-permute-start.22 = (bf16[16,4224]{1,0:T(8,128)(2,1)S(1)}, bf16[16,4224]{1,0:T(8,128)(2,1)S(1)}, u32[]{:S(2)}, u32[]{:S(2)}) collective-permute-start(bf16[16,4224]{1,0:T(8,128)(2,1)S(1)} %add_convert_fusion.2), channel_id=1, source_target_pairs={{0,4},{1,3},{2,0},{3,7},{4,8},{5,1},{6,2},{7,11},{8,12},{9,5},{10,... | collective-permute-start | bytes 405512 | tf_op jit(solution)/shard_map/ppermute | solution.py:358
  60.1 4.2 %collective-permute-start.17 = (bf16[16,4096]{1,0:T(8,128)(2,1)S(1)}, bf16[16,4096]{1,0:T(8,128)(2,1)S(1)}, u32[]{:S(2)}, u32[]{:S(2)}) collective-permute-start(bf16[16,4096]{1,0:T(8,128)(2,1)S(1)} %add_convert_fusion.4), channel_id=1, source_target_pairs={{0,4},{1,3},{2,0},{3,7},{4,8},{5,1},{6,2},{7,11},{8,12},{9,5},{10,... | collective-permute-start | bytes 393224 | tf_op jit(solution)/shard_map/ppermute | solution.py:358
  61.6 4.1 %collective-permute-start.23 = (bf16[16,4224]{1,0:T(8,128)(2,1)S(1)}, bf16[16,4224]{1,0:T(8,128)(2,1)S(1)}, u32[]{:S(2)}, u32[]{:S(2)}) collective-permute-start(bf16[16,4224]{1,0:T(8,128)(2,1)S(1)} %add_convert_fusion.1), channel_id=1, source_target_pairs={{0,4},{1,3},{2,0},{3,7},{4,8},{5,1},{6,2},{7,11},{8,12},{9,5},{10,... | collective-permute-start | bytes 405512 | tf_op jit(solution)/shard_map/ppermute | solution.py:358
  64.4 4.2 %collective-permute-start.18 = (bf16[16,4096]{1,0:T(8,128)(2,1)S(1)}, bf16[16,4096]{1,0:T(8,128)(2,1)S(1)}, u32[]{:S(2)}, u32[]{:S(2)}) collective-permute-start(bf16[16,4096]{1,0:T(8,128)(2,1)S(1)} %add_convert_fusion.3), channel_id=1, source_target_pairs={{0,4},{1,3},{2,0},{3,7},{4,8},{5,1},{6,2},{7,11},{8,12},{9,5},{10,... | collective-permute-start | bytes 393224 | tf_op jit(solution)/shard_map/ppermute | solution.py:358
  65.8 5.6 %collective-permute-start.24 = (bf16[16,4224]{1,0:T(8,128)(2,1)S(1)}, bf16[16,4224]{1,0:T(8,128)(2,1)S(1)}, u32[]{:S(2)}, u32[]{:S(2)}) collective-permute-start(bf16[16,4224]{1,0:T(8,128)(2,1)S(1)} %add_convert_fusion), channel_id=1, source_target_pairs={{0,4},{1,3},{2,0},{3,7},{4,8},{5,1},{6,2},{7,11},{8,12},{9,5},{10,... | collective-permute-start | bytes 405512 | tf_op jit(solution)/shard_map/ppermute | solution.py:358
  68.6 6.3 %collective-permute-start.19 = (f32[16,4096]{1,0:T(8,128)S(1)}, f32[16,4096]{1,0:T(8,128)S(1)}, u32[]{:S(2)}, u32[]{:S(2)}) collective-permute-start(f32[16,4096]{1,0:T(8,128)S(1)} %convert_add_fusion.1.mine_ref), channel_id=1, source_target_pairs={{0,1},{1,0},{2,3},{3,2},{4,5},{5,4},{6,7},{7,6},{8,9},{9,8},{10,11... | collective-permute-start | bytes 786440 | tf_op jit(solution)/shard_map/ppermute | solution.py:361
  71.4 5.5 %collective-permute-start.25 = (f32[16,4224]{1,0:T(8,128)S(1)}, f32[16,4224]{1,0:T(8,128)S(1)}, u32[]{:S(2)}, u32[]{:S(2)}) collective-permute-start(f32[16,4224]{1,0:T(8,128)S(1)} %convert_add_fusion), channel_id=1, source_target_pairs={{0,1},{1,0},{2,3},{3,2},{4,5},{5,4},{6,7},{7,6},{8,9},{9,8},{10,11... | collective-permute-start | bytes 811016 | tf_op jit(solution)/shard_map/ppermute | solution.py:361
  (5 other events, 61.6 us)

commit v3 on v2

--- a/solution.py
+++ b/solution.py
@@ -88,12 +88,12 @@
     return pl.ds(pl.multiple_of(c * step, step), step)
 
 
-def pack_kernel(
-    hidden_hbm, basis_hbm, learned_hbm, bias_hbm, packed_ref, basis_ref, learned_ref, bias_ref, sems
+def pack_upstream_kernel(
+    upstream_hbm, basis_hbm, learned_hbm, bias_hbm, packed_ref, basis_ref, learned_ref, bias_ref, sems
 ):
-    width = hidden_hbm.shape[1]
+    width = upstream_hbm.shape[1]
     copies = (
-        pltpu.make_async_copy(hidden_hbm, packed_ref.at[:SEG, :width], sems.at[0]),
+        pltpu.make_async_copy(upstream_hbm, packed_ref.at[:, :width], sems.at[0]),
         pltpu.make_async_copy(basis_hbm, basis_ref, sems.at[1]),
         pltpu.make_async_copy(learned_hbm, learned_ref, sems.at[2]),
         pltpu.make_async_copy(bias_hbm, bias_ref, sems.at[3]),
@@ -102,18 +102,39 @@
         copy.start()
     for copy in copies:
         copy.wait()
-    packed_ref[SEG:, :width] = jnp.concatenate(
-        [basis_ref[0].astype(F32), learned_ref[0].astype(F32)], axis=0
-    ).astype(BF)
+    half = width // 2
+    table = jnp.concatenate(
+        [basis_ref[0, :, half:].astype(F32), learned_ref[0, :, half:].astype(F32)], axis=0
+    )
+    packed_ref[:, width : width + half] = table.astype(BF)
     shape = (SEG, PAD)
     row = lax.broadcasted_iota(jnp.int32, shape, 0)
     lane = lax.broadcasted_iota(jnp.int32, shape, 1)
-    packed_ref[:SEG, width:] = jnp.where(lane == 0, 1.0, 0.0).astype(BF)
     bias = jnp.zeros(shape, F32)
     wide = bias_ref[...].astype(F32)
     for r in range(RANK):
         bias = jnp.where((row == RANK + r) & (lane == 0), wide[:, r : r + 1], bias)
-    packed_ref[SEG:, width:] = bias.astype(BF)
+    packed_ref[:, width + half :] = bias.astype(BF)
+
+
+def pack_rows_kernel(hidden_hbm, basis_hbm, learned_hbm, packed_ref, basis_ref, learned_ref, sems):
+    width = hidden_hbm.shape[1]
+    copies = (
+        pltpu.make_async_copy(hidden_hbm, packed_ref.at[:, :width], sems.at[0]),
+        pltpu.make_async_copy(basis_hbm, basis_ref, sems.at[1]),
+        pltpu.make_async_copy(learned_hbm, learned_ref, sems.at[2]),
+    )
+    for copy in copies:
+        copy.start()
+    for copy in copies:
+        copy.wait()
+    lane = lax.broadcasted_iota(jnp.int32, (SEG, PAD), 1)
+    packed_ref[:, width : width + PAD] = jnp.where(lane == 0, 1.0, 0.0).astype(BF)
+    half = width // 2
+    table = jnp.concatenate(
+        [basis_ref[0, :, :half].astype(F32), learned_ref[0, :, :half].astype(F32)], axis=0
+    )
+    packed_ref[:, width + PAD :] = table.astype(BF)
 
 
 def mark_kernel(after, out_ref):
@@ -122,9 +143,11 @@
 
 
 def back_kernel(n, *refs):
-    pieces, (down_ref, upstream_ref, back_ref) = refs[:n], refs[-3:]
+    pieces, (down_ref, upstream_ref, tables_ref, back_ref) = refs[:n], refs[-4:]
+    width = upstream_ref.shape[1]
     for k, piece in enumerate(pieces):
-        upstream_ref[k * SEG : (k + 1) * SEG, :] = piece[...]
+        upstream_ref[k * SEG : (k + 1) * SEG, :] = piece[:, :width]
+        tables_ref[k * SEG : (k + 1) * SEG, :] = piece[:, width:]
     back_ref[...] = dot_nt(upstream_ref[...], down_ref[...])
 
 
@@ -134,6 +157,7 @@
     (
         gain_ref,
         back_ref,
+        right_ref,
         gate_ref,
         up_ref,
         own_ref,
@@ -143,6 +167,7 @@
         tables_ref,
         middle_ref,
         coeffs_ref,
+        weights_ref,
         stats_ref,
         normed_ref,
         gate_grad_ref,
@@ -151,8 +176,9 @@
     row_total, width = middle_ref.shape
     chunks = width // step
     for k, piece in enumerate(pieces):
-        rows_ref[k * SEG : (k + 1) * SEG, :] = piece[:SEG, :]
-        tables_ref[k * SEG : (k + 1) * SEG, :] = piece[SEG:, :]
+        rows_ref[k * SEG : (k + 1) * SEG, :] = piece[:, : width + PAD]
+        tables_ref[k * SEG : (k + 1) * SEG, : width // 2] = piece[:, width + PAD :]
+    tables_ref[:, width // 2 :] = right_ref[...]
 
     columns = tables_ref.shape[0]
     products = dot_nt(rows_ref[...], tables_ref[...])
@@ -161,7 +187,8 @@
     coeffs_ref[...] = coeffs
     coeff_high, coeff_low = split(coeffs)
 
-    def middle_step(c, squares):
+    def middle_step(c, carry):
+        squares, middle_tables = carry
         cols = columns_at(c, step)
         table = tables_ref[:, cols]
         value = rows_ref[:, cols].astype(F32) + (
@@ -169,10 +196,13 @@
         )
         value = value.astype(BF)
         middle_ref[:, cols] = value
+        middle_tables = middle_tables + dot_nt(value, table)
         value = value.astype(F32)
-        return squares + jnp.sum(value * value, axis=1, keepdims=True)
-
-    squares = lax.fori_loop(0, chunks, middle_step, jnp.zeros((row_total, 1), F32))
+        return squares + jnp.sum(value * value, axis=1, keepdims=True), middle_tables
+
+    column_zero = jnp.zeros((row_total, 1), F32)
+    square_zero = jnp.zeros((row_total, columns), F32)
+    squares, middle_tables = lax.fori_loop(0, chunks, middle_step, (column_zero, square_zero))
     inverse = lax.rsqrt(squares / width + EPS)
 
     def normed_step(c, carry):
@@ -194,85 +224,104 @@
         gate_grad_ref[:, cols] = (back * upward * sigma * (1.0 + gate * (1.0 - sigma))).astype(BF)
         up_grad_ref[:, cols] = (back * gate * sigma).astype(BF)
 
-    def scaled_step(c, inner):
+    def scaled_step(c, carry):
+        inner, scaled_tables = carry
         cols = columns_at(c, step)
         value = dot_nt(gate_grad_ref[...], gate_ref[cols, :])
         value = value + dot_nt(up_grad_ref[...], up_ref[cols, :])
         value = value * gain_ref[:, cols]
         scaled_ref[:, cols] = value
         own_ref[:, cols] = value[:SEG]
+        high = value.astype(BF)
+        sent_ref[:, cols] = high[SEG:]
+        scaled_tables = scaled_tables + dot_nt(high, tables_ref[:, cols])
+        inner = inner + jnp.sum(value * middle_ref[:, cols].astype(F32), axis=1, keepdims=True)
+        return inner, scaled_tables
+
+    inner, scaled_tables = lax.fori_loop(0, chunks, scaled_step, (column_zero, square_zero))
+    shrink = inverse * inverse * (inner / width)
+    lane = lax.broadcasted_iota(jnp.int32, stats_ref.shape, 1)
+    stats_ref[...] = jnp.where(lane == 0, inverse, shrink)
+    pulled = mask * (inverse * (scaled_tables - shrink * middle_tables))
+    pulled = pltpu.roll(pulled, RANK, 1) - pulled
+    weights_ref[:, :row_total] = coeffs.T.astype(BF)
+    weights_ref[:, row_total:] = pulled.T.astype(BF)
+
+
+def slot_kernel(
+    step,
+    scaled_ref,
+    rows_ref,
+    middle_ref,
+    weights_ref,
+    stats_ref,
+    own_ref,
+    sent_ref,
+):
+    row_total, width = middle_ref.shape
+    inverse, shrink = stats_ref[:, 0:1], stats_ref[:, 1:2]
+
+    def slot_step(c, carry):
+        cols = columns_at(c, step)
+        value = inverse * (scaled_ref[:, cols] - middle_ref[:, cols].astype(F32) * shrink)
+        both = jnp.concatenate([value.astype(BF), rows_ref[:, cols]], axis=0)
+        value = dot_nn(weights_ref[...], both)
         sent_ref[:, cols] = value[SEG:].astype(BF)
-        return inner + jnp.sum(value * middle_ref[:, cols].astype(F32), axis=1, keepdims=True)
-
-    inner = lax.fori_loop(0, chunks, scaled_step, jnp.zeros((row_total, 1), F32))
-    lane = lax.broadcasted_iota(jnp.int32, stats_ref.shape, 1)
-    stats_ref[...] = jnp.where(lane == 0, inverse, inverse * inverse * (inner / width))
-
-
-def slot_kernel(
+        own_ref[:, cols] = value[:SEG]
+        return carry
+
+    lax.fori_loop(0, width // step, slot_step, 0)
+    value = dot_nn(weights_ref[:, row_total:], rows_ref[:, width:])
+    sent_ref[:, width:] = value[SEG:].astype(BF)
+    own_ref[:, width:] = value[:SEG]
+
+
+def local_kernel(
     n,
     step,
     where_ref,
     counts_ref,
     starts_ref,
     slots_ref,
-    scaled_ref,
     rows_ref,
     tables_ref,
     upstream_ref,
-    middle_ref,
     coeffs_ref,
-    stats_ref,
-    own_ref,
-    sent_ref,
-    total_ref,
+    local_ref,
 ):
-    row_total, width = middle_ref.shape
+    row_total, width = upstream_ref.shape
     columns = tables_ref.shape[0]
-    chunks = width // step
-    inverse, shrink = stats_ref[:, 0:1], stats_ref[:, 1:2]
-
-    def total_step(c, carry):
-        pulled, pulled_up = carry
-        cols = columns_at(c, step)
-        value = inverse * (scaled_ref[:, cols] - middle_ref[:, cols].astype(F32) * shrink)
-        high, low = split(value)
-        total_ref[0, :, cols] = high
-        total_ref[1, :, cols] = low
-        table = tables_ref[:, cols]
-        pulled = pulled + (dot_nt(high, table) + dot_nt(low, table))
-        return pulled, pulled_up + dot_nt(upstream_ref[:, cols], table)
-
-    zero = jnp.zeros((row_total, columns), F32)
-    pulled, pulled_up = lax.fori_loop(0, chunks, total_step, (zero, zero))
     mask = tenant_mask(n, where_ref, counts_ref, starts_ref, slots_ref)
     lane = lax.broadcasted_iota(jnp.int32, (row_total, columns), 1)
-    first_slot = jnp.where(lane < RANK, 0.5, 0.0)
-    pulled = mask * (pulled + first_slot * pulled_up)
+    first = lane < RANK
+    pulled = jnp.where(first, mask, 0.0) * dot_nt(upstream_ref[...], tables_ref[:, :width])
     pulled = pltpu.roll(pulled, RANK, 1) - pulled
-    coeffs = coeffs_ref[...]
-    coeff_high, coeff_low = split(coeffs.T)
-    first_high, first_low = split((coeffs * first_slot).T[:SEG])
-    pulled_high, pulled_low = split(pulled.T)
-
-    def slot_step(c, carry):
+    coeffs = jnp.where(first, coeffs_ref[...], 0.0)
+    coeff_high, coeff_low = split(coeffs.T[:SEG])
+    pulled_high, pulled_low = split(pulled.T[:SEG])
+
+    def local_step(c, carry):
         cols = columns_at(c, step)
-        high, low = total_ref[0, :, cols], total_ref[1, :, cols]
-        rows = rows_ref[:, cols]
-        value = dot_nn(coeff_high, high) + dot_nn(coeff_high, low) + dot_nn(coeff_low, high)
-        value = value + dot_nn(pulled_high, rows) + dot_nn(pulled_low, rows)
-        sent_ref[:, cols] = value[SEG:].astype(BF)
-        upstream = upstream_ref[:, cols]
-        own_ref[:, cols] = value[:SEG] + (
-            dot_nn(first_high, upstream) + dot_nn(first_low, upstream)
-        )
+        upstream, rows = upstream_ref[:, cols], rows_ref[:, cols]
+        value = dot_nn(coeff_high, upstream) + dot_nn(coeff_low, upstream)
+        local_ref[:, cols] = value + (dot_nn(pulled_high, rows) + dot_nn(pulled_low, rows))
         return carry
 
-    lax.fori_loop(0, chunks, slot_step, 0)
-    extra = rows_ref[:, width:]
-    value = dot_nn(pulled_high, extra) + dot_nn(pulled_low, extra)
-    sent_ref[:, width:] = value[SEG:].astype(BF)
-    own_ref[:, width:] = value[:SEG]
+    lax.fori_loop(0, width // step, local_step, 0)
+    rows = rows_ref[:, width:]
+    local_ref[:, width:] = dot_nn(pulled_high, rows) + dot_nn(pulled_low, rows)
+
+
+def ends_kernel(mine_ref, other_ref, local_ref, after, basis_ref, learned_ref, bias_ref):
+    del after
+    width = basis_ref.shape[2]
+    value = mine_ref[...] + other_ref[...] + local_ref[...]
+    basis_ref[0, :, :] = value[:RANK, :width]
+    learned_ref[0, :, :] = value[RANK:, :width]
+    row = lax.broadcasted_iota(jnp.int32, (RANK, RANK), 0)
+    lane = lax.broadcasted_iota(jnp.int32, (RANK, RANK), 1)
+    bias = jnp.where(row == lane, value[RANK:, width : width + 1], 0.0)
+    bias_ref[...] = jnp.sum(bias, axis=0, keepdims=True)
 
 
 def rows_kernel(
@@ -316,13 +365,16 @@
 LONG_FLOPS = 40 * 10**9
 SMEM_SPEC = pl.BlockSpec(memory_space=pltpu.SMEM)
 VMEM_SPEC = pl.BlockSpec(memory_space=pltpu.VMEM)
-
-
-def call(kernel, outs, scalars, arrays, scratch=(), flops=0, moved=0, limit=4, spec=None):
+ANY_SPEC = pl.BlockSpec(memory_space=pl.ANY)
+
+
+def call(kernel, outs, scalars, arrays, scratch=(), flops=0, moved=0, limit=4, spec=None, loose=0):
     return pl.pallas_call(
         kernel,
         out_shape=tuple(jax.ShapeDtypeStruct(s, d) for s, d in outs),
-        in_specs=[SMEM_SPEC] * len(scalars) + [spec or VMEM_SPEC] * len(arrays),
+        in_specs=[SMEM_SPEC] * len(scalars)
+        + [spec or VMEM_SPEC] * (len(arrays) - loose)
+        + [ANY_SPEC] * loose,
         out_specs=tuple(VMEM_SPEC for _ in outs),
         scratch_shapes=list(scratch),
         compiler_params=pltpu.CompilerParams(vmem_limit_bytes=limit * 1024 * 1024),
@@ -399,33 +451,47 @@
         work = 2 * rows_total * width * hidden
         where = jnp.stack([lax.axis_index("dp"), lax.axis_index("tensor")]).astype(jnp.int32)
         scalars = (where, row_counts, segment_starts, owner_slot)
-        (packed,) = call(
-            pack_kernel,
-            [((2 * SEG, wide), BF)],
+        tables_scratch = [
+            pltpu.VMEM(tenant_basis.shape, BF),
+            pltpu.VMEM(tenant_learned.shape, BF),
+        ]
+        hbm = pl.BlockSpec(memory_space=pltpu.MemorySpace.HBM)
+        (packed_upstream,) = call(
+            pack_upstream_kernel,
+            [((SEG, width + width // 2 + PAD), BF)],
             (),
-            tuple(remote(x) for x in (hidden_in, tenant_basis, tenant_learned, tenant_bias)),
-            scratch=[
-                pltpu.VMEM(tenant_basis.shape, BF),
-                pltpu.VMEM(tenant_learned.shape, BF),
-                pltpu.VMEM(tenant_bias.shape, BF),
-                pltpu.SemaphoreType.DMA((4,)),
+            tuple(remote(x) for x in (grad_out, tenant_basis, tenant_learned, tenant_bias)),
+            scratch=tables_scratch
+            + [pltpu.VMEM(tenant_bias.shape, BF), pltpu.SemaphoreType.DMA((4,))],
+            moved=4 * SEG * wide * 2,
+            spec=hbm,
+        )
+        (packed_rows,) = call(
+            pack_rows_kernel,
+            [((SEG, width + width // 2 + PAD), BF)],
+            (),
+            tuple(remote(x) for x in (hidden_in, tenant_basis, tenant_learned)),
+            scratch=tables_scratch + [pltpu.SemaphoreType.DMA((3,))],
+            moved=4 * SEG * wide * 2,
+            spec=hbm,
+        )
+        upstream_pieces = gather(packed_upstream)
+        row_pieces = gather(packed_rows)
+        marks = tuple(mark(x) for x in (packed_rows, upstream_pieces[1], upstream_pieces[2]))
+        upstream, right, back = call(
+            functools.partial(back_kernel, n),
+            [
+                ((rows_total, width), BF),
+                ((rows_total, width // 2 + PAD), BF),
+                ((rows_total, hidden), F32),
             ],
-            moved=4 * SEG * wide * 2,
-            spec=pl.BlockSpec(memory_space=pl.ANY),
-        )
-        upstream_pieces = gather(grad_out)
-        packed_pieces = gather(packed)
-        marks = tuple(mark(x) for x in (packed, upstream_pieces[1], upstream_pieces[2]))
-        upstream, back = call(
-            functools.partial(back_kernel, n),
-            [((rows_total, width), BF), ((rows_total, hidden), F32)],
             (),
             (*upstream_pieces, *marks, resident(down_weight)),
             flops=LONG_FLOPS,
             moved=2 * width * hidden,
             limit=n,
         )
-        own, sent, scaled, rows, tables, middle, coeffs, stats = call(
+        own, sent, scaled, rows, tables, middle, coeffs, weights, stats = call(
             functools.partial(hidden_kernel, n, 1024),
             [
                 ((SEG, width), F32),
@@ -435,13 +501,15 @@
                 ((rows_total, wide), BF),
                 ((rows_total, width), BF),
                 ((rows_total, rows_total), F32),
+                ((rows_total, 2 * rows_total), BF),
                 ((rows_total, 128), F32),
             ],
             scalars,
             (
-                *packed_pieces,
+                *row_pieces,
                 norm_gain.reshape(1, width),
                 back,
+                right,
                 resident(gate_weight),
                 resident(up_weight),
             ),
@@ -455,11 +523,19 @@
             limit=n + n // 2,
         )
         own_slot, sent_slot = call(
-            functools.partial(slot_kernel, n, 512),
+            functools.partial(slot_kernel, 1024),
             [((SEG, wide), F32), ((rows_total - SEG, wide), BF)],
+            (),
+            (scaled, rows, middle, weights, stats),
+            flops=work,
+            moved=10 * rows_total * width,
+            limit=n + n // 2,
+        )
+        (local,) = call(
+            functools.partial(local_kernel, n, 1024),
+            [((SEG, wide), F32)],
             scalars,
-            (scaled, rows, tables, upstream, middle, coeffs, stats),
-            scratch=[pltpu.VMEM((2, rows_total, width), BF)],
+            (rows, tables, upstream, coeffs),
             flops=work,
             moved=10 * rows_total * width,
             limit=n + n // 2,
@@ -475,13 +551,15 @@
             flops=LONG_FLOPS,
             moved=14 * SEG * width,
         )
-        slots = slots + swap(slots)
-        return (
-            grad_rows,
-            slots[None, :RANK, :width],
-            slots[None, RANK:, :width],
-            slots[None, RANK:, width],
-        )
+        outs = call(
+            ends_kernel,
+            [((1, RANK, width), F32), ((1, RANK, width), F32), ((1, RANK), F32)],
+            (),
+            (slots, swap(slots), local, grad_rows),
+            moved=20 * SEG * width,
+            loose=1,
+        )
+        return (grad_rows, *outs)
 
     return on_device
 

time: 78.5 us -> 70.8 us (0.902)
  starting transfers between devices: 36.9 us -> 30.1 us
    ppermute x10, starting transfers between devices: 21.9 us -> 17.4 us  [swap(): return lax.ppermute(x, 'tensor', [(0, 1), (1, 0)])]
    ppermute x16, starting transfers between devices: 15 us -> 12.7 us  [hop(): return lax.ppermute(x, ('dp', 'tensor'), pairs)]
    unnamed x22 -> x24, local copies, waits for them, and re-layouts: 0.06 us -> 0.96 us
    pallas_call x8 -> x11, Pallas kernels: 24.7 us -> 24.3 us  [call(): pl.pallas_call(kernel, out_shape=tuple((jax.ShapeDtypeStruct(s, d) for s,...]
  transfers between devices with their start and end apart: 26 -> 26, of which waited for: 9 -> 9; matrix products, arithmetic and copies ran while one was open for 1% -> 1% of each run, Pallas kernels for 16% -> 14%
where the time goes in v3:
time: 70.8 us; the launch traced here: 70.6 us
  starting transfers between devices  30.1 us (43%)
  Pallas kernels  24.3 us (34%)
  waiting for transfers between devices  13.8 us (19%)
  local copies, waits for them, and re-layouts  1.04 us (1%)
  between operations  0.95 us (1%)
    pallas_call x11, Pallas kernels, call(): pl.pallas_call(kernel, out_shape=tuple((jax.ShapeDtypeStruct(s, d) for s,...  24.3 us
    ppermute x10, starting transfers between devices, swap(): return lax.ppermute(x, 'tensor', [(0, 1), (1, 0)])  17.4 us
    ppermute x16, waiting for transfers between devices, hop(): return lax.ppermute(x, ('dp', 'tensor'), pairs)  13.7 us
    ppermute x16, starting transfers between devices, hop(): return lax.ppermute(x, ('dp', 'tensor'), pairs)  12.7 us
  transfers between devices with their start and end apart: 26, of which 9 were waited for; matrix products, arithmetic and copies ran while one was open for 1% of the time, Pallas kernels for 14%

profile of v3, /device:TPU:1, one launch (start us, length us, event | category | flops | bytes accessed | tf_op | source)
XLA Modules:
  0.0 70.6 jit_solution(18431586317163106843)
XLA Ops:
  0.6 1.1 %shard_map.148.refs_0_ = bf16[16,6272]{1,0:T(8,128)(2,1)S(1)} custom-call(bf16[16,4096]{1,0:T(8,128)(2,1)} %upstream_ref.1, bf16[1,8,4096]{2,1,0:T(8,128)(2,1)} %basis_hbm.3, bf16[1,8,4096]{2,1,0:T(8,128)(2,1)} %learned_hbm.3, bf16[1,8]{1,0:T(2,128)(2,1)} %bias_hbm.1), custom_call_target="tpu_custom_call" | custom-call | bytes 540672 | tf_op jit(solution)/shard_map/pallas_call | solution.py:372
  1.7 2.1 %collective-permute-start.7 = (bf16[16,6272]{1,0:T(8,128)(2,1)S(1)}, bf16[16,6272]{1,0:T(8,128)(2,1)S(1)}, u32[]{:S(2)}, u32[]{:S(2)}) collective-permute-start(bf16[16,6272]{1,0:T(8,128)(2,1)S(1)} %shard_map.148.refs_0_), channel_id=1, source_target_pairs={{0,4},{1,3},{2,0},{3,7},{4,8},{5,1},{6,2},{7,11},{8,12},{9,5},{10,... | collective-permute-start | bytes 602120 | tf_op jit(solution)/shard_map/ppermute | solution.py:410
  3.9 1.0 %shard_map.147.after.refs_4_ = bf16[16,6272]{1,0:T(8,128)(2,1)S(1)} custom-call(bf16[16,4096]{1,0:T(8,128)(2,1)} %hidden_hbm.1, bf16[1,8,4096]{2,1,0:T(8,128)(2,1)} %basis_hbm.3, bf16[1,8,4096]{2,1,0:T(8,128)(2,1)} %learned_hbm.3), custom_call_target="tpu_custom_call" | custom-call | bytes 540672 | tf_op jit(solution)/shard_map/pallas_call | solution.py:372
  4.8 1.3 %collective-permute-start = (bf16[16,6272]{1,0:T(8,128)(2,1)S(1)}, bf16[16,6272]{1,0:T(8,128)(2,1)S(1)}, u32[]{:S(2)}, u32[]{:S(2)}) collective-permute-start(bf16[16,6272]{1,0:T(8,128)(2,1)S(1)} %shard_map.147.after.refs_4_), channel_id=1, source_target_pairs={{0,4},{1,3},{2,0},{3,7},{4,8},{5,1},{6,2},{7,11},{8,12},{9,5},{10,... | collective-permute-start | bytes 602120 | tf_op jit(solution)/shard_map/ppermute | solution.py:410
  6.2 1.1 %collective-permute-done.7.after.refs_1_ = bf16[16,6272]{1,0:T(8,128)(2,1)S(1)} collective-permute-done((bf16[16,6272]{1,0:T(8,128)(2,1)S(1)}, bf16[16,6272]{1,0:T(8,128)(2,1)S(1)}, u32[]{:S(2)}, u32[]{:S(2)}) %collective-permute-start.7) | collective-permute-done | bytes 200736 | tf_op jit(solution)/shard_map/ppermute | solution.py:410
  7.3 1.4 %collective-permute-start.8 = (bf16[16,6272]{1,0:T(8,128)(2,1)S(1)}, bf16[16,6272]{1,0:T(8,128)(2,1)S(1)}, u32[]{:S(2)}, u32[]{:S(2)}) collective-permute-start(bf16[16,6272]{1,0:T(8,128)(2,1)S(1)} %collective-permute-done.7.after.refs_1_), channel_id=1, source_target_pairs={{0,4},{1,3},{2,0},{3,7},{4,8},{5,1},{6,2},{7,11},{8,12},{9,5},{10,... | collective-permute-start | bytes 602120 | tf_op jit(solution)/shard_map/ppermute | solution.py:410
  8.8 1.9 %collective-permute-start.10 = (bf16[16,6272]{1,0:T(8,128)(2,1)S(1)}, bf16[16,6272]{1,0:T(8,128)(2,1)S(1)}, u32[]{:S(2)}, u32[]{:S(2)}) collective-permute-start(bf16[16,6272]{1,0:T(8,128)(2,1)S(1)} %collective-permute-done.7.after.refs_1_), channel_id=1, source_target_pairs={{0,1},{1,0},{2,3},{3,2},{4,5},{5,4},{6,7},{7,6},{8,9},{9,8},{10,11... | collective-permute-start | bytes 602120 | tf_op jit(solution)/shard_map/ppermute | solution.py:413
  11.0 1.1 %collective-permute-done.8.after.refs_2_ = bf16[16,6272]{1,0:T(8,128)(2,1)S(1)} collective-permute-done((bf16[16,6272]{1,0:T(8,128)(2,1)S(1)}, bf16[16,6272]{1,0:T(8,128)(2,1)S(1)}, u32[]{:S(2)}, u32[]{:S(2)}) %collective-permute-start.8) | collective-permute-done | bytes 200736 | tf_op jit(solution)/shard_map/ppermute | solution.py:410
  12.2 1.4 %collective-permute-start.9 = (bf16[16,6272]{1,0:T(8,128)(2,1)S(1)}, bf16[16,6272]{1,0:T(8,128)(2,1)S(1)}, u32[]{:S(2)}, u32[]{:S(2)}) collective-permute-start(bf16[16,6272]{1,0:T(8,128)(2,1)S(1)} %collective-permute-done.8.after.refs_2_), channel_id=1, source_target_pairs={{0,4},{1,3},{2,0},{3,7},{4,8},{5,1},{6,2},{7,11},{8,12},{9,5},{10,... | collective-permute-start | bytes 602120 | tf_op jit(solution)/shard_map/ppermute | solution.py:410
  13.6 2.7 %collective-permute-start.11 = (bf16[16,6272]{1,0:T(8,128)(2,1)S(1)}, bf16[16,6272]{1,0:T(8,128)(2,1)S(1)}, u32[]{:S(2)}, u32[]{:S(2)}) collective-permute-start(bf16[16,6272]{1,0:T(8,128)(2,1)S(1)} %collective-permute-done.8.after.refs_2_), channel_id=1, source_target_pairs={{0,1},{1,0},{2,3},{3,2},{4,5},{5,4},{6,7},{7,6},{8,9},{9,8},{10,11... | collective-permute-start | bytes 602120 | tf_op jit(solution)/shard_map/ppermute | solution.py:413
  16.3 1.4 %collective-permute-done.9.refs_3_ = bf16[16,6272]{1,0:T(8,128)(2,1)S(1)} collective-permute-done((bf16[16,6272]{1,0:T(8,128)(2,1)S(1)}, bf16[16,6272]{1,0:T(8,128)(2,1)S(1)}, u32[]{:S(2)}, u32[]{:S(2)}) %collective-permute-start.9) | collective-permute-done | bytes 200736 | tf_op jit(solution)/shard_map/ppermute | solution.py:410
  18.1 3.9 %collective-permute-start.12 = (bf16[16,6272]{1,0:T(8,128)(2,1)S(1)}, bf16[16,6272]{1,0:T(8,128)(2,1)S(1)}, u32[]{:S(2)}, u32[]{:S(2)}) collective-permute-start(bf16[16,6272]{1,0:T(8,128)(2,1)S(1)} %collective-permute-done.9.refs_3_), channel_id=1, source_target_pairs={{0,1},{1,0},{2,3},{3,2},{4,5},{5,4},{6,7},{7,6},{8,9},{9,8},{10,11... | collective-permute-start | bytes 602120 | tf_op jit(solution)/shard_map/ppermute | solution.py:413
  22.7 0.6 collective-permute-done.13.refs_7_
  23.3 2.3 %collective-permute-start.5 = (bf16[16,6272]{1,0:T(8,128)(2,1)S(1)}, bf16[16,6272]{1,0:T(8,128)(2,1)S(1)}, u32[]{:S(2)}, u32[]{:S(2)}) collective-permute-start(bf16[16,6272]{1,0:T(8,128)(2,1)S(1)} %collective-permute-done.2.refs_7_), channel_id=1, source_target_pairs={{0,1},{1,0},{2,3},{3,2},{4,5},{5,4},{6,7},{7,6},{8,9},{9,8},{10,11... | collective-permute-start | bytes 602120 | tf_op jit(solution)/shard_map/ppermute | solution.py:413
  25.7 2.9 %shard_map.152 = (bf16[128,4096]{1,0:T(8,128)(2,1)S(1)}, bf16[128,2176]{1,0:T(8,128)(2,1)S(1)}, f32[128,1024]{1,0:T(8,128)S(1)}) custom-call(bf16[16,6272]{1,0:T(8,128)(2,1)S(1)} %shard_map.148.refs_0_, bf16[16,6272]{1,0:T(8,128)(2,1)S(1)} %collective-permute-done.7.after.refs_1_, bf16[16,6272]{1,0:T(8,128)(2,1)S(1)} %collective-permute-done.8.after.refs_2_, ...), custom_call_target="tpu_custom_call" | custom-call | flops 40000000000 | bytes 8388608 | tf_op jit(solution)/shard_map/pallas_call | solution.py:372
  28.7 12.8 %shard_map.153 = (f32[16,4096]{1,0:T(8,128)S(1)}, bf16[112,4096]{1,0:T(8,128)(2,1)S(1)}, f32[128,4096]{1,0:T(8,128)S(1)}, bf16[128,4224]{1,0:T(8,128)(2,1)S(1)},...) custom-call(s32[2]{0:T(128)S(1)} %pad_add_fusion.refs_0_.where_ref, ...), custom_call_target="tpu_custom_call" | custom-call | flops 4294967296 | bytes 16777216 | tf_op jit(solution)/shard_map/pallas_call | solution.py:372
  41.8 1.7 %collective-permute-start.14 = (bf16[16,4096]{1,0:T(8,128)(2,1)S(1)}, bf16[16,4096]{1,0:T(8,128)(2,1)S(1)}, u32[]{:S(2)}, u32[]{:S(2)}) collective-permute-start(bf16[16,4096]{1,0:T(8,128)(2,1)S(1)} %slice.48), channel_id=1, source_target_pairs={{0,4},{1,3},{2,0},{3,7},{4,8},{5,1},{6,2},{7,11},{8,12},{9,5},{10,... | collective-permute-start | bytes 393224 | tf_op jit(solution)/shard_map/ppermute | solution.py:410
  43.5 1.5 %shard_map.155 = (f32[16,4224]{1,0:T(8,128)S(1)}, bf16[112,4224]{1,0:T(8,128)(2,1)S(1)}) custom-call(f32[128,4096]{1,0:T(8,128)S(1)} %get-tuple-element.28.scaled_ref, bf16[128,4224]{1,0:T(8,128)(2,1)S(1)} %get-tuple-element.29.rows_ref, bf16[128,4096]{1,0:T(8,128)(2,1)S(1)} %get-tuple-element.25.middle_ref, ...), custom_call_target="tpu_custom_call" | custom-call | flops 1073741824 | bytes 5242880 | tf_op jit(solution)/shard_map/pallas_call | solution.py:372
  45.0 1.3 %collective-permute-start.20 = (bf16[16,4224]{1,0:T(8,128)(2,1)S(1)}, bf16[16,4224]{1,0:T(8,128)(2,1)S(1)}, u32[]{:S(2)}, u32[]{:S(2)}) collective-permute-start(bf16[16,4224]{1,0:T(8,128)(2,1)S(1)} %slice.56), channel_id=1, source_target_pairs={{0,4},{1,3},{2,0},{3,7},{4,8},{5,1},{6,2},{7,11},{8,12},{9,5},{10,... | collective-permute-start | bytes 405512 | tf_op jit(solution)/shard_map/ppermute | solution.py:410
  46.4 1.1 %collective-permute-start.21 = (bf16[48,4224]{1,0:T(8,128)(2,1)S(1)}, bf16[48,4224]{1,0:T(8,128)(2,1)S(1)}, u32[]{:S(2)}, u32[]{:S(2)}) collective-permute-start(bf16[48,4224]{1,0:T(8,128)(2,1)S(1)} %slice.58), channel_id=1, source_target_pairs={{0,1},{1,0},{2,3},{3,2},{4,5},{5,4},{6,7},{7,6},{8,9},{9,8},{10,11... | collective-permute-start | bytes 1216520 | tf_op jit(solution)/shard_map/ppermute | solution.py:413
  47.5 2.3 %shard_map.156.local_ref = f32[16,4224]{1,0:T(8,128)S(1)} custom-call(s32[2]{0:T(128)S(1)} %pad_add_fusion.refs_0_.where_ref, s32[8]{0:T(128)S(1)} %copy-done.3, s32[8]{0:T(128)S(1)} %copy-done.4, s32[8]{0:T(128)S(1)} %copy-done.5, bf16[128,4224]{1,0:T(8,128)(2,1)S(1)} %get-tuple-element.29.rows_ref, bf16[128,4224]{1,0:T(8,128)(2,1)S(1)} %get-tuple-element.27.tables_ref, ...), custom_call_target="tpu_custom_call" | custom-call | flops 1073741824 | bytes 5242880 | tf_op jit(solution)/shard_map/pallas_call | solution.py:372
  50.1 1.4 %collective-permute-start.22 = (bf16[16,4224]{1,0:T(8,128)(2,1)S(1)}, bf16[16,4224]{1,0:T(8,128)(2,1)S(1)}, u32[]{:S(2)}, u32[]{:S(2)}) collective-permute-start(bf16[16,4224]{1,0:T(8,128)(2,1)S(1)} %add_convert_fusion.2), channel_id=1, source_target_pairs={{0,4},{1,3},{2,0},{3,7},{4,8},{5,1},{6,2},{7,11},{8,12},{9,5},{10,... | collective-permute-start | bytes 405512 | tf_op jit(solution)/shard_map/ppermute | solution.py:410
  51.5 2.5 %collective-permute-done.16 = bf16[16,4096]{1,0:T(8,128)(2,1)S(1)} collective-permute-done((bf16[16,4096]{1,0:T(8,128)(2,1)S(1)}, bf16[16,4096]{1,0:T(8,128)(2,1)S(1)}, u32[]{:S(2)}, u32[]{:S(2)}) %collective-permute-start.16) | collective-permute-done | bytes 131104 | tf_op jit(solution)/shard_map/ppermute | solution.py:410
  54.3 1.1 %collective-permute-done.22 = bf16[16,4224]{1,0:T(8,128)(2,1)S(1)} collective-permute-done((bf16[16,4224]{1,0:T(8,128)(2,1)S(1)}, bf16[16,4224]{1,0:T(8,128)(2,1)S(1)}, u32[]{:S(2)}, u32[]{:S(2)}) %collective-permute-start.22) | collective-permute-done | bytes 135200 | tf_op jit(solution)/shard_map/ppermute | solution.py:410
  55.7 2.5 %collective-permute-done.17 = bf16[16,4096]{1,0:T(8,128)(2,1)S(1)} collective-permute-done((bf16[16,4096]{1,0:T(8,128)(2,1)S(1)}, bf16[16,4096]{1,0:T(8,128)(2,1)S(1)}, u32[]{:S(2)}, u32[]{:S(2)}) %collective-permute-start.17) | collective-permute-done | bytes 131104 | tf_op jit(solution)/shard_map/ppermute | solution.py:410
  58.3 1.2 %collective-permute-done.23 = bf16[16,4224]{1,0:T(8,128)(2,1)S(1)} collective-permute-done((bf16[16,4224]{1,0:T(8,128)(2,1)S(1)}, bf16[16,4224]{1,0:T(8,128)(2,1)S(1)}, u32[]{:S(2)}, u32[]{:S(2)}) %collective-permute-start.23) | collective-permute-done | bytes 135200 | tf_op jit(solution)/shard_map/ppermute | solution.py:410
  60.0 2.1 %collective-permute-done.18 = bf16[16,4096]{1,0:T(8,128)(2,1)S(1)} collective-permute-done((bf16[16,4096]{1,0:T(8,128)(2,1)S(1)}, bf16[16,4096]{1,0:T(8,128)(2,1)S(1)}, u32[]{:S(2)}, u32[]{:S(2)}) %collective-permute-start.18) | collective-permute-done | bytes 131104 | tf_op jit(solution)/shard_map/ppermute | solution.py:410
  62.1 2.9 %collective-permute-start.19 = (f32[16,4096]{1,0:T(8,128)S(1)}, f32[16,4096]{1,0:T(8,128)S(1)}, u32[]{:S(2)}, u32[]{:S(2)}) collective-permute-start(f32[16,4096]{1,0:T(8,128)S(1)} %convert_add_fusion.1.mine_ref), channel_id=1, source_target_pairs={{0,1},{1,0},{2,3},{3,2},{4,5},{5,4},{6,7},{7,6},{8,9},{9,8},{10,11... | collective-permute-start | bytes 786440 | tf_op jit(solution)/shard_map/ppermute | solution.py:413
  65.1 1.8 %collective-permute-start.25 = (f32[16,4224]{1,0:T(8,128)S(1)}, f32[16,4224]{1,0:T(8,128)S(1)}, u32[]{:S(2)}, u32[]{:S(2)}) collective-permute-start(f32[16,4224]{1,0:T(8,128)S(1)} %convert_add_fusion.mine_ref), channel_id=1, source_target_pairs={{0,1},{1,0},{2,3},{3,2},{4,5},{5,4},{6,7},{7,6},{8,9},{9,8},{10,11... | collective-permute-start | bytes 811016 | tf_op jit(solution)/shard_map/ppermute | solution.py:413
  66.9 2.1 %shard_map.154.after = bf16[16,4096]{1,0:T(8,128)(2,1)} custom-call(s32[2]{0:T(128)S(1)} %pad_add_fusion.refs_0_.where_ref, s32[8]{0:T(128)S(1)} %copy-done.3, s32[8]{0:T(128)S(1)} %copy-done.4, s32[8]{0:T(128)S(1)} %copy-done.5, f32[16,4096]{1,0:T(8,128)S(1)} %convert_add_fusion.1.mine_ref, f32[16,4096]{1,0:T(8,128)S(1)} %collective-permute-done.19.other_ref, ...), custom_call_target="tpu_custom_call" | custom-call | flops 40000000000 | bytes 917504 | tf_op jit(solution)/shard_map/pallas_call | solution.py:372
  69.0 0.9 %copy-done.1 = bf16[16,4096]{1,0:T(8,128)(2,1)S(1)} copy-done((bf16[16,4096]{1,0:T(8,128)(2,1)S(1)}, bf16[16,4096]{1,0:T(8,128)(2,1)}, u32[]{:S(2)}) %copy-start.1) | copy-done | bytes 131096
  69.9 0.7 %shard_map.157 = (f32[1,8,4096]{2,1,0:T(8,128)}, f32[1,8,4096]{2,1,0:T(8,128)}, f32[1,8]{1,0:T(1,128)}) custom-call(f32[16,4224]{1,0:T(8,128)S(1)} %convert_add_fusion.mine_ref, f32[16,4224]{1,0:T(8,128)S(1)} %collective-permute-done.25.other_ref, f32[16,4224]{1,0:T(8,128)S(1)} %shard_map.156.local_ref, bf16[16,4096]{1,0:T(8,128)(2,1)S(1)} %copy-done.1), custom_call_target="tpu_custom_call" | custom-call | bytes 1310720 | tf_op jit(solution)/shard_map/pallas_call | solution.py:372
  (71 shorter events, 3.5 us)
Async XLA Ops:
  1.7 5.6 %collective-permute-start.7 = (bf16[16,6272]{1,0:T(8,128)(2,1)S(1)}, bf16[16,6272]{1,0:T(8,128)(2,1)S(1)}, u32[]{:S(2)}, u32[]{:S(2)}) collective-permute-start(bf16[16,6272]{1,0:T(8,128)(2,1)S(1)} %shard_map.148.refs_0_), channel_id=1, source_target_pairs={{0,4},{1,3},{2,0},{3,7},{4,8},{5,1},{6,2},{7,11},{8,12},{9,5},{10,... | collective-permute-start | bytes 602120 | tf_op jit(solution)/shard_map/ppermute | solution.py:410
  4.8 5.8 %collective-permute-start = (bf16[16,6272]{1,0:T(8,128)(2,1)S(1)}, bf16[16,6272]{1,0:T(8,128)(2,1)S(1)}, u32[]{:S(2)}, u32[]{:S(2)}) collective-permute-start(bf16[16,6272]{1,0:T(8,128)(2,1)S(1)} %shard_map.147.after.refs_4_), channel_id=1, source_target_pairs={{0,4},{1,3},{2,0},{3,7},{4,8},{5,1},{6,2},{7,11},{8,12},{9,5},{10,... | collective-permute-start | bytes 602120 | tf_op jit(solution)/shard_map/ppermute | solution.py:410
  7.3 4.9 %collective-permute-start.8 = (bf16[16,6272]{1,0:T(8,128)(2,1)S(1)}, bf16[16,6272]{1,0:T(8,128)(2,1)S(1)}, u32[]{:S(2)}, u32[]{:S(2)}) collective-permute-start(bf16[16,6272]{1,0:T(8,128)(2,1)S(1)} %collective-permute-done.7.after.refs_1_), channel_id=1, source_target_pairs={{0,4},{1,3},{2,0},{3,7},{4,8},{5,1},{6,2},{7,11},{8,12},{9,5},{10,... | collective-permute-start | bytes 602120 | tf_op jit(solution)/shard_map/ppermute | solution.py:410
  8.8 13.3 %collective-permute-start.10 = (bf16[16,6272]{1,0:T(8,128)(2,1)S(1)}, bf16[16,6272]{1,0:T(8,128)(2,1)S(1)}, u32[]{:S(2)}, u32[]{:S(2)}) collective-permute-start(bf16[16,6272]{1,0:T(8,128)(2,1)S(1)} %collective-permute-done.7.after.refs_1_), channel_id=1, source_target_pairs={{0,1},{1,0},{2,3},{3,2},{4,5},{5,4},{6,7},{7,6},{8,9},{9,8},{10,11... | collective-permute-start | bytes 602120 | tf_op jit(solution)/shard_map/ppermute | solution.py:413
  10.7 5.6 %collective-permute-start.1 = (bf16[16,6272]{1,0:T(8,128)(2,1)S(1)}, bf16[16,6272]{1,0:T(8,128)(2,1)S(1)}, u32[]{:S(2)}, u32[]{:S(2)}) collective-permute-start(bf16[16,6272]{1,0:T(8,128)(2,1)S(1)} %collective-permute-done.refs_5_), channel_id=1, source_target_pairs={{0,4},{1,3},{2,0},{3,7},{4,8},{5,1},{6,2},{7,11},{8,12},{9,5},{10,... | collective-permute-start | bytes 602120 | tf_op jit(solution)/shard_map/ppermute | solution.py:410
  12.2 5.5 %collective-permute-start.9 = (bf16[16,6272]{1,0:T(8,128)(2,1)S(1)}, bf16[16,6272]{1,0:T(8,128)(2,1)S(1)}, u32[]{:S(2)}, u32[]{:S(2)}) collective-permute-start(bf16[16,6272]{1,0:T(8,128)(2,1)S(1)} %collective-permute-done.8.after.refs_2_), channel_id=1, source_target_pairs={{0,4},{1,3},{2,0},{3,7},{4,8},{5,1},{6,2},{7,11},{8,12},{9,5},{10,... | collective-permute-start | bytes 602120 | tf_op jit(solution)/shard_map/ppermute | solution.py:410
  13.6 12.1 %slice-start.4 = ((s8[8388608]{0:T(1024)(128)(4,1)}), s8[4194304]{0:T(1024)(128)(4,1)S(1)}, s32[]{:S(2)}) async-start(s8[8388608]{0:T(1024)(128)(4,1)} %bitcast.8), calls=%async_computation.4 | async-start | bytes 8388608
  13.6 12.1 %slice-start.5 = ((s8[8388608]{0:T(1024)(128)(4,1)}), s8[4194304]{0:T(1024)(128)(4,1)S(1)}, s32[]{:S(2)}) async-start(s8[8388608]{0:T(1024)(128)(4,1)} %bitcast.8), calls=%async_computation.5 | async-start | bytes 8388608
  13.6 8.6 %collective-permute-start.11 = (bf16[16,6272]{1,0:T(8,128)(2,1)S(1)}, bf16[16,6272]{1,0:T(8,128)(2,1)S(1)}, u32[]{:S(2)}, u32[]{:S(2)}) collective-permute-start(bf16[16,6272]{1,0:T(8,128)(2,1)S(1)} %collective-permute-done.8.after.refs_2_), channel_id=1, source_target_pairs={{0,1},{1,0},{2,3},{3,2},{4,5},{5,4},{6,7},{7,6},{8,9},{9,8},{10,11... | collective-permute-start | bytes 602120 | tf_op jit(solution)/shard_map/ppermute | solution.py:413
  16.3 6.4 %collective-permute-start.2 = (bf16[16,6272]{1,0:T(8,128)(2,1)S(1)}, bf16[16,6272]{1,0:T(8,128)(2,1)S(1)}, u32[]{:S(2)}, u32[]{:S(2)}) collective-permute-start(bf16[16,6272]{1,0:T(8,128)(2,1)S(1)} %collective-permute-done.1.refs_6_), channel_id=1, source_target_pairs={{0,4},{1,3},{2,0},{3,7},{4,8},{5,1},{6,2},{7,11},{8,12},{9,5},{10,... | collective-permute-start | bytes 602120 | tf_op jit(solution)/shard_map/ppermute | solution.py:410
  17.7 5.6 %collective-permute-start.13 = (bf16[16,6272]{1,0:T(8,128)(2,1)S(1)}, bf16[16,6272]{1,0:T(8,128)(2,1)S(1)}, u32[]{:S(2)}, u32[]{:S(2)}) collective-permute-start(bf16[16,6272]{1,0:T(8,128)(2,1)S(1)} %collective-permute-done.9.refs_3_), channel_id=1, source_target_pairs={{0,4},{1,3},{2,0},{3,7},{4,8},{5,1},{6,2},{7,11},{8,12},{9,5},{10,... | collective-permute-start | bytes 602120 | tf_op jit(solution)/shard_map/ppermute | solution.py:410
  18.1 7.5 %collective-permute-start.12 = (bf16[16,6272]{1,0:T(8,128)(2,1)S(1)}, bf16[16,6272]{1,0:T(8,128)(2,1)S(1)}, u32[]{:S(2)}, u32[]{:S(2)}) collective-permute-start(bf16[16,6272]{1,0:T(8,128)(2,1)S(1)} %collective-permute-done.9.refs_3_), channel_id=1, source_target_pairs={{0,1},{1,0},{2,3},{3,2},{4,5},{5,4},{6,7},{7,6},{8,9},{9,8},{10,11... | collective-permute-start | bytes 602120 | tf_op jit(solution)/shard_map/ppermute | solution.py:413
  22.0 6.6 %slice-start.1 = ((s8[8388608]{0:T(1024)(128)(4,1)}), s8[4194304]{0:T(1024)(128)(4,1)S(1)}, s32[]{:S(2)}) async-start(s8[8388608]{0:T(1024)(128)(4,1)} %bitcast.3), calls=%async_computation.1 | async-start | bytes 8388608
  22.0 6.6 %slice-start.3 = ((s8[8388608]{0:T(1024)(128)(4,1)}), s8[4194304]{0:T(1024)(128)(4,1)S(1)}, s32[]{:S(2)}) async-start(s8[8388608]{0:T(1024)(128)(4,1)} %bitcast.5), calls=%async_computation.3 | async-start | bytes 8388608
  22.0 6.6 %copy-start.2 = (f32[4096]{0:T(1024)S(1)}, f32[4096]{0:T(1024)}, u32[]{:S(2)}) copy-start(f32[4096]{0:T(1024)} %param.14) | copy-start | bytes 49156
  22.1 6.5 %collective-permute-start.3 = (bf16[16,6272]{1,0:T(8,128)(2,1)S(1)}, bf16[16,6272]{1,0:T(8,128)(2,1)S(1)}, u32[]{:S(2)}, u32[]{:S(2)}) collective-permute-start(bf16[16,6272]{1,0:T(8,128)(2,1)S(1)} %collective-permute-done.refs_5_), channel_id=1, source_target_pairs={{0,1},{1,0},{2,3},{3,2},{4,5},{5,4},{6,7},{7,6},{8,9},{9,8},{10,11... | collective-permute-start | bytes 602120 | tf_op jit(solution)/shard_map/ppermute | solution.py:413
  22.2 6.4 %collective-permute-start.4 = (bf16[16,6272]{1,0:T(8,128)(2,1)S(1)}, bf16[16,6272]{1,0:T(8,128)(2,1)S(1)}, u32[]{:S(2)}, u32[]{:S(2)}) collective-permute-start(bf16[16,6272]{1,0:T(8,128)(2,1)S(1)} %collective-permute-done.1.refs_6_), channel_id=1, source_target_pairs={{0,1},{1,0},{2,3},{3,2},{4,5},{5,4},{6,7},{7,6},{8,9},{9,8},{10,11... | collective-permute-start | bytes 602120 | tf_op jit(solution)/shard_map/ppermute | solution.py:413
  22.7 5.9 %collective-permute-start.6 = (bf16[16,6272]{1,0:T(8,128)(2,1)S(1)}, bf16[16,6272]{1,0:T(8,128)(2,1)S(1)}, u32[]{:S(2)}, u32[]{:S(2)}) collective-permute-start(bf16[16,6272]{1,0:T(8,128)(2,1)S(1)} %collective-permute-done.2.refs_7_), channel_id=1, source_target_pairs={{0,4},{1,3},{2,0},{3,7},{4,8},{5,1},{6,2},{7,11},{8,12},{9,5},{10,... | collective-permute-start | bytes 602120 | tf_op jit(solution)/shard_map/ppermute | solution.py:410
  23.3 5.3 %collective-permute-start.5 = (bf16[16,6272]{1,0:T(8,128)(2,1)S(1)}, bf16[16,6272]{1,0:T(8,128)(2,1)S(1)}, u32[]{:S(2)}, u32[]{:S(2)}) collective-permute-start(bf16[16,6272]{1,0:T(8,128)(2,1)S(1)} %collective-permute-done.2.refs_7_), channel_id=1, source_target_pairs={{0,1},{1,0},{2,3},{3,2},{4,5},{5,4},{6,7},{7,6},{8,9},{9,8},{10,11... | collective-permute-start | bytes 602120 | tf_op jit(solution)/shard_map/ppermute | solution.py:413
  41.5 25.4 %copy-start = (bf16[16,4096]{1,0:T(8,128)(2,1)S(1)}, bf16[16,4096]{1,0:T(8,128)(2,1)}, u32[]{:S(2)}) copy-start(bf16[16,4096]{1,0:T(8,128)(2,1)} %upstream_ref.1) | copy-start | bytes 393220
  41.6 8.2 %collective-permute-start.15 = (bf16[48,4096]{1,0:T(8,128)(2,1)S(1)}, bf16[48,4096]{1,0:T(8,128)(2,1)S(1)}, u32[]{:S(2)}, u32[]{:S(2)}) collective-permute-start(bf16[48,4096]{1,0:T(8,128)(2,1)S(1)} %slice.50), channel_id=1, source_target_pairs={{0,1},{1,0},{2,3},{3,2},{4,5},{5,4},{6,7},{7,6},{8,9},{9,8},{10,11... | collective-permute-start | bytes 1179656 | tf_op jit(solution)/shard_map/ppermute | solution.py:413
  41.8 8.0 %collective-permute-start.14 = (bf16[16,4096]{1,0:T(8,128)(2,1)S(1)}, bf16[16,4096]{1,0:T(8,128)(2,1)S(1)}, u32[]{:S(2)}, u32[]{:S(2)}) collective-permute-start(bf16[16,4096]{1,0:T(8,128)(2,1)S(1)} %slice.48), channel_id=1, source_target_pairs={{0,4},{1,3},{2,0},{3,7},{4,8},{5,1},{6,2},{7,11},{8,12},{9,5},{10,... | collective-permute-start | bytes 393224 | tf_op jit(solution)/shard_map/ppermute | solution.py:410
  45.0 5.0 %collective-permute-start.20 = (bf16[16,4224]{1,0:T(8,128)(2,1)S(1)}, bf16[16,4224]{1,0:T(8,128)(2,1)S(1)}, u32[]{:S(2)}, u32[]{:S(2)}) collective-permute-start(bf16[16,4224]{1,0:T(8,128)(2,1)S(1)} %slice.56), channel_id=1, source_target_pairs={{0,4},{1,3},{2,0},{3,7},{4,8},{5,1},{6,2},{7,11},{8,12},{9,5},{10,... | collective-permute-start | bytes 405512 | tf_op jit(solution)/shard_map/ppermute | solution.py:410
  46.4 3.7 %collective-permute-start.21 = (bf16[48,4224]{1,0:T(8,128)(2,1)S(1)}, bf16[48,4224]{1,0:T(8,128)(2,1)S(1)}, u32[]{:S(2)}, u32[]{:S(2)}) collective-permute-start(bf16[48,4224]{1,0:T(8,128)(2,1)S(1)} %slice.58), channel_id=1, source_target_pairs={{0,1},{1,0},{2,3},{3,2},{4,5},{5,4},{6,7},{7,6},{8,9},{9,8},{10,11... | collective-permute-start | bytes 1216520 | tf_op jit(solution)/shard_map/ppermute | solution.py:413
  49.8 4.2 %collective-permute-start.16 = (bf16[16,4096]{1,0:T(8,128)(2,1)S(1)}, bf16[16,4096]{1,0:T(8,128)(2,1)S(1)}, u32[]{:S(2)}, u32[]{:S(2)}) collective-permute-start(bf16[16,4096]{1,0:T(8,128)(2,1)S(1)} %add_convert_fusion.5), channel_id=1, source_target_pairs={{0,4},{1,3},{2,0},{3,7},{4,8},{5,1},{6,2},{7,11},{8,12},{9,5},{10,... | collective-permute-start | bytes 393224 | tf_op jit(solution)/shard_map/ppermute | solution.py:410
  50.1 5.3 %collective-permute-start.22 = (bf16[16,4224]{1,0:T(8,128)(2,1)S(1)}, bf16[16,4224]{1,0:T(8,128)(2,1)S(1)}, u32[]{:S(2)}, u32[]{:S(2)}) collective-permute-start(bf16[16,4224]{1,0:T(8,128)(2,1)S(1)} %add_convert_fusion.2), channel_id=1, source_target_pairs={{0,4},{1,3},{2,0},{3,7},{4,8},{5,1},{6,2},{7,11},{8,12},{9,5},{10,... | collective-permute-start | bytes 405512 | tf_op jit(solution)/shard_map/ppermute | solution.py:410
  54.0 4.2 %collective-permute-start.17 = (bf16[16,4096]{1,0:T(8,128)(2,1)S(1)}, bf16[16,4096]{1,0:T(8,128)(2,1)S(1)}, u32[]{:S(2)}, u32[]{:S(2)}) collective-permute-start(bf16[16,4096]{1,0:T(8,128)(2,1)S(1)} %add_convert_fusion.4), channel_id=1, source_target_pairs={{0,4},{1,3},{2,0},{3,7},{4,8},{5,1},{6,2},{7,11},{8,12},{9,5},{10,... | collective-permute-start | bytes 393224 | tf_op jit(solution)/shard_map/ppermute | solution.py:410
  55.5 4.0 %collective-permute-start.23 = (bf16[16,4224]{1,0:T(8,128)(2,1)S(1)}, bf16[16,4224]{1,0:T(8,128)(2,1)S(1)}, u32[]{:S(2)}, u32[]{:S(2)}) collective-permute-start(bf16[16,4224]{1,0:T(8,128)(2,1)S(1)} %add_convert_fusion.1), channel_id=1, source_target_pairs={{0,4},{1,3},{2,0},{3,7},{4,8},{5,1},{6,2},{7,11},{8,12},{9,5},{10,... | collective-permute-start | bytes 405512 | tf_op jit(solution)/shard_map/ppermute | solution.py:410
  58.2 3.9 %collective-permute-start.18 = (bf16[16,4096]{1,0:T(8,128)(2,1)S(1)}, bf16[16,4096]{1,0:T(8,128)(2,1)S(1)}, u32[]{:S(2)}, u32[]{:S(2)}) collective-permute-start(bf16[16,4096]{1,0:T(8,128)(2,1)S(1)} %add_convert_fusion.3), channel_id=1, source_target_pairs={{0,4},{1,3},{2,0},{3,7},{4,8},{5,1},{6,2},{7,11},{8,12},{9,5},{10,... | collective-permute-start | bytes 393224 | tf_op jit(solution)/shard_map/ppermute | solution.py:410
  59.6 5.5 %collective-permute-start.24 = (bf16[16,4224]{1,0:T(8,128)(2,1)S(1)}, bf16[16,4224]{1,0:T(8,128)(2,1)S(1)}, u32[]{:S(2)}, u32[]{:S(2)}) collective-permute-start(bf16[16,4224]{1,0:T(8,128)(2,1)S(1)} %add_convert_fusion), channel_id=1, source_target_pairs={{0,4},{1,3},{2,0},{3,7},{4,8},{5,1},{6,2},{7,11},{8,12},{9,5},{10,... | collective-permute-start | bytes 405512 | tf_op jit(solution)/shard_map/ppermute | solution.py:410
  62.1 4.8 %collective-permute-start.19 = (f32[16,4096]{1,0:T(8,128)S(1)}, f32[16,4096]{1,0:T(8,128)S(1)}, u32[]{:S(2)}, u32[]{:S(2)}) collective-permute-start(f32[16,4096]{1,0:T(8,128)S(1)} %convert_add_fusion.1.mine_ref), channel_id=1, source_target_pairs={{0,1},{1,0},{2,3},{3,2},{4,5},{5,4},{6,7},{7,6},{8,9},{9,8},{10,11... | collective-permute-start | bytes 786440 | tf_op jit(solution)/shard_map/ppermute | solution.py:413
  65.1 3.9 %collective-permute-start.25 = (f32[16,4224]{1,0:T(8,128)S(1)}, f32[16,4224]{1,0:T(8,128)S(1)}, u32[]{:S(2)}, u32[]{:S(2)}) collective-permute-start(f32[16,4224]{1,0:T(8,128)S(1)} %convert_add_fusion.mine_ref), channel_id=1, source_target_pairs={{0,1},{1,0},{2,3},{3,2},{4,5},{5,4},{6,7},{7,6},{8,9},{9,8},{10,11... | collective-permute-start | bytes 811016 | tf_op jit(solution)/shard_map/ppermute | solution.py:413
  (6 other events, 33.9 us)

commit v4 on v3

--- a/solution.py
+++ b/solution.py
@@ -142,6 +142,11 @@
     out_ref[...] = jnp.zeros_like(out_ref)
 
 
+def mask_kernel(n, where_ref, counts_ref, starts_ref, slots_ref, after, mask_ref):
+    del after
+    mask_ref[...] = tenant_mask(n, where_ref, counts_ref, starts_ref, slots_ref)
+
+
 def back_kernel(n, *refs):
     pieces, (down_ref, upstream_ref, tables_ref, back_ref) = refs[:n], refs[-4:]
     width = upstream_ref.shape[1]
@@ -152,9 +157,9 @@
 
 
 def hidden_kernel(n, step, *refs):
-    where_ref, counts_ref, starts_ref, slots_ref = refs[:4]
-    pieces = refs[4 : 4 + n]
+    pieces = refs[:n]
     (
+        mask_ref,
         gain_ref,
         back_ref,
         right_ref,
@@ -167,12 +172,13 @@
         tables_ref,
         middle_ref,
         coeffs_ref,
-        weights_ref,
+        pulled_ref,
         stats_ref,
         normed_ref,
+        gate_t_ref,
         gate_grad_ref,
         up_grad_ref,
-    ) = refs[4 + n :]
+    ) = refs[n:]
     row_total, width = middle_ref.shape
     chunks = width // step
     for k, piece in enumerate(pieces):
@@ -182,7 +188,7 @@
 
     columns = tables_ref.shape[0]
     products = dot_nt(rows_ref[...], tables_ref[...])
-    mask = tenant_mask(n, where_ref, counts_ref, starts_ref, slots_ref)
+    mask = mask_ref[...]
     coeffs = mask * (pltpu.roll(products, columns - RANK, 1) - products)
     coeffs_ref[...] = coeffs
     coeff_high, coeff_low = split(coeffs)
@@ -218,16 +224,17 @@
     for j in range(hidden // tile):
         cols = slice(j * tile, (j + 1) * tile)
         gate = dot_nn(normed_ref[...], gate_ref[:, cols])
+        gate_t_ref[cols, :] = gate_ref[:, cols].T
         upward = dot_nn(normed_ref[...], up_ref[:, cols])
         back = back_ref[:, cols]
         sigma = jax.nn.sigmoid(gate)
         gate_grad_ref[:, cols] = (back * upward * sigma * (1.0 + gate * (1.0 - sigma))).astype(BF)
         up_grad_ref[:, cols] = (back * gate * sigma).astype(BF)
 
-    def scaled_step(c, carry):
-        inner, scaled_tables = carry
-        cols = columns_at(c, step)
-        value = dot_nt(gate_grad_ref[...], gate_ref[cols, :])
+    inner, scaled_tables = column_zero, square_zero
+    for c in range(chunks):
+        cols = slice(c * step, (c + 1) * step)
+        value = dot_nn(gate_grad_ref[...], gate_t_ref[:, cols])
         value = value + dot_nt(up_grad_ref[...], up_ref[cols, :])
         value = value * gain_ref[:, cols]
         scaled_ref[:, cols] = value
@@ -236,16 +243,11 @@
         sent_ref[:, cols] = high[SEG:]
         scaled_tables = scaled_tables + dot_nt(high, tables_ref[:, cols])
         inner = inner + jnp.sum(value * middle_ref[:, cols].astype(F32), axis=1, keepdims=True)
-        return inner, scaled_tables
-
-    inner, scaled_tables = lax.fori_loop(0, chunks, scaled_step, (column_zero, square_zero))
+
     shrink = inverse * inverse * (inner / width)
     lane = lax.broadcasted_iota(jnp.int32, stats_ref.shape, 1)
     stats_ref[...] = jnp.where(lane == 0, inverse, shrink)
-    pulled = mask * (inverse * (scaled_tables - shrink * middle_tables))
-    pulled = pltpu.roll(pulled, RANK, 1) - pulled
-    weights_ref[:, :row_total] = coeffs.T.astype(BF)
-    weights_ref[:, row_total:] = pulled.T.astype(BF)
+    pulled_ref[...] = mask * (inverse * (scaled_tables - shrink * middle_tables))
 
 
 def slot_kernel(
@@ -253,45 +255,37 @@
     scaled_ref,
     rows_ref,
     middle_ref,
-    weights_ref,
+    coeffs_ref,
+    pulled_ref,
     stats_ref,
     own_ref,
     sent_ref,
+    weights_ref,
 ):
     row_total, width = middle_ref.shape
     inverse, shrink = stats_ref[:, 0:1], stats_ref[:, 1:2]
-
-    def slot_step(c, carry):
-        cols = columns_at(c, step)
+    pulled = pulled_ref[...]
+    pulled = pltpu.roll(pulled, RANK, 1) - pulled
+    weights_ref[:, :row_total] = coeffs_ref[...].T.astype(BF)
+    weights_ref[:, row_total:] = pulled.T.astype(BF)
+
+    for c in range(width // step):
+        cols = slice(c * step, (c + 1) * step)
         value = inverse * (scaled_ref[:, cols] - middle_ref[:, cols].astype(F32) * shrink)
         both = jnp.concatenate([value.astype(BF), rows_ref[:, cols]], axis=0)
         value = dot_nn(weights_ref[...], both)
         sent_ref[:, cols] = value[SEG:].astype(BF)
         own_ref[:, cols] = value[:SEG]
-        return carry
-
-    lax.fori_loop(0, width // step, slot_step, 0)
     value = dot_nn(weights_ref[:, row_total:], rows_ref[:, width:])
     sent_ref[:, width:] = value[SEG:].astype(BF)
     own_ref[:, width:] = value[:SEG]
 
 
-def local_kernel(
-    n,
-    step,
-    where_ref,
-    counts_ref,
-    starts_ref,
-    slots_ref,
-    rows_ref,
-    tables_ref,
-    upstream_ref,
-    coeffs_ref,
-    local_ref,
-):
+def local_kernel(step, mask_ref, rows_ref, tables_ref, upstream_ref, coeffs_ref, after, local_ref):
+    del after
     row_total, width = upstream_ref.shape
     columns = tables_ref.shape[0]
-    mask = tenant_mask(n, where_ref, counts_ref, starts_ref, slots_ref)
+    mask = mask_ref[...]
     lane = lax.broadcasted_iota(jnp.int32, (row_total, columns), 1)
     first = lane < RANK
     pulled = jnp.where(first, mask, 0.0) * dot_nt(upstream_ref[...], tables_ref[:, :width])
@@ -337,8 +331,10 @@
     stats_ref,
     tables_ref,
     out_ref,
+    token_ref,
 ):
     width = out_ref.shape[1]
+    token_ref[...] = jnp.zeros_like(token_ref)
     devices = piece_devices(n, where_ref)
     slot, limit = block_tenant(devices[0], counts_ref, starts_ref, slots_ref)
     which = 0
@@ -349,16 +345,14 @@
     inverse = stats_ref[:SEG, 0:1]
     scaled = mine_ref[...] + other_ref[...]
     inner = jnp.sum(scaled * middle, axis=1, keepdims=True) / width
-    total = upstream_ref[...].astype(F32) + inverse * (
+    total = upstream_ref[:SEG, :].astype(F32) + inverse * (
         scaled - middle * (inverse * inverse * inner)
     )
-    high, low = split(total)
-    pulled = dot_nt(high, table) + dot_nt(low, table)
+    pulled = dot_nt(total.astype(BF), table)
     row = lax.broadcasted_iota(jnp.int32, (SEG, RANK), 0)
     pulled = jnp.where(row < limit, pulled[:, :RANK], 0.0)
-    pulled = jnp.concatenate([-pulled, pulled], axis=1)
-    high, low = split(pulled)
-    out_ref[...] = (total + dot_nn(high, table) + dot_nn(low, table)).astype(BF)
+    pulled = jnp.concatenate([-pulled, pulled], axis=1).astype(BF)
+    out_ref[...] = (total + dot_nn(pulled, table)).astype(BF)
 
 
 LOAD_FLOPS = 4 * 10**9
@@ -424,11 +418,13 @@
     def reduce(own, sent):
         other = swap(sent[: half * SEG])
         state = hop(sent[2 * half * SEG :])
+        states = [state]
         for t in range(half - 1, -1, -1):
             mine = sent[(half + t) * SEG : (half + t + 1) * SEG].astype(F32)
             partner = other[t * SEG : (t + 1) * SEG].astype(F32)
             state = hop((state.astype(F32) + (mine + partner)).astype(BF))
-        return own + state.astype(F32)
+            states.append(state)
+        return own + state.astype(F32), states
 
     def on_device(
         hidden_in,
@@ -477,7 +473,16 @@
         )
         upstream_pieces = gather(packed_upstream)
         row_pieces = gather(packed_rows)
-        marks = tuple(mark(x) for x in (packed_rows, upstream_pieces[1], upstream_pieces[2]))
+        marks = tuple(mark(x) for x in (packed_rows, upstream_pieces[2]))
+        (mask,) = call(
+            functools.partial(mask_kernel, n),
+            [((rows_total, rows_total), F32)],
+            scalars,
+            (upstream_pieces[1],),
+            flops=LOAD_FLOPS,
+            loose=1,
+            limit=max(4, n // 2),
+        )
         upstream, right, back = call(
             functools.partial(back_kernel, n),
             [
@@ -491,7 +496,7 @@
             moved=2 * width * hidden,
             limit=n,
         )
-        own, sent, scaled, rows, tables, middle, coeffs, weights, stats = call(
+        own, sent, scaled, rows, tables, middle, coeffs, pulled, stats = call(
             functools.partial(hidden_kernel, n, 1024),
             [
                 ((SEG, width), F32),
@@ -501,12 +506,13 @@
                 ((rows_total, wide), BF),
                 ((rows_total, width), BF),
                 ((rows_total, rows_total), F32),
-                ((rows_total, 2 * rows_total), BF),
+                ((rows_total, rows_total), F32),
                 ((rows_total, 128), F32),
             ],
-            scalars,
+            (),
             (
                 *row_pieces,
+                mask,
                 norm_gain.reshape(1, width),
                 back,
                 right,
@@ -515,39 +521,42 @@
             ),
             scratch=[
                 pltpu.VMEM((rows_total, width), BF),
+                pltpu.VMEM((hidden, width), BF),
                 pltpu.VMEM((rows_total, hidden), BF),
                 pltpu.VMEM((rows_total, hidden), BF),
             ],
             flops=4 * work,
             moved=4 * width * hidden,
-            limit=n + n // 2,
+            limit=n + n // 2 + 8,
         )
         own_slot, sent_slot = call(
             functools.partial(slot_kernel, 1024),
             [((SEG, wide), F32), ((rows_total - SEG, wide), BF)],
             (),
-            (scaled, rows, middle, weights, stats),
+            (scaled, rows, middle, coeffs, pulled, stats),
+            scratch=[pltpu.VMEM((rows_total, 2 * rows_total), BF)],
             flops=work,
             moved=10 * rows_total * width,
             limit=n + n // 2,
         )
+        mine, states = reduce(own, sent)
+        other = swap(mine)
+        slots, _ = reduce(own_slot, sent_slot)
         (local,) = call(
-            functools.partial(local_kernel, n, 1024),
+            functools.partial(local_kernel, 1024),
             [((SEG, wide), F32)],
-            scalars,
-            (rows, tables, upstream, coeffs),
+            (),
+            (mask, rows, tables, upstream, coeffs, states[-1]),
             flops=work,
             moved=10 * rows_total * width,
             limit=n + n // 2,
-        )
-        mine = reduce(own, sent)
-        other = swap(mine)
-        slots = reduce(own_slot, sent_slot)
-        (grad_rows,) = call(
+            loose=1,
+        )
+        grad_rows, token = call(
             functools.partial(rows_kernel, n),
-            [((SEG, width), BF)],
+            [((SEG, width), BF), ((8, 128), F32)],
             scalars,
-            (mine, other, grad_out, middle, stats, tables),
+            (mine, other, upstream, middle, stats, tables),
             flops=LONG_FLOPS,
             moved=14 * SEG * width,
         )
@@ -555,7 +564,7 @@
             ends_kernel,
             [((1, RANK, width), F32), ((1, RANK, width), F32), ((1, RANK), F32)],
             (),
-            (slots, swap(slots), local, grad_rows),
+            (slots, swap(slots), local, token),
             moved=20 * SEG * width,
             loose=1,
         )

time: 70.8 us -> 65 us (0.918)
  waiting for transfers between devices: 13.8 us -> 9.39 us
  Pallas kernels: 24.3 us -> 20.1 us
  starting transfers between devices: 30.1 us -> 33.8 us
  local copies, waits for them, and re-layouts: 1.04 us -> 0.13 us
    ppermute x16, starting transfers between devices: 12.7 us -> 17.5 us  [hop(): return lax.ppermute(x, ('dp', 'tensor'), pairs)]
    ppermute x16, waiting for transfers between devices: 13.7 us -> 9.37 us  [hop(): return lax.ppermute(x, ('dp', 'tensor'), pairs)]
    pallas_call x11, Pallas kernels: 24.3 us -> 20.1 us  [call(): pl.pallas_call(kernel, out_shape=tuple((jax.ShapeDtypeStruct(s, d) for s,...]
    ppermute x10, starting transfers between devices: 17.4 us -> 16.2 us  [swap(): return lax.ppermute(x, 'tensor', [(0, 1), (1, 0)])]
    unnamed x24 -> x20, local copies, waits for them, and re-layouts: 0.96 us -> 0.05 us
  transfers between devices with their start and end apart: 26 -> 26, of which waited for: 9 -> 10; matrix products, arithmetic and copies ran while one was open for 1% -> 1% of each run, Pallas kernels for 14% -> 14%
where the time goes in v4:
time: 65 us; the launch traced here: 64.8 us
  starting transfers between devices  33.8 us (52%)
  Pallas kernels  20.1 us (31%)
  waiting for transfers between devices  9.39 us (14%)
  between operations  0.94 us (1%)
    pallas_call x11, Pallas kernels, call(): pl.pallas_call(kernel, out_shape=tuple((jax.ShapeDtypeStruct(s, d) for s,...  20.1 us
    ppermute x16, starting transfers between devices, hop(): return lax.ppermute(x, ('dp', 'tensor'), pairs)  17.5 us
    ppermute x10, starting transfers between devices, swap(): return lax.ppermute(x, 'tensor', [(0, 1), (1, 0)])  16.2 us
    ppermute x16, waiting for transfers between devices, hop(): return lax.ppermute(x, ('dp', 'tensor'), pairs)  9.37 us
  transfers between devices with their start and end apart: 26, of which 10 were waited for; matrix products, arithmetic and copies ran while one was open for 1% of the time, Pallas kernels for 14%

profile of v4, /device:TPU:1, one launch (start us, length us, event | category | flops | bytes accessed | tf_op | source)
XLA Modules:
  0.0 64.8 jit_solution(1584225143982589286)
XLA Ops:
  0.7 1.1 %shard_map.148.refs_0_ = bf16[16,6272]{1,0:T(8,128)(2,1)S(1)} custom-call(bf16[16,4096]{1,0:T(8,128)(2,1)} %upstream_hbm.1, bf16[1,8,4096]{2,1,0:T(8,128)(2,1)} %basis_hbm.3, bf16[1,8,4096]{2,1,0:T(8,128)(2,1)} %learned_hbm.3, bf16[1,8]{1,0:T(2,128)(2,1)} %bias_hbm.1), custom_call_target="tpu_custom_call" | custom-call | bytes 540672 | tf_op jit(solution)/shard_map/pallas_call | solution.py:366
  1.8 2.1 %collective-permute-start.7 = (bf16[16,6272]{1,0:T(8,128)(2,1)S(1)}, bf16[16,6272]{1,0:T(8,128)(2,1)S(1)}, u32[]{:S(2)}, u32[]{:S(2)}) collective-permute-start(bf16[16,6272]{1,0:T(8,128)(2,1)S(1)} %shard_map.148.refs_0_), channel_id=1, source_target_pairs={{0,4},{1,3},{2,0},{3,7},{4,8},{5,1},{6,2},{7,11},{8,12},{9,5},{10,... | collective-permute-start | bytes 602120 | tf_op jit(solution)/shard_map/ppermute | solution.py:404
  3.9 1.0 %shard_map.147.after.refs_0_ = bf16[16,6272]{1,0:T(8,128)(2,1)S(1)} custom-call(bf16[16,4096]{1,0:T(8,128)(2,1)} %hidden_hbm.1, bf16[1,8,4096]{2,1,0:T(8,128)(2,1)} %basis_hbm.3, bf16[1,8,4096]{2,1,0:T(8,128)(2,1)} %learned_hbm.3), custom_call_target="tpu_custom_call" | custom-call | bytes 540672 | tf_op jit(solution)/shard_map/pallas_call | solution.py:366
  4.9 1.3 %collective-permute-start = (bf16[16,6272]{1,0:T(8,128)(2,1)S(1)}, bf16[16,6272]{1,0:T(8,128)(2,1)S(1)}, u32[]{:S(2)}, u32[]{:S(2)}) collective-permute-start(bf16[16,6272]{1,0:T(8,128)(2,1)S(1)} %shard_map.147.after.refs_0_), channel_id=1, source_target_pairs={{0,4},{1,3},{2,0},{3,7},{4,8},{5,1},{6,2},{7,11},{8,12},{9,5},{10,... | collective-permute-start | bytes 602120 | tf_op jit(solution)/shard_map/ppermute | solution.py:404
  6.2 1.1 %collective-permute-done.7.after.refs_1_ = bf16[16,6272]{1,0:T(8,128)(2,1)S(1)} collective-permute-done((bf16[16,6272]{1,0:T(8,128)(2,1)S(1)}, bf16[16,6272]{1,0:T(8,128)(2,1)S(1)}, u32[]{:S(2)}, u32[]{:S(2)}) %collective-permute-start.7) | collective-permute-done | bytes 200736 | tf_op jit(solution)/shard_map/ppermute | solution.py:404
  7.4 1.4 %collective-permute-start.8 = (bf16[16,6272]{1,0:T(8,128)(2,1)S(1)}, bf16[16,6272]{1,0:T(8,128)(2,1)S(1)}, u32[]{:S(2)}, u32[]{:S(2)}) collective-permute-start(bf16[16,6272]{1,0:T(8,128)(2,1)S(1)} %collective-permute-done.7.after.refs_1_), channel_id=1, source_target_pairs={{0,4},{1,3},{2,0},{3,7},{4,8},{5,1},{6,2},{7,11},{8,12},{9,5},{10,... | collective-permute-start | bytes 602120 | tf_op jit(solution)/shard_map/ppermute | solution.py:404
  8.8 1.9 %collective-permute-start.10 = (bf16[16,6272]{1,0:T(8,128)(2,1)S(1)}, bf16[16,6272]{1,0:T(8,128)(2,1)S(1)}, u32[]{:S(2)}, u32[]{:S(2)}) collective-permute-start(bf16[16,6272]{1,0:T(8,128)(2,1)S(1)} %collective-permute-done.7.after.refs_1_), channel_id=1, source_target_pairs={{0,1},{1,0},{2,3},{3,2},{4,5},{5,4},{6,7},{7,6},{8,9},{9,8},{10,11... | collective-permute-start | bytes 602120 | tf_op jit(solution)/shard_map/ppermute | solution.py:407
  11.1 1.1 %collective-permute-done.8.after.refs_2_ = bf16[16,6272]{1,0:T(8,128)(2,1)S(1)} collective-permute-done((bf16[16,6272]{1,0:T(8,128)(2,1)S(1)}, bf16[16,6272]{1,0:T(8,128)(2,1)S(1)}, u32[]{:S(2)}, u32[]{:S(2)}) %collective-permute-start.8) | collective-permute-done | bytes 200736 | tf_op jit(solution)/shard_map/ppermute | solution.py:404
  12.2 1.4 %collective-permute-start.9 = (bf16[16,6272]{1,0:T(8,128)(2,1)S(1)}, bf16[16,6272]{1,0:T(8,128)(2,1)S(1)}, u32[]{:S(2)}, u32[]{:S(2)}) collective-permute-start(bf16[16,6272]{1,0:T(8,128)(2,1)S(1)} %collective-permute-done.8.after.refs_2_), channel_id=1, source_target_pairs={{0,4},{1,3},{2,0},{3,7},{4,8},{5,1},{6,2},{7,11},{8,12},{9,5},{10,... | collective-permute-start | bytes 602120 | tf_op jit(solution)/shard_map/ppermute | solution.py:404
  13.6 0.7 %shard_map.149.refs_8_.mask_ref = f32[128,128]{1,0:T(8,128)S(1)} custom-call(s32[2]{0:T(128)S(1)} %pad_add_fusion.where_ref, s32[8]{0:T(128)S(1)} %copy-done.1, s32[8]{0:T(128)S(1)} %copy-done.2, s32[8]{0:T(128)S(1)} %copy-done.3, bf16[16,6272]{1,0:T(8,128)(2,1)S(1)} %collective-permute-done.7.after.refs_1_), custom_call_target="tpu_custom_call" | custom-call | flops 4000000000 | tf_op jit(solution)/shard_map/pallas_call | solution.py:366
  14.4 2.8 %collective-permute-start.11 = (bf16[16,6272]{1,0:T(8,128)(2,1)S(1)}, bf16[16,6272]{1,0:T(8,128)(2,1)S(1)}, u32[]{:S(2)}, u32[]{:S(2)}) collective-permute-start(bf16[16,6272]{1,0:T(8,128)(2,1)S(1)} %collective-permute-done.8.after.refs_2_), channel_id=1, source_target_pairs={{0,1},{1,0},{2,3},{3,2},{4,5},{5,4},{6,7},{7,6},{8,9},{9,8},{10,11... | collective-permute-start | bytes 602120 | tf_op jit(solution)/shard_map/ppermute | solution.py:407
  17.7 0.9 %collective-permute-start.13 = (bf16[16,6272]{1,0:T(8,128)(2,1)S(1)}, bf16[16,6272]{1,0:T(8,128)(2,1)S(1)}, u32[]{:S(2)}, u32[]{:S(2)}) collective-permute-start(bf16[16,6272]{1,0:T(8,128)(2,1)S(1)} %collective-permute-done.9.refs_3_), channel_id=1, source_target_pairs={{0,4},{1,3},{2,0},{3,7},{4,8},{5,1},{6,2},{7,11},{8,12},{9,5},{10,... | collective-permute-start | bytes 602120 | tf_op jit(solution)/shard_map/ppermute | solution.py:404
  18.6 3.4 %collective-permute-start.12 = (bf16[16,6272]{1,0:T(8,128)(2,1)S(1)}, bf16[16,6272]{1,0:T(8,128)(2,1)S(1)}, u32[]{:S(2)}, u32[]{:S(2)}) collective-permute-start(bf16[16,6272]{1,0:T(8,128)(2,1)S(1)} %collective-permute-done.9.refs_3_), channel_id=1, source_target_pairs={{0,1},{1,0},{2,3},{3,2},{4,5},{5,4},{6,7},{7,6},{8,9},{9,8},{10,11... | collective-permute-start | bytes 602120 | tf_op jit(solution)/shard_map/ppermute | solution.py:407
  22.7 1.5 %collective-permute-done.13.refs_7_ = bf16[16,6272]{1,0:T(8,128)(2,1)S(1)} collective-permute-done((bf16[16,6272]{1,0:T(8,128)(2,1)S(1)}, bf16[16,6272]{1,0:T(8,128)(2,1)S(1)}, u32[]{:S(2)}, u32[]{:S(2)}) %collective-permute-start.13) | collective-permute-done | bytes 200736 | tf_op jit(solution)/shard_map/ppermute | solution.py:404
  24.2 1.5 %collective-permute-start.5 = (bf16[16,6272]{1,0:T(8,128)(2,1)S(1)}, bf16[16,6272]{1,0:T(8,128)(2,1)S(1)}, u32[]{:S(2)}, u32[]{:S(2)}) collective-permute-start(bf16[16,6272]{1,0:T(8,128)(2,1)S(1)} %collective-permute-done.2.refs_3_), channel_id=1, source_target_pairs={{0,1},{1,0},{2,3},{3,2},{4,5},{5,4},{6,7},{7,6},{8,9},{9,8},{10,11... | collective-permute-start | bytes 602120 | tf_op jit(solution)/shard_map/ppermute | solution.py:407
  25.7 2.9 %shard_map.152 = (bf16[128,4096]{1,0:T(8,128)(2,1)S(1)}, bf16[128,2176]{1,0:T(8,128)(2,1)S(1)}, f32[128,1024]{1,0:T(8,128)S(1)}) custom-call(bf16[16,6272]{1,0:T(8,128)(2,1)S(1)} %shard_map.148.refs_0_, bf16[16,6272]{1,0:T(8,128)(2,1)S(1)} %collective-permute-done.7.after.refs_1_, bf16[16,6272]{1,0:T(8,128)(2,1)S(1)} %collective-permute-done.8.after.refs_2_, ...), custom_call_target="tpu_custom_call" | custom-call | flops 40000000000 | bytes 8388608 | tf_op jit(solution)/shard_map/pallas_call | solution.py:366
  28.7 9.4 %shard_map.153 = (f32[16,4096]{1,0:T(8,128)S(1)}, bf16[112,4096]{1,0:T(8,128)(2,1)S(1)}, f32[128,4096]{1,0:T(8,128)S(1)}, bf16[128,4224]{1,0:T(8,128)(2,1)S(1)},...) custom-call(bf16[16,6272]{1,0:T(8,128)(2,1)S(1)} %shard_map.147.afte, ...), custom_call_target="tpu_custom_call" | custom-call | flops 4294967296 | bytes 16777216 | tf_op jit(solution)/shard_map/pallas_call | solution.py:366
  38.4 1.7 %collective-permute-start.14 = (bf16[16,4096]{1,0:T(8,128)(2,1)S(1)}, bf16[16,4096]{1,0:T(8,128)(2,1)S(1)}, u32[]{:S(2)}, u32[]{:S(2)}) collective-permute-start(bf16[16,4096]{1,0:T(8,128)(2,1)S(1)} %slice.48), channel_id=1, source_target_pairs={{0,4},{1,3},{2,0},{3,7},{4,8},{5,1},{6,2},{7,11},{8,12},{9,5},{10,... | collective-permute-start | bytes 393224 | tf_op jit(solution)/shard_map/ppermute | solution.py:404
  40.8 1.3 %collective-permute-start.20 = (bf16[16,4224]{1,0:T(8,128)(2,1)S(1)}, bf16[16,4224]{1,0:T(8,128)(2,1)S(1)}, u32[]{:S(2)}, u32[]{:S(2)}) collective-permute-start(bf16[16,4224]{1,0:T(8,128)(2,1)S(1)} %slice.56), channel_id=1, source_target_pairs={{0,4},{1,3},{2,0},{3,7},{4,8},{5,1},{6,2},{7,11},{8,12},{9,5},{10,... | collective-permute-start | bytes 405512 | tf_op jit(solution)/shard_map/ppermute | solution.py:404
  42.2 1.1 %collective-permute-start.21 = (bf16[48,4224]{1,0:T(8,128)(2,1)S(1)}, bf16[48,4224]{1,0:T(8,128)(2,1)S(1)}, u32[]{:S(2)}, u32[]{:S(2)}) collective-permute-start(bf16[48,4224]{1,0:T(8,128)(2,1)S(1)} %slice.58), channel_id=1, source_target_pairs={{0,1},{1,0},{2,3},{3,2},{4,5},{5,4},{6,7},{7,6},{8,9},{9,8},{10,11... | collective-permute-start | bytes 1216520 | tf_op jit(solution)/shard_map/ppermute | solution.py:407
  43.3 1.0 %collective-permute-start.16 = (bf16[16,4096]{1,0:T(8,128)(2,1)S(1)}, bf16[16,4096]{1,0:T(8,128)(2,1)S(1)}, u32[]{:S(2)}, u32[]{:S(2)}) collective-permute-start(bf16[16,4096]{1,0:T(8,128)(2,1)S(1)} %add_convert_fusion.5), channel_id=1, source_target_pairs={{0,4},{1,3},{2,0},{3,7},{4,8},{5,1},{6,2},{7,11},{8,12},{9,5},{10,... | collective-permute-start | bytes 393224 | tf_op jit(solution)/shard_map/ppermute | solution.py:404
  45.1 1.3 %collective-permute-start.22 = (bf16[16,4224]{1,0:T(8,128)(2,1)S(1)}, bf16[16,4224]{1,0:T(8,128)(2,1)S(1)}, u32[]{:S(2)}, u32[]{:S(2)}) collective-permute-start(bf16[16,4224]{1,0:T(8,128)(2,1)S(1)} %add_convert_fusion.2), channel_id=1, source_target_pairs={{0,4},{1,3},{2,0},{3,7},{4,8},{5,1},{6,2},{7,11},{8,12},{9,5},{10,... | collective-permute-start | bytes 405512 | tf_op jit(solution)/shard_map/ppermute | solution.py:404
  46.4 1.0 %collective-permute-done.16 = bf16[16,4096]{1,0:T(8,128)(2,1)S(1)} collective-permute-done((bf16[16,4096]{1,0:T(8,128)(2,1)S(1)}, bf16[16,4096]{1,0:T(8,128)(2,1)S(1)}, u32[]{:S(2)}, u32[]{:S(2)}) %collective-permute-start.16) | collective-permute-done | bytes 131104 | tf_op jit(solution)/shard_map/ppermute | solution.py:404
  48.2 0.8 %collective-permute-done.22 = bf16[16,4224]{1,0:T(8,128)(2,1)S(1)} collective-permute-done((bf16[16,4224]{1,0:T(8,128)(2,1)S(1)}, bf16[16,4224]{1,0:T(8,128)(2,1)S(1)}, u32[]{:S(2)}, u32[]{:S(2)}) %collective-permute-start.22) | collective-permute-done | bytes 135200 | tf_op jit(solution)/shard_map/ppermute | solution.py:404
  49.1 1.6 %collective-permute-start.23 = (bf16[16,4224]{1,0:T(8,128)(2,1)S(1)}, bf16[16,4224]{1,0:T(8,128)(2,1)S(1)}, u32[]{:S(2)}, u32[]{:S(2)}) collective-permute-start(bf16[16,4224]{1,0:T(8,128)(2,1)S(1)} %add_convert_fusion.1), channel_id=1, source_target_pairs={{0,4},{1,3},{2,0},{3,7},{4,8},{5,1},{6,2},{7,11},{8,12},{9,5},{10,... | collective-permute-start | bytes 405512 | tf_op jit(solution)/shard_map/ppermute | solution.py:404
  52.2 1.1 %collective-permute-done.23 = bf16[16,4224]{1,0:T(8,128)(2,1)S(1)} collective-permute-done((bf16[16,4224]{1,0:T(8,128)(2,1)S(1)}, bf16[16,4224]{1,0:T(8,128)(2,1)S(1)}, u32[]{:S(2)}, u32[]{:S(2)}) %collective-permute-start.23) | collective-permute-done | bytes 135200 | tf_op jit(solution)/shard_map/ppermute | solution.py:404
  53.3 1.6 %collective-permute-start.24 = (bf16[16,4224]{1,0:T(8,128)(2,1)S(1)}, bf16[16,4224]{1,0:T(8,128)(2,1)S(1)}, u32[]{:S(2)}, u32[]{:S(2)}) collective-permute-start(bf16[16,4224]{1,0:T(8,128)(2,1)S(1)} %add_convert_fusion), channel_id=1, source_target_pairs={{0,4},{1,3},{2,0},{3,7},{4,8},{5,1},{6,2},{7,11},{8,12},{9,5},{10,... | collective-permute-start | bytes 405512 | tf_op jit(solution)/shard_map/ppermute | solution.py:404
  55.7 3.4 %collective-permute-start.19 = (f32[16,4096]{1,0:T(8,128)S(1)}, f32[16,4096]{1,0:T(8,128)S(1)}, u32[]{:S(2)}, u32[]{:S(2)}) collective-permute-start(f32[16,4096]{1,0:T(8,128)S(1)} %convert_add_fusion.1.mine_ref), channel_id=1, source_target_pairs={{0,1},{1,0},{2,3},{3,2},{4,5},{5,4},{6,7},{7,6},{8,9},{9,8},{10,11... | collective-permute-start | bytes 786440 | tf_op jit(solution)/shard_map/ppermute | solution.py:407
  59.1 1.7 %shard_map.156.local_ref = f32[16,4224]{1,0:T(8,128)S(1)} custom-call(f32[128,128]{1,0:T(8,128)S(1)} %shard_map.149.refs_8_.mask_ref, bf16[128,4224]{1,0:T(8,128)(2,1)S(1)} %get-tuple-element.33.rows_ref, bf16[128,4224]{1,0:T(8,128)(2,1)S(1)} %get-tuple-element.30.tables_ref, bf16[128,4096]{1,0:T(8,128)(2,1)S(1)} %get-tuple-element.27.upstream_ref, ...), custom_call_target="tpu_custom_call" | custom-call | flops 1073741824 | bytes 5242880 | tf_op jit(solution)/shard_map/pallas_call | solution.py:366
  60.8 1.3 %collective-permute-start.25 = (f32[16,4224]{1,0:T(8,128)S(1)}, f32[16,4224]{1,0:T(8,128)S(1)}, u32[]{:S(2)}, u32[]{:S(2)}) collective-permute-start(f32[16,4224]{1,0:T(8,128)S(1)} %convert_add_fusion.mine_ref), channel_id=1, source_target_pairs={{0,1},{1,0},{2,3},{3,2},{4,5},{5,4},{6,7},{7,6},{8,9},{9,8},{10,11... | collective-permute-start | bytes 811016 | tf_op jit(solution)/shard_map/ppermute | solution.py:407
  62.2 1.9 %shard_map.154 = (bf16[16,4096]{1,0:T(8,128)(2,1)}, f32[8,128]{1,0:T(8,128)S(1)}) custom-call(s32[2]{0:T(128)S(1)} %pad_add_fusion.where_ref, s32[8]{0:T(128)S(1)} %copy-done.1, s32[8]{0:T(128)S(1)} %copy-done.2, s32[8]{0:T(128)S(1)} %copy-done.3, f32[16,4096]{1,0:T(8,128)S(1)} %convert_add_fusion.1.mine_ref, ...), custom_call_target="tpu_custom_call" | custom-call | flops 40000000000 | bytes 917504 | tf_op jit(solution)/shard_map/pallas_call | solution.py:366
  64.1 0.7 %shard_map.157 = (f32[1,8,4096]{2,1,0:T(8,128)}, f32[1,8,4096]{2,1,0:T(8,128)}, f32[1,8]{1,0:T(1,128)}) custom-call(f32[16,4224]{1,0:T(8,128)S(1)} %convert_add_fusion.mine_ref, f32[16,4224]{1,0:T(8,128)S(1)} %collective-permute-done.25.other_ref, f32[16,4224]{1,0:T(8,128)S(1)} %shard_map.156.local_ref, f32[8,128]{1,0:T(8,128)S(1)} %get-tuple-element.38.after), custom_call_target="tpu_custom_call" | custom-call | bytes 1310720 | tf_op jit(solution)/shard_map/pallas_call | solution.py:366
  (67 shorter events, 6.5 us)
Async XLA Ops:
  0.6 13.0 %copy-start.3 = (s32[8]{0:T(128)S(1)}, s32[8]{0:T(128)}, u32[]{:S(2)}) copy-start(s32[8]{0:T(128)} %slots_ref.3) | copy-start | bytes 100
  0.6 13.0 %copy-start.2 = (s32[8]{0:T(128)S(1)}, s32[8]{0:T(128)}, u32[]{:S(2)}) copy-start(s32[8]{0:T(128)} %starts_ref.3) | copy-start | bytes 100
  0.7 13.0 %copy-start.1 = (s32[8]{0:T(128)S(1)}, s32[8]{0:T(128)}, u32[]{:S(2)}) copy-start(s32[8]{0:T(128)} %counts_ref.3) | copy-start | bytes 100
  1.8 5.6 %collective-permute-start.7 = (bf16[16,6272]{1,0:T(8,128)(2,1)S(1)}, bf16[16,6272]{1,0:T(8,128)(2,1)S(1)}, u32[]{:S(2)}, u32[]{:S(2)}) collective-permute-start(bf16[16,6272]{1,0:T(8,128)(2,1)S(1)} %shard_map.148.refs_0_), channel_id=1, source_target_pairs={{0,4},{1,3},{2,0},{3,7},{4,8},{5,1},{6,2},{7,11},{8,12},{9,5},{10,... | collective-permute-start | bytes 602120 | tf_op jit(solution)/shard_map/ppermute | solution.py:404
  4.9 5.8 %collective-permute-start = (bf16[16,6272]{1,0:T(8,128)(2,1)S(1)}, bf16[16,6272]{1,0:T(8,128)(2,1)S(1)}, u32[]{:S(2)}, u32[]{:S(2)}) collective-permute-start(bf16[16,6272]{1,0:T(8,128)(2,1)S(1)} %shard_map.147.after.refs_0_), channel_id=1, source_target_pairs={{0,4},{1,3},{2,0},{3,7},{4,8},{5,1},{6,2},{7,11},{8,12},{9,5},{10,... | collective-permute-start | bytes 602120 | tf_op jit(solution)/shard_map/ppermute | solution.py:404
  7.4 4.9 %collective-permute-start.8 = (bf16[16,6272]{1,0:T(8,128)(2,1)S(1)}, bf16[16,6272]{1,0:T(8,128)(2,1)S(1)}, u32[]{:S(2)}, u32[]{:S(2)}) collective-permute-start(bf16[16,6272]{1,0:T(8,128)(2,1)S(1)} %collective-permute-done.7.after.refs_1_), channel_id=1, source_target_pairs={{0,4},{1,3},{2,0},{3,7},{4,8},{5,1},{6,2},{7,11},{8,12},{9,5},{10,... | collective-permute-start | bytes 602120 | tf_op jit(solution)/shard_map/ppermute | solution.py:404
  8.8 13.3 %collective-permute-start.10 = (bf16[16,6272]{1,0:T(8,128)(2,1)S(1)}, bf16[16,6272]{1,0:T(8,128)(2,1)S(1)}, u32[]{:S(2)}, u32[]{:S(2)}) collective-permute-start(bf16[16,6272]{1,0:T(8,128)(2,1)S(1)} %collective-permute-done.7.after.refs_1_), channel_id=1, source_target_pairs={{0,1},{1,0},{2,3},{3,2},{4,5},{5,4},{6,7},{7,6},{8,9},{9,8},{10,11... | collective-permute-start | bytes 602120 | tf_op jit(solution)/shard_map/ppermute | solution.py:407
  10.7 6.5 %collective-permute-start.1 = (bf16[16,6272]{1,0:T(8,128)(2,1)S(1)}, bf16[16,6272]{1,0:T(8,128)(2,1)S(1)}, u32[]{:S(2)}, u32[]{:S(2)}) collective-permute-start(bf16[16,6272]{1,0:T(8,128)(2,1)S(1)} %collective-permute-done.refs_1_), channel_id=1, source_target_pairs={{0,4},{1,3},{2,0},{3,7},{4,8},{5,1},{6,2},{7,11},{8,12},{9,5},{10,... | collective-permute-start | bytes 602120 | tf_op jit(solution)/shard_map/ppermute | solution.py:404
  12.2 5.5 %collective-permute-start.9 = (bf16[16,6272]{1,0:T(8,128)(2,1)S(1)}, bf16[16,6272]{1,0:T(8,128)(2,1)S(1)}, u32[]{:S(2)}, u32[]{:S(2)}) collective-permute-start(bf16[16,6272]{1,0:T(8,128)(2,1)S(1)} %collective-permute-done.8.after.refs_2_), channel_id=1, source_target_pairs={{0,4},{1,3},{2,0},{3,7},{4,8},{5,1},{6,2},{7,11},{8,12},{9,5},{10,... | collective-permute-start | bytes 602120 | tf_op jit(solution)/shard_map/ppermute | solution.py:404
  13.6 12.1 %slice-start.4 = ((s8[8388608]{0:T(1024)(128)(4,1)}), s8[4194304]{0:T(1024)(128)(4,1)S(1)}, s32[]{:S(2)}) async-start(s8[8388608]{0:T(1024)(128)(4,1)} %bitcast.8), calls=%async_computation.4 | async-start | bytes 8388608
  14.4 11.3 %slice-start.5 = ((s8[8388608]{0:T(1024)(128)(4,1)}), s8[4194304]{0:T(1024)(128)(4,1)S(1)}, s32[]{:S(2)}) async-start(s8[8388608]{0:T(1024)(128)(4,1)} %bitcast.8), calls=%async_computation.5 | async-start | bytes 8388608
  14.4 7.8 %collective-permute-start.11 = (bf16[16,6272]{1,0:T(8,128)(2,1)S(1)}, bf16[16,6272]{1,0:T(8,128)(2,1)S(1)}, u32[]{:S(2)}, u32[]{:S(2)}) collective-permute-start(bf16[16,6272]{1,0:T(8,128)(2,1)S(1)} %collective-permute-done.8.after.refs_2_), channel_id=1, source_target_pairs={{0,1},{1,0},{2,3},{3,2},{4,5},{5,4},{6,7},{7,6},{8,9},{9,8},{10,11... | collective-permute-start | bytes 602120 | tf_op jit(solution)/shard_map/ppermute | solution.py:407
  17.2 5.5 %collective-permute-start.2 = (bf16[16,6272]{1,0:T(8,128)(2,1)S(1)}, bf16[16,6272]{1,0:T(8,128)(2,1)S(1)}, u32[]{:S(2)}, u32[]{:S(2)}) collective-permute-start(bf16[16,6272]{1,0:T(8,128)(2,1)S(1)} %collective-permute-done.1.refs_2_), channel_id=1, source_target_pairs={{0,4},{1,3},{2,0},{3,7},{4,8},{5,1},{6,2},{7,11},{8,12},{9,5},{10,... | collective-permute-start | bytes 602120 | tf_op jit(solution)/shard_map/ppermute | solution.py:404
  17.7 6.5 %collective-permute-start.13 = (bf16[16,6272]{1,0:T(8,128)(2,1)S(1)}, bf16[16,6272]{1,0:T(8,128)(2,1)S(1)}, u32[]{:S(2)}, u32[]{:S(2)}) collective-permute-start(bf16[16,6272]{1,0:T(8,128)(2,1)S(1)} %collective-permute-done.9.refs_3_), channel_id=1, source_target_pairs={{0,4},{1,3},{2,0},{3,7},{4,8},{5,1},{6,2},{7,11},{8,12},{9,5},{10,... | collective-permute-start | bytes 602120 | tf_op jit(solution)/shard_map/ppermute | solution.py:404
  18.6 7.1 %collective-permute-start.12 = (bf16[16,6272]{1,0:T(8,128)(2,1)S(1)}, bf16[16,6272]{1,0:T(8,128)(2,1)S(1)}, u32[]{:S(2)}, u32[]{:S(2)}) collective-permute-start(bf16[16,6272]{1,0:T(8,128)(2,1)S(1)} %collective-permute-done.9.refs_3_), channel_id=1, source_target_pairs={{0,1},{1,0},{2,3},{3,2},{4,5},{5,4},{6,7},{7,6},{8,9},{9,8},{10,11... | collective-permute-start | bytes 602120 | tf_op jit(solution)/shard_map/ppermute | solution.py:407
  22.1 6.6 %slice-start.3 = ((s8[8388608]{0:T(1024)(128)(4,1)}), s8[4194304]{0:T(1024)(128)(4,1)S(1)}, s32[]{:S(2)}) async-start(s8[8388608]{0:T(1024)(128)(4,1)} %bitcast.5), calls=%async_computation.3 | async-start | bytes 8388608
  22.1 6.5 %collective-permute-start.3 = (bf16[16,6272]{1,0:T(8,128)(2,1)S(1)}, bf16[16,6272]{1,0:T(8,128)(2,1)S(1)}, u32[]{:S(2)}, u32[]{:S(2)}) collective-permute-start(bf16[16,6272]{1,0:T(8,128)(2,1)S(1)} %collective-permute-done.refs_1_), channel_id=1, source_target_pairs={{0,1},{1,0},{2,3},{3,2},{4,5},{5,4},{6,7},{7,6},{8,9},{9,8},{10,11... | collective-permute-start | bytes 602120 | tf_op jit(solution)/shard_map/ppermute | solution.py:407
  22.2 6.4 %collective-permute-start.4 = (bf16[16,6272]{1,0:T(8,128)(2,1)S(1)}, bf16[16,6272]{1,0:T(8,128)(2,1)S(1)}, u32[]{:S(2)}, u32[]{:S(2)}) collective-permute-start(bf16[16,6272]{1,0:T(8,128)(2,1)S(1)} %collective-permute-done.1.refs_2_), channel_id=1, source_target_pairs={{0,1},{1,0},{2,3},{3,2},{4,5},{5,4},{6,7},{7,6},{8,9},{9,8},{10,11... | collective-permute-start | bytes 602120 | tf_op jit(solution)/shard_map/ppermute | solution.py:407
  22.7 5.9 %collective-permute-start.6 = (bf16[16,6272]{1,0:T(8,128)(2,1)S(1)}, bf16[16,6272]{1,0:T(8,128)(2,1)S(1)}, u32[]{:S(2)}, u32[]{:S(2)}) collective-permute-start(bf16[16,6272]{1,0:T(8,128)(2,1)S(1)} %collective-permute-done.2.refs_3_), channel_id=1, source_target_pairs={{0,4},{1,3},{2,0},{3,7},{4,8},{5,1},{6,2},{7,11},{8,12},{9,5},{10,... | collective-permute-start | bytes 602120 | tf_op jit(solution)/shard_map/ppermute | solution.py:404
  24.2 4.4 %collective-permute-start.5 = (bf16[16,6272]{1,0:T(8,128)(2,1)S(1)}, bf16[16,6272]{1,0:T(8,128)(2,1)S(1)}, u32[]{:S(2)}, u32[]{:S(2)}) collective-permute-start(bf16[16,6272]{1,0:T(8,128)(2,1)S(1)} %collective-permute-done.2.refs_3_), channel_id=1, source_target_pairs={{0,1},{1,0},{2,3},{3,2},{4,5},{5,4},{6,7},{7,6},{8,9},{9,8},{10,11... | collective-permute-start | bytes 602120 | tf_op jit(solution)/shard_map/ppermute | solution.py:407
  38.2 5.1 %collective-permute-start.15 = (bf16[48,4096]{1,0:T(8,128)(2,1)S(1)}, bf16[48,4096]{1,0:T(8,128)(2,1)S(1)}, u32[]{:S(2)}, u32[]{:S(2)}) collective-permute-start(bf16[48,4096]{1,0:T(8,128)(2,1)S(1)} %slice.50), channel_id=1, source_target_pairs={{0,1},{1,0},{2,3},{3,2},{4,5},{5,4},{6,7},{7,6},{8,9},{9,8},{10,11... | collective-permute-start | bytes 1179656 | tf_op jit(solution)/shard_map/ppermute | solution.py:407
  38.4 4.8 %collective-permute-start.14 = (bf16[16,4096]{1,0:T(8,128)(2,1)S(1)}, bf16[16,4096]{1,0:T(8,128)(2,1)S(1)}, u32[]{:S(2)}, u32[]{:S(2)}) collective-permute-start(bf16[16,4096]{1,0:T(8,128)(2,1)S(1)} %slice.48), channel_id=1, source_target_pairs={{0,4},{1,3},{2,0},{3,7},{4,8},{5,1},{6,2},{7,11},{8,12},{9,5},{10,... | collective-permute-start | bytes 393224 | tf_op jit(solution)/shard_map/ppermute | solution.py:404
  40.8 4.2 %collective-permute-start.20 = (bf16[16,4224]{1,0:T(8,128)(2,1)S(1)}, bf16[16,4224]{1,0:T(8,128)(2,1)S(1)}, u32[]{:S(2)}, u32[]{:S(2)}) collective-permute-start(bf16[16,4224]{1,0:T(8,128)(2,1)S(1)} %slice.56), channel_id=1, source_target_pairs={{0,4},{1,3},{2,0},{3,7},{4,8},{5,1},{6,2},{7,11},{8,12},{9,5},{10,... | collective-permute-start | bytes 405512 | tf_op jit(solution)/shard_map/ppermute | solution.py:404
  42.2 2.9 %collective-permute-start.21 = (bf16[48,4224]{1,0:T(8,128)(2,1)S(1)}, bf16[48,4224]{1,0:T(8,128)(2,1)S(1)}, u32[]{:S(2)}, u32[]{:S(2)}) collective-permute-start(bf16[48,4224]{1,0:T(8,128)(2,1)S(1)} %slice.58), channel_id=1, source_target_pairs={{0,1},{1,0},{2,3},{3,2},{4,5},{5,4},{6,7},{7,6},{8,9},{9,8},{10,11... | collective-permute-start | bytes 1216520 | tf_op jit(solution)/shard_map/ppermute | solution.py:407
  43.3 4.2 %collective-permute-start.16 = (bf16[16,4096]{1,0:T(8,128)(2,1)S(1)}, bf16[16,4096]{1,0:T(8,128)(2,1)S(1)}, u32[]{:S(2)}, u32[]{:S(2)}) collective-permute-start(bf16[16,4096]{1,0:T(8,128)(2,1)S(1)} %add_convert_fusion.5), channel_id=1, source_target_pairs={{0,4},{1,3},{2,0},{3,7},{4,8},{5,1},{6,2},{7,11},{8,12},{9,5},{10,... | collective-permute-start | bytes 393224 | tf_op jit(solution)/shard_map/ppermute | solution.py:404
  45.1 3.9 %collective-permute-start.22 = (bf16[16,4224]{1,0:T(8,128)(2,1)S(1)}, bf16[16,4224]{1,0:T(8,128)(2,1)S(1)}, u32[]{:S(2)}, u32[]{:S(2)}) collective-permute-start(bf16[16,4224]{1,0:T(8,128)(2,1)S(1)} %add_convert_fusion.2), channel_id=1, source_target_pairs={{0,4},{1,3},{2,0},{3,7},{4,8},{5,1},{6,2},{7,11},{8,12},{9,5},{10,... | collective-permute-start | bytes 405512 | tf_op jit(solution)/shard_map/ppermute | solution.py:404
  47.5 3.9 %collective-permute-start.17 = (bf16[16,4096]{1,0:T(8,128)(2,1)S(1)}, bf16[16,4096]{1,0:T(8,128)(2,1)S(1)}, u32[]{:S(2)}, u32[]{:S(2)}) collective-permute-start(bf16[16,4096]{1,0:T(8,128)(2,1)S(1)} %add_convert_fusion.4), channel_id=1, source_target_pairs={{0,4},{1,3},{2,0},{3,7},{4,8},{5,1},{6,2},{7,11},{8,12},{9,5},{10,... | collective-permute-start | bytes 393224 | tf_op jit(solution)/shard_map/ppermute | solution.py:404
  49.1 4.2 %collective-permute-start.23 = (bf16[16,4224]{1,0:T(8,128)(2,1)S(1)}, bf16[16,4224]{1,0:T(8,128)(2,1)S(1)}, u32[]{:S(2)}, u32[]{:S(2)}) collective-permute-start(bf16[16,4224]{1,0:T(8,128)(2,1)S(1)} %add_convert_fusion.1), channel_id=1, source_target_pairs={{0,4},{1,3},{2,0},{3,7},{4,8},{5,1},{6,2},{7,11},{8,12},{9,5},{10,... | collective-permute-start | bytes 405512 | tf_op jit(solution)/shard_map/ppermute | solution.py:404
  51.5 4.2 %collective-permute-start.18 = (bf16[16,4096]{1,0:T(8,128)(2,1)S(1)}, bf16[16,4096]{1,0:T(8,128)(2,1)S(1)}, u32[]{:S(2)}, u32[]{:S(2)}) collective-permute-start(bf16[16,4096]{1,0:T(8,128)(2,1)S(1)} %add_convert_fusion.3), channel_id=1, source_target_pairs={{0,4},{1,3},{2,0},{3,7},{4,8},{5,1},{6,2},{7,11},{8,12},{9,5},{10,... | collective-permute-start | bytes 393224 | tf_op jit(solution)/shard_map/ppermute | solution.py:404
  53.3 7.4 %collective-permute-start.24 = (bf16[16,4224]{1,0:T(8,128)(2,1)S(1)}, bf16[16,4224]{1,0:T(8,128)(2,1)S(1)}, u32[]{:S(2)}, u32[]{:S(2)}) collective-permute-start(bf16[16,4224]{1,0:T(8,128)(2,1)S(1)} %add_convert_fusion), channel_id=1, source_target_pairs={{0,4},{1,3},{2,0},{3,7},{4,8},{5,1},{6,2},{7,11},{8,12},{9,5},{10,... | collective-permute-start | bytes 405512 | tf_op jit(solution)/shard_map/ppermute | solution.py:404
  55.7 6.5 %collective-permute-start.19 = (f32[16,4096]{1,0:T(8,128)S(1)}, f32[16,4096]{1,0:T(8,128)S(1)}, u32[]{:S(2)}, u32[]{:S(2)}) collective-permute-start(f32[16,4096]{1,0:T(8,128)S(1)} %convert_add_fusion.1.mine_ref), channel_id=1, source_target_pairs={{0,1},{1,0},{2,3},{3,2},{4,5},{5,4},{6,7},{7,6},{8,9},{9,8},{10,11... | collective-permute-start | bytes 786440 | tf_op jit(solution)/shard_map/ppermute | solution.py:407
  60.8 3.3 %collective-permute-start.25 = (f32[16,4224]{1,0:T(8,128)S(1)}, f32[16,4224]{1,0:T(8,128)S(1)}, u32[]{:S(2)}, u32[]{:S(2)}) collective-permute-start(f32[16,4224]{1,0:T(8,128)S(1)} %convert_add_fusion.mine_ref), channel_id=1, source_target_pairs={{0,1},{1,0},{2,3},{3,2},{4,5},{5,4},{6,7},{7,6},{8,9},{9,8},{10,11... | collective-permute-start | bytes 811016 | tf_op jit(solution)/shard_map/ppermute | solution.py:407
  (4 other events, 26.4 us)

commit v5 on v4

--- a/solution.py
+++ b/solution.py
@@ -176,6 +176,7 @@
         stats_ref,
         normed_ref,
         gate_t_ref,
+        up_t_ref,
         gate_grad_ref,
         up_grad_ref,
     ) = refs[n:]
@@ -193,9 +194,11 @@
     coeffs_ref[...] = coeffs
     coeff_high, coeff_low = split(coeffs)
 
-    def middle_step(c, carry):
-        squares, middle_tables = carry
-        cols = columns_at(c, step)
+    column_zero = jnp.zeros((row_total, 1), F32)
+    square_zero = jnp.zeros((row_total, columns), F32)
+    squares, middle_tables = column_zero, square_zero
+    for c in range(chunks):
+        cols = slice(c * step, (c + 1) * step)
         table = tables_ref[:, cols]
         value = rows_ref[:, cols].astype(F32) + (
             dot_nn(coeff_high, table) + dot_nn(coeff_low, table)
@@ -204,20 +207,13 @@
         middle_ref[:, cols] = value
         middle_tables = middle_tables + dot_nt(value, table)
         value = value.astype(F32)
-        return squares + jnp.sum(value * value, axis=1, keepdims=True), middle_tables
-
-    column_zero = jnp.zeros((row_total, 1), F32)
-    square_zero = jnp.zeros((row_total, columns), F32)
-    squares, middle_tables = lax.fori_loop(0, chunks, middle_step, (column_zero, square_zero))
+        squares = squares + jnp.sum(value * value, axis=1, keepdims=True)
     inverse = lax.rsqrt(squares / width + EPS)
 
-    def normed_step(c, carry):
-        cols = columns_at(c, step)
+    for c in range(chunks):
+        cols = slice(c * step, (c + 1) * step)
         value = middle_ref[:, cols].astype(F32) * inverse * gain_ref[:, cols]
         normed_ref[:, cols] = value.astype(BF)
-        return carry
-
-    lax.fori_loop(0, chunks, normed_step, 0)
 
     hidden = gate_ref.shape[1]
     tile = min(256, hidden)
@@ -226,6 +222,7 @@
         gate = dot_nn(normed_ref[...], gate_ref[:, cols])
         gate_t_ref[cols, :] = gate_ref[:, cols].T
         upward = dot_nn(normed_ref[...], up_ref[:, cols])
+        up_t_ref[cols, :] = up_ref[:, cols].T
         back = back_ref[:, cols]
         sigma = jax.nn.sigmoid(gate)
         gate_grad_ref[:, cols] = (back * upward * sigma * (1.0 + gate * (1.0 - sigma))).astype(BF)
@@ -235,7 +232,7 @@
     for c in range(chunks):
         cols = slice(c * step, (c + 1) * step)
         value = dot_nn(gate_grad_ref[...], gate_t_ref[:, cols])
-        value = value + dot_nt(up_grad_ref[...], up_ref[cols, :])
+        value = value + dot_nn(up_grad_ref[...], up_t_ref[:, cols])
         value = value * gain_ref[:, cols]
         scaled_ref[:, cols] = value
         own_ref[:, cols] = value[:SEG]
@@ -522,12 +519,13 @@
             scratch=[
                 pltpu.VMEM((rows_total, width), BF),
                 pltpu.VMEM((hidden, width), BF),
+                pltpu.VMEM((hidden, width), BF),
                 pltpu.VMEM((rows_total, hidden), BF),
                 pltpu.VMEM((rows_total, hidden), BF),
             ],
             flops=4 * work,
             moved=4 * width * hidden,
-            limit=n + n // 2 + 8,
+            limit=n + n // 2 + (4 * hidden * width) // 2**20,
         )
         own_slot, sent_slot = call(
             functools.partial(slot_kernel, 1024),

time: 65 us -> 63.3 us (0.974)
  Pallas kernels: 20.1 us -> 18.4 us
    pallas_call x11, Pallas kernels: 20.1 us -> 18.4 us  [call(): pl.pallas_call(kernel, out_shape=tuple((jax.ShapeDtypeStruct(s, d) for s,...]
where the time goes in v5:
time: 63.3 us; the launch traced here: 63.1 us
  starting transfers between devices  33.8 us (53%)
  Pallas kernels  18.4 us (29%)
  waiting for transfers between devices  9.44 us (15%)
  between operations  0.93 us (1%)
    pallas_call x11, Pallas kernels, call(): pl.pallas_call(kernel, out_shape=tuple((jax.ShapeDtypeStruct(s, d) for s,...  18.4 us
    ppermute x16, starting transfers between devices, hop(): return lax.ppermute(x, ('dp', 'tensor'), pairs)  17.5 us
    ppermute x10, starting transfers between devices, swap(): return lax.ppermute(x, 'tensor', [(0, 1), (1, 0)])  16.3 us
    ppermute x16, waiting for transfers between devices, hop(): return lax.ppermute(x, ('dp', 'tensor'), pairs)  9.42 us
  transfers between devices with their start and end apart: 26, of which 10 were waited for; matrix products, arithmetic and copies ran while one was open for 1% of the time, Pallas kernels for 14%

profile of v5, /device:TPU:1, one launch (start us, length us, event | category | flops | bytes accessed | tf_op | source)
XLA Modules:
  0.0 63.1 jit_solution(9668391845807984647)
XLA Ops:
  0.7 1.1 %shard_map.148.refs_0_ = bf16[16,6272]{1,0:T(8,128)(2,1)S(1)} custom-call(bf16[16,4096]{1,0:T(8,128)(2,1)} %upstream_hbm.1, bf16[1,8,4096]{2,1,0:T(8,128)(2,1)} %basis_hbm.3, bf16[1,8,4096]{2,1,0:T(8,128)(2,1)} %learned_hbm.3, bf16[1,8]{1,0:T(2,128)(2,1)} %bias_hbm.1), custom_call_target="tpu_custom_call" | custom-call | bytes 540672 | tf_op jit(solution)/shard_map/pallas_call | solution.py:363
  1.8 2.1 %collective-permute-start.7 = (bf16[16,6272]{1,0:T(8,128)(2,1)S(1)}, bf16[16,6272]{1,0:T(8,128)(2,1)S(1)}, u32[]{:S(2)}, u32[]{:S(2)}) collective-permute-start(bf16[16,6272]{1,0:T(8,128)(2,1)S(1)} %shard_map.148.refs_0_), channel_id=1, source_target_pairs={{0,4},{1,3},{2,0},{3,7},{4,8},{5,1},{6,2},{7,11},{8,12},{9,5},{10,... | collective-permute-start | bytes 602120 | tf_op jit(solution)/shard_map/ppermute | solution.py:401
  3.9 1.0 %shard_map.147.after.refs_0_ = bf16[16,6272]{1,0:T(8,128)(2,1)S(1)} custom-call(bf16[16,4096]{1,0:T(8,128)(2,1)} %hidden_hbm.1, bf16[1,8,4096]{2,1,0:T(8,128)(2,1)} %basis_hbm.3, bf16[1,8,4096]{2,1,0:T(8,128)(2,1)} %learned_hbm.3), custom_call_target="tpu_custom_call" | custom-call | bytes 540672 | tf_op jit(solution)/shard_map/pallas_call | solution.py:363
  4.9 1.3 %collective-permute-start = (bf16[16,6272]{1,0:T(8,128)(2,1)S(1)}, bf16[16,6272]{1,0:T(8,128)(2,1)S(1)}, u32[]{:S(2)}, u32[]{:S(2)}) collective-permute-start(bf16[16,6272]{1,0:T(8,128)(2,1)S(1)} %shard_map.147.after.refs_0_), channel_id=1, source_target_pairs={{0,4},{1,3},{2,0},{3,7},{4,8},{5,1},{6,2},{7,11},{8,12},{9,5},{10,... | collective-permute-start | bytes 602120 | tf_op jit(solution)/shard_map/ppermute | solution.py:401
  6.2 1.1 %collective-permute-done.7.after.refs_1_ = bf16[16,6272]{1,0:T(8,128)(2,1)S(1)} collective-permute-done((bf16[16,6272]{1,0:T(8,128)(2,1)S(1)}, bf16[16,6272]{1,0:T(8,128)(2,1)S(1)}, u32[]{:S(2)}, u32[]{:S(2)}) %collective-permute-start.7) | collective-permute-done | bytes 200736 | tf_op jit(solution)/shard_map/ppermute | solution.py:401
  7.4 1.4 %collective-permute-start.8 = (bf16[16,6272]{1,0:T(8,128)(2,1)S(1)}, bf16[16,6272]{1,0:T(8,128)(2,1)S(1)}, u32[]{:S(2)}, u32[]{:S(2)}) collective-permute-start(bf16[16,6272]{1,0:T(8,128)(2,1)S(1)} %collective-permute-done.7.after.refs_1_), channel_id=1, source_target_pairs={{0,4},{1,3},{2,0},{3,7},{4,8},{5,1},{6,2},{7,11},{8,12},{9,5},{10,... | collective-permute-start | bytes 602120 | tf_op jit(solution)/shard_map/ppermute | solution.py:401
  8.8 1.9 %collective-permute-start.10 = (bf16[16,6272]{1,0:T(8,128)(2,1)S(1)}, bf16[16,6272]{1,0:T(8,128)(2,1)S(1)}, u32[]{:S(2)}, u32[]{:S(2)}) collective-permute-start(bf16[16,6272]{1,0:T(8,128)(2,1)S(1)} %collective-permute-done.7.after.refs_1_), channel_id=1, source_target_pairs={{0,1},{1,0},{2,3},{3,2},{4,5},{5,4},{6,7},{7,6},{8,9},{9,8},{10,11... | collective-permute-start | bytes 602120 | tf_op jit(solution)/shard_map/ppermute | solution.py:404
  11.1 1.1 %collective-permute-done.8.after.refs_2_ = bf16[16,6272]{1,0:T(8,128)(2,1)S(1)} collective-permute-done((bf16[16,6272]{1,0:T(8,128)(2,1)S(1)}, bf16[16,6272]{1,0:T(8,128)(2,1)S(1)}, u32[]{:S(2)}, u32[]{:S(2)}) %collective-permute-start.8) | collective-permute-done | bytes 200736 | tf_op jit(solution)/shard_map/ppermute | solution.py:401
  12.2 1.4 %collective-permute-start.9 = (bf16[16,6272]{1,0:T(8,128)(2,1)S(1)}, bf16[16,6272]{1,0:T(8,128)(2,1)S(1)}, u32[]{:S(2)}, u32[]{:S(2)}) collective-permute-start(bf16[16,6272]{1,0:T(8,128)(2,1)S(1)} %collective-permute-done.8.after.refs_2_), channel_id=1, source_target_pairs={{0,4},{1,3},{2,0},{3,7},{4,8},{5,1},{6,2},{7,11},{8,12},{9,5},{10,... | collective-permute-start | bytes 602120 | tf_op jit(solution)/shard_map/ppermute | solution.py:401
  13.6 0.7 %shard_map.149.refs_8_.mask_ref = f32[128,128]{1,0:T(8,128)S(1)} custom-call(s32[2]{0:T(128)S(1)} %pad_add_fusion.where_ref, s32[8]{0:T(128)S(1)} %copy-done.1, s32[8]{0:T(128)S(1)} %copy-done.2, s32[8]{0:T(128)S(1)} %copy-done.3, bf16[16,6272]{1,0:T(8,128)(2,1)S(1)} %collective-permute-done.7.after.refs_1_), custom_call_target="tpu_custom_call" | custom-call | flops 4000000000 | tf_op jit(solution)/shard_map/pallas_call | solution.py:363
  14.4 2.8 %collective-permute-start.11 = (bf16[16,6272]{1,0:T(8,128)(2,1)S(1)}, bf16[16,6272]{1,0:T(8,128)(2,1)S(1)}, u32[]{:S(2)}, u32[]{:S(2)}) collective-permute-start(bf16[16,6272]{1,0:T(8,128)(2,1)S(1)} %collective-permute-done.8.after.refs_2_), channel_id=1, source_target_pairs={{0,1},{1,0},{2,3},{3,2},{4,5},{5,4},{6,7},{7,6},{8,9},{9,8},{10,11... | collective-permute-start | bytes 602120 | tf_op jit(solution)/shard_map/ppermute | solution.py:404
  17.7 0.9 %collective-permute-start.13 = (bf16[16,6272]{1,0:T(8,128)(2,1)S(1)}, bf16[16,6272]{1,0:T(8,128)(2,1)S(1)}, u32[]{:S(2)}, u32[]{:S(2)}) collective-permute-start(bf16[16,6272]{1,0:T(8,128)(2,1)S(1)} %collective-permute-done.9.refs_3_), channel_id=1, source_target_pairs={{0,4},{1,3},{2,0},{3,7},{4,8},{5,1},{6,2},{7,11},{8,12},{9,5},{10,... | collective-permute-start | bytes 602120 | tf_op jit(solution)/shard_map/ppermute | solution.py:401
  18.6 3.4 %collective-permute-start.12 = (bf16[16,6272]{1,0:T(8,128)(2,1)S(1)}, bf16[16,6272]{1,0:T(8,128)(2,1)S(1)}, u32[]{:S(2)}, u32[]{:S(2)}) collective-permute-start(bf16[16,6272]{1,0:T(8,128)(2,1)S(1)} %collective-permute-done.9.refs_3_), channel_id=1, source_target_pairs={{0,1},{1,0},{2,3},{3,2},{4,5},{5,4},{6,7},{7,6},{8,9},{9,8},{10,11... | collective-permute-start | bytes 602120 | tf_op jit(solution)/shard_map/ppermute | solution.py:404
  22.7 1.5 %collective-permute-done.13.refs_7_ = bf16[16,6272]{1,0:T(8,128)(2,1)S(1)} collective-permute-done((bf16[16,6272]{1,0:T(8,128)(2,1)S(1)}, bf16[16,6272]{1,0:T(8,128)(2,1)S(1)}, u32[]{:S(2)}, u32[]{:S(2)}) %collective-permute-start.13) | collective-permute-done | bytes 200736 | tf_op jit(solution)/shard_map/ppermute | solution.py:401
  24.2 1.5 %collective-permute-start.5 = (bf16[16,6272]{1,0:T(8,128)(2,1)S(1)}, bf16[16,6272]{1,0:T(8,128)(2,1)S(1)}, u32[]{:S(2)}, u32[]{:S(2)}) collective-permute-start(bf16[16,6272]{1,0:T(8,128)(2,1)S(1)} %collective-permute-done.2.refs_3_), channel_id=1, source_target_pairs={{0,1},{1,0},{2,3},{3,2},{4,5},{5,4},{6,7},{7,6},{8,9},{9,8},{10,11... | collective-permute-start | bytes 602120 | tf_op jit(solution)/shard_map/ppermute | solution.py:404
  25.7 2.9 %shard_map.152 = (bf16[128,4096]{1,0:T(8,128)(2,1)S(1)}, bf16[128,2176]{1,0:T(8,128)(2,1)S(1)}, f32[128,1024]{1,0:T(8,128)S(1)}) custom-call(bf16[16,6272]{1,0:T(8,128)(2,1)S(1)} %shard_map.148.refs_0_, bf16[16,6272]{1,0:T(8,128)(2,1)S(1)} %collective-permute-done.7.after.refs_1_, bf16[16,6272]{1,0:T(8,128)(2,1)S(1)} %collective-permute-done.8.after.refs_2_, ...), custom_call_target="tpu_custom_call" | custom-call | flops 40000000000 | bytes 8388608 | tf_op jit(solution)/shard_map/pallas_call | solution.py:363
  28.7 7.7 %shard_map.153 = (f32[16,4096]{1,0:T(8,128)S(1)}, bf16[112,4096]{1,0:T(8,128)(2,1)S(1)}, f32[128,4096]{1,0:T(8,128)S(1)}, bf16[128,4224]{1,0:T(8,128)(2,1)S(1)},...) custom-call(bf16[16,6272]{1,0:T(8,128)(2,1)S(1)} %shard_map.147.afte, ...), custom_call_target="tpu_custom_call" | custom-call | flops 4294967296 | bytes 16777216 | tf_op jit(solution)/shard_map/pallas_call | solution.py:363
  36.7 1.7 %collective-permute-start.14 = (bf16[16,4096]{1,0:T(8,128)(2,1)S(1)}, bf16[16,4096]{1,0:T(8,128)(2,1)S(1)}, u32[]{:S(2)}, u32[]{:S(2)}) collective-permute-start(bf16[16,4096]{1,0:T(8,128)(2,1)S(1)} %slice.48), channel_id=1, source_target_pairs={{0,4},{1,3},{2,0},{3,7},{4,8},{5,1},{6,2},{7,11},{8,12},{9,5},{10,... | collective-permute-start | bytes 393224 | tf_op jit(solution)/shard_map/ppermute | solution.py:401
  39.1 1.3 %collective-permute-start.20 = (bf16[16,4224]{1,0:T(8,128)(2,1)S(1)}, bf16[16,4224]{1,0:T(8,128)(2,1)S(1)}, u32[]{:S(2)}, u32[]{:S(2)}) collective-permute-start(bf16[16,4224]{1,0:T(8,128)(2,1)S(1)} %slice.56), channel_id=1, source_target_pairs={{0,4},{1,3},{2,0},{3,7},{4,8},{5,1},{6,2},{7,11},{8,12},{9,5},{10,... | collective-permute-start | bytes 405512 | tf_op jit(solution)/shard_map/ppermute | solution.py:401
  40.4 1.1 %collective-permute-start.21 = (bf16[48,4224]{1,0:T(8,128)(2,1)S(1)}, bf16[48,4224]{1,0:T(8,128)(2,1)S(1)}, u32[]{:S(2)}, u32[]{:S(2)}) collective-permute-start(bf16[48,4224]{1,0:T(8,128)(2,1)S(1)} %slice.58), channel_id=1, source_target_pairs={{0,1},{1,0},{2,3},{3,2},{4,5},{5,4},{6,7},{7,6},{8,9},{9,8},{10,11... | collective-permute-start | bytes 1216520 | tf_op jit(solution)/shard_map/ppermute | solution.py:404
  41.6 1.0 %collective-permute-start.16 = (bf16[16,4096]{1,0:T(8,128)(2,1)S(1)}, bf16[16,4096]{1,0:T(8,128)(2,1)S(1)}, u32[]{:S(2)}, u32[]{:S(2)}) collective-permute-start(bf16[16,4096]{1,0:T(8,128)(2,1)S(1)} %add_convert_fusion.5), channel_id=1, source_target_pairs={{0,4},{1,3},{2,0},{3,7},{4,8},{5,1},{6,2},{7,11},{8,12},{9,5},{10,... | collective-permute-start | bytes 393224 | tf_op jit(solution)/shard_map/ppermute | solution.py:401
  43.4 1.3 %collective-permute-start.22 = (bf16[16,4224]{1,0:T(8,128)(2,1)S(1)}, bf16[16,4224]{1,0:T(8,128)(2,1)S(1)}, u32[]{:S(2)}, u32[]{:S(2)}) collective-permute-start(bf16[16,4224]{1,0:T(8,128)(2,1)S(1)} %add_convert_fusion.2), channel_id=1, source_target_pairs={{0,4},{1,3},{2,0},{3,7},{4,8},{5,1},{6,2},{7,11},{8,12},{9,5},{10,... | collective-permute-start | bytes 405512 | tf_op jit(solution)/shard_map/ppermute | solution.py:401
  44.7 1.1 %collective-permute-done.16 = bf16[16,4096]{1,0:T(8,128)(2,1)S(1)} collective-permute-done((bf16[16,4096]{1,0:T(8,128)(2,1)S(1)}, bf16[16,4096]{1,0:T(8,128)(2,1)S(1)}, u32[]{:S(2)}, u32[]{:S(2)}) %collective-permute-start.16) | collective-permute-done | bytes 131104 | tf_op jit(solution)/shard_map/ppermute | solution.py:401
  46.5 0.8 %collective-permute-done.22 = bf16[16,4224]{1,0:T(8,128)(2,1)S(1)} collective-permute-done((bf16[16,4224]{1,0:T(8,128)(2,1)S(1)}, bf16[16,4224]{1,0:T(8,128)(2,1)S(1)}, u32[]{:S(2)}, u32[]{:S(2)}) %collective-permute-start.22) | collective-permute-done | bytes 135200 | tf_op jit(solution)/shard_map/ppermute | solution.py:401
  47.3 1.6 %collective-permute-start.23 = (bf16[16,4224]{1,0:T(8,128)(2,1)S(1)}, bf16[16,4224]{1,0:T(8,128)(2,1)S(1)}, u32[]{:S(2)}, u32[]{:S(2)}) collective-permute-start(bf16[16,4224]{1,0:T(8,128)(2,1)S(1)} %add_convert_fusion.1), channel_id=1, source_target_pairs={{0,4},{1,3},{2,0},{3,7},{4,8},{5,1},{6,2},{7,11},{8,12},{9,5},{10,... | collective-permute-start | bytes 405512 | tf_op jit(solution)/shard_map/ppermute | solution.py:401
  49.0 0.7 %collective-permute-done.17 = bf16[16,4096]{1,0:T(8,128)(2,1)S(1)} collective-permute-done((bf16[16,4096]{1,0:T(8,128)(2,1)S(1)}, bf16[16,4096]{1,0:T(8,128)(2,1)S(1)}, u32[]{:S(2)}, u32[]{:S(2)}) %collective-permute-start.17) | collective-permute-done | bytes 131104 | tf_op jit(solution)/shard_map/ppermute | solution.py:401
  50.4 1.1 %collective-permute-done.23 = bf16[16,4224]{1,0:T(8,128)(2,1)S(1)} collective-permute-done((bf16[16,4224]{1,0:T(8,128)(2,1)S(1)}, bf16[16,4224]{1,0:T(8,128)(2,1)S(1)}, u32[]{:S(2)}, u32[]{:S(2)}) %collective-permute-start.23) | collective-permute-done | bytes 135200 | tf_op jit(solution)/shard_map/ppermute | solution.py:401
  51.6 1.6 %collective-permute-start.24 = (bf16[16,4224]{1,0:T(8,128)(2,1)S(1)}, bf16[16,4224]{1,0:T(8,128)(2,1)S(1)}, u32[]{:S(2)}, u32[]{:S(2)}) collective-permute-start(bf16[16,4224]{1,0:T(8,128)(2,1)S(1)} %add_convert_fusion), channel_id=1, source_target_pairs={{0,4},{1,3},{2,0},{3,7},{4,8},{5,1},{6,2},{7,11},{8,12},{9,5},{10,... | collective-permute-start | bytes 405512 | tf_op jit(solution)/shard_map/ppermute | solution.py:401
  54.0 3.4 %collective-permute-start.19 = (f32[16,4096]{1,0:T(8,128)S(1)}, f32[16,4096]{1,0:T(8,128)S(1)}, u32[]{:S(2)}, u32[]{:S(2)}) collective-permute-start(f32[16,4096]{1,0:T(8,128)S(1)} %convert_add_fusion.1.mine_ref), channel_id=1, source_target_pairs={{0,1},{1,0},{2,3},{3,2},{4,5},{5,4},{6,7},{7,6},{8,9},{9,8},{10,11... | collective-permute-start | bytes 786440 | tf_op jit(solution)/shard_map/ppermute | solution.py:404
  57.4 1.7 %shard_map.156.local_ref = f32[16,4224]{1,0:T(8,128)S(1)} custom-call(f32[128,128]{1,0:T(8,128)S(1)} %shard_map.149.refs_8_.mask_ref, bf16[128,4224]{1,0:T(8,128)(2,1)S(1)} %get-tuple-element.33.rows_ref, bf16[128,4224]{1,0:T(8,128)(2,1)S(1)} %get-tuple-element.30.tables_ref, bf16[128,4096]{1,0:T(8,128)(2,1)S(1)} %get-tuple-element.27.upstream_ref, ...), custom_call_target="tpu_custom_call" | custom-call | flops 1073741824 | bytes 5242880 | tf_op jit(solution)/shard_map/pallas_call | solution.py:363
  59.1 1.4 %collective-permute-start.25 = (f32[16,4224]{1,0:T(8,128)S(1)}, f32[16,4224]{1,0:T(8,128)S(1)}, u32[]{:S(2)}, u32[]{:S(2)}) collective-permute-start(f32[16,4224]{1,0:T(8,128)S(1)} %convert_add_fusion.mine_ref), channel_id=1, source_target_pairs={{0,1},{1,0},{2,3},{3,2},{4,5},{5,4},{6,7},{7,6},{8,9},{9,8},{10,11... | collective-permute-start | bytes 811016 | tf_op jit(solution)/shard_map/ppermute | solution.py:404
  60.5 1.9 %shard_map.154 = (bf16[16,4096]{1,0:T(8,128)(2,1)}, f32[8,128]{1,0:T(8,128)S(1)}) custom-call(s32[2]{0:T(128)S(1)} %pad_add_fusion.where_ref, s32[8]{0:T(128)S(1)} %copy-done.1, s32[8]{0:T(128)S(1)} %copy-done.2, s32[8]{0:T(128)S(1)} %copy-done.3, f32[16,4096]{1,0:T(8,128)S(1)} %convert_add_fusion.1.mine_ref, ...), custom_call_target="tpu_custom_call" | custom-call | flops 40000000000 | bytes 917504 | tf_op jit(solution)/shard_map/pallas_call | solution.py:363
  (67 shorter events, 6.4 us)
Async XLA Ops:
  0.6 13.0 %copy-start.3 = (s32[8]{0:T(128)S(1)}, s32[8]{0:T(128)}, u32[]{:S(2)}) copy-start(s32[8]{0:T(128)} %slots_ref.3) | copy-start | bytes 100
  0.6 13.0 %copy-start.2 = (s32[8]{0:T(128)S(1)}, s32[8]{0:T(128)}, u32[]{:S(2)}) copy-start(s32[8]{0:T(128)} %starts_ref.3) | copy-start | bytes 100
  0.7 13.0 %copy-start.1 = (s32[8]{0:T(128)S(1)}, s32[8]{0:T(128)}, u32[]{:S(2)}) copy-start(s32[8]{0:T(128)} %counts_ref.3) | copy-start | bytes 100
  1.8 5.6 %collective-permute-start.7 = (bf16[16,6272]{1,0:T(8,128)(2,1)S(1)}, bf16[16,6272]{1,0:T(8,128)(2,1)S(1)}, u32[]{:S(2)}, u32[]{:S(2)}) collective-permute-start(bf16[16,6272]{1,0:T(8,128)(2,1)S(1)} %shard_map.148.refs_0_), channel_id=1, source_target_pairs={{0,4},{1,3},{2,0},{3,7},{4,8},{5,1},{6,2},{7,11},{8,12},{9,5},{10,... | collective-permute-start | bytes 602120 | tf_op jit(solution)/shard_map/ppermute | solution.py:401
  4.9 5.8 %collective-permute-start = (bf16[16,6272]{1,0:T(8,128)(2,1)S(1)}, bf16[16,6272]{1,0:T(8,128)(2,1)S(1)}, u32[]{:S(2)}, u32[]{:S(2)}) collective-permute-start(bf16[16,6272]{1,0:T(8,128)(2,1)S(1)} %shard_map.147.after.refs_0_), channel_id=1, source_target_pairs={{0,4},{1,3},{2,0},{3,7},{4,8},{5,1},{6,2},{7,11},{8,12},{9,5},{10,... | collective-permute-start | bytes 602120 | tf_op jit(solution)/shard_map/ppermute | solution.py:401
  7.4 4.9 %collective-permute-start.8 = (bf16[16,6272]{1,0:T(8,128)(2,1)S(1)}, bf16[16,6272]{1,0:T(8,128)(2,1)S(1)}, u32[]{:S(2)}, u32[]{:S(2)}) collective-permute-start(bf16[16,6272]{1,0:T(8,128)(2,1)S(1)} %collective-permute-done.7.after.refs_1_), channel_id=1, source_target_pairs={{0,4},{1,3},{2,0},{3,7},{4,8},{5,1},{6,2},{7,11},{8,12},{9,5},{10,... | collective-permute-start | bytes 602120 | tf_op jit(solution)/shard_map/ppermute | solution.py:401
  8.8 13.3 %collective-permute-start.10 = (bf16[16,6272]{1,0:T(8,128)(2,1)S(1)}, bf16[16,6272]{1,0:T(8,128)(2,1)S(1)}, u32[]{:S(2)}, u32[]{:S(2)}) collective-permute-start(bf16[16,6272]{1,0:T(8,128)(2,1)S(1)} %collective-permute-done.7.after.refs_1_), channel_id=1, source_target_pairs={{0,1},{1,0},{2,3},{3,2},{4,5},{5,4},{6,7},{7,6},{8,9},{9,8},{10,11... | collective-permute-start | bytes 602120 | tf_op jit(solution)/shard_map/ppermute | solution.py:404
  10.7 6.5 %collective-permute-start.1 = (bf16[16,6272]{1,0:T(8,128)(2,1)S(1)}, bf16[16,6272]{1,0:T(8,128)(2,1)S(1)}, u32[]{:S(2)}, u32[]{:S(2)}) collective-permute-start(bf16[16,6272]{1,0:T(8,128)(2,1)S(1)} %collective-permute-done.refs_1_), channel_id=1, source_target_pairs={{0,4},{1,3},{2,0},{3,7},{4,8},{5,1},{6,2},{7,11},{8,12},{9,5},{10,... | collective-permute-start | bytes 602120 | tf_op jit(solution)/shard_map/ppermute | solution.py:401
  12.2 5.5 %collective-permute-start.9 = (bf16[16,6272]{1,0:T(8,128)(2,1)S(1)}, bf16[16,6272]{1,0:T(8,128)(2,1)S(1)}, u32[]{:S(2)}, u32[]{:S(2)}) collective-permute-start(bf16[16,6272]{1,0:T(8,128)(2,1)S(1)} %collective-permute-done.8.after.refs_2_), channel_id=1, source_target_pairs={{0,4},{1,3},{2,0},{3,7},{4,8},{5,1},{6,2},{7,11},{8,12},{9,5},{10,... | collective-permute-start | bytes 602120 | tf_op jit(solution)/shard_map/ppermute | solution.py:401
  13.6 12.1 %slice-start.4 = ((s8[8388608]{0:T(1024)(128)(4,1)}), s8[4194304]{0:T(1024)(128)(4,1)S(1)}, s32[]{:S(2)}) async-start(s8[8388608]{0:T(1024)(128)(4,1)} %bitcast.8), calls=%async_computation.4 | async-start | bytes 8388608
  14.4 11.3 %slice-start.5 = ((s8[8388608]{0:T(1024)(128)(4,1)}), s8[4194304]{0:T(1024)(128)(4,1)S(1)}, s32[]{:S(2)}) async-start(s8[8388608]{0:T(1024)(128)(4,1)} %bitcast.8), calls=%async_computation.5 | async-start | bytes 8388608
  14.4 7.8 %collective-permute-start.11 = (bf16[16,6272]{1,0:T(8,128)(2,1)S(1)}, bf16[16,6272]{1,0:T(8,128)(2,1)S(1)}, u32[]{:S(2)}, u32[]{:S(2)}) collective-permute-start(bf16[16,6272]{1,0:T(8,128)(2,1)S(1)} %collective-permute-done.8.after.refs_2_), channel_id=1, source_target_pairs={{0,1},{1,0},{2,3},{3,2},{4,5},{5,4},{6,7},{7,6},{8,9},{9,8},{10,11... | collective-permute-start | bytes 602120 | tf_op jit(solution)/shard_map/ppermute | solution.py:404
  17.2 5.5 %collective-permute-start.2 = (bf16[16,6272]{1,0:T(8,128)(2,1)S(1)}, bf16[16,6272]{1,0:T(8,128)(2,1)S(1)}, u32[]{:S(2)}, u32[]{:S(2)}) collective-permute-start(bf16[16,6272]{1,0:T(8,128)(2,1)S(1)} %collective-permute-done.1.refs_2_), channel_id=1, source_target_pairs={{0,4},{1,3},{2,0},{3,7},{4,8},{5,1},{6,2},{7,11},{8,12},{9,5},{10,... | collective-permute-start | bytes 602120 | tf_op jit(solution)/shard_map/ppermute | solution.py:401
  17.7 6.5 %collective-permute-start.13 = (bf16[16,6272]{1,0:T(8,128)(2,1)S(1)}, bf16[16,6272]{1,0:T(8,128)(2,1)S(1)}, u32[]{:S(2)}, u32[]{:S(2)}) collective-permute-start(bf16[16,6272]{1,0:T(8,128)(2,1)S(1)} %collective-permute-done.9.refs_3_), channel_id=1, source_target_pairs={{0,4},{1,3},{2,0},{3,7},{4,8},{5,1},{6,2},{7,11},{8,12},{9,5},{10,... | collective-permute-start | bytes 602120 | tf_op jit(solution)/shard_map/ppermute | solution.py:401
  18.6 7.1 %collective-permute-start.12 = (bf16[16,6272]{1,0:T(8,128)(2,1)S(1)}, bf16[16,6272]{1,0:T(8,128)(2,1)S(1)}, u32[]{:S(2)}, u32[]{:S(2)}) collective-permute-start(bf16[16,6272]{1,0:T(8,128)(2,1)S(1)} %collective-permute-done.9.refs_3_), channel_id=1, source_target_pairs={{0,1},{1,0},{2,3},{3,2},{4,5},{5,4},{6,7},{7,6},{8,9},{9,8},{10,11... | collective-permute-start | bytes 602120 | tf_op jit(solution)/shard_map/ppermute | solution.py:404
  22.1 6.6 %slice-start.3 = ((s8[8388608]{0:T(1024)(128)(4,1)}), s8[4194304]{0:T(1024)(128)(4,1)S(1)}, s32[]{:S(2)}) async-start(s8[8388608]{0:T(1024)(128)(4,1)} %bitcast.5), calls=%async_computation.3 | async-start | bytes 8388608
  22.1 6.5 %collective-permute-start.3 = (bf16[16,6272]{1,0:T(8,128)(2,1)S(1)}, bf16[16,6272]{1,0:T(8,128)(2,1)S(1)}, u32[]{:S(2)}, u32[]{:S(2)}) collective-permute-start(bf16[16,6272]{1,0:T(8,128)(2,1)S(1)} %collective-permute-done.refs_1_), channel_id=1, source_target_pairs={{0,1},{1,0},{2,3},{3,2},{4,5},{5,4},{6,7},{7,6},{8,9},{9,8},{10,11... | collective-permute-start | bytes 602120 | tf_op jit(solution)/shard_map/ppermute | solution.py:404
  22.2 6.4 %collective-permute-start.4 = (bf16[16,6272]{1,0:T(8,128)(2,1)S(1)}, bf16[16,6272]{1,0:T(8,128)(2,1)S(1)}, u32[]{:S(2)}, u32[]{:S(2)}) collective-permute-start(bf16[16,6272]{1,0:T(8,128)(2,1)S(1)} %collective-permute-done.1.refs_2_), channel_id=1, source_target_pairs={{0,1},{1,0},{2,3},{3,2},{4,5},{5,4},{6,7},{7,6},{8,9},{9,8},{10,11... | collective-permute-start | bytes 602120 | tf_op jit(solution)/shard_map/ppermute | solution.py:404
  22.7 5.9 %collective-permute-start.6 = (bf16[16,6272]{1,0:T(8,128)(2,1)S(1)}, bf16[16,6272]{1,0:T(8,128)(2,1)S(1)}, u32[]{:S(2)}, u32[]{:S(2)}) collective-permute-start(bf16[16,6272]{1,0:T(8,128)(2,1)S(1)} %collective-permute-done.2.refs_3_), channel_id=1, source_target_pairs={{0,4},{1,3},{2,0},{3,7},{4,8},{5,1},{6,2},{7,11},{8,12},{9,5},{10,... | collective-permute-start | bytes 602120 | tf_op jit(solution)/shard_map/ppermute | solution.py:401
  24.2 4.4 %collective-permute-start.5 = (bf16[16,6272]{1,0:T(8,128)(2,1)S(1)}, bf16[16,6272]{1,0:T(8,128)(2,1)S(1)}, u32[]{:S(2)}, u32[]{:S(2)}) collective-permute-start(bf16[16,6272]{1,0:T(8,128)(2,1)S(1)} %collective-permute-done.2.refs_3_), channel_id=1, source_target_pairs={{0,1},{1,0},{2,3},{3,2},{4,5},{5,4},{6,7},{7,6},{8,9},{9,8},{10,11... | collective-permute-start | bytes 602120 | tf_op jit(solution)/shard_map/ppermute | solution.py:404
  36.5 5.1 %collective-permute-start.15 = (bf16[48,4096]{1,0:T(8,128)(2,1)S(1)}, bf16[48,4096]{1,0:T(8,128)(2,1)S(1)}, u32[]{:S(2)}, u32[]{:S(2)}) collective-permute-start(bf16[48,4096]{1,0:T(8,128)(2,1)S(1)} %slice.50), channel_id=1, source_target_pairs={{0,1},{1,0},{2,3},{3,2},{4,5},{5,4},{6,7},{7,6},{8,9},{9,8},{10,11... | collective-permute-start | bytes 1179656 | tf_op jit(solution)/shard_map/ppermute | solution.py:404
  36.7 4.9 %collective-permute-start.14 = (bf16[16,4096]{1,0:T(8,128)(2,1)S(1)}, bf16[16,4096]{1,0:T(8,128)(2,1)S(1)}, u32[]{:S(2)}, u32[]{:S(2)}) collective-permute-start(bf16[16,4096]{1,0:T(8,128)(2,1)S(1)} %slice.48), channel_id=1, source_target_pairs={{0,4},{1,3},{2,0},{3,7},{4,8},{5,1},{6,2},{7,11},{8,12},{9,5},{10,... | collective-permute-start | bytes 393224 | tf_op jit(solution)/shard_map/ppermute | solution.py:401
  39.1 4.2 %collective-permute-start.20 = (bf16[16,4224]{1,0:T(8,128)(2,1)S(1)}, bf16[16,4224]{1,0:T(8,128)(2,1)S(1)}, u32[]{:S(2)}, u32[]{:S(2)}) collective-permute-start(bf16[16,4224]{1,0:T(8,128)(2,1)S(1)} %slice.56), channel_id=1, source_target_pairs={{0,4},{1,3},{2,0},{3,7},{4,8},{5,1},{6,2},{7,11},{8,12},{9,5},{10,... | collective-permute-start | bytes 405512 | tf_op jit(solution)/shard_map/ppermute | solution.py:401
  40.4 2.9 %collective-permute-start.21 = (bf16[48,4224]{1,0:T(8,128)(2,1)S(1)}, bf16[48,4224]{1,0:T(8,128)(2,1)S(1)}, u32[]{:S(2)}, u32[]{:S(2)}) collective-permute-start(bf16[48,4224]{1,0:T(8,128)(2,1)S(1)} %slice.58), channel_id=1, source_target_pairs={{0,1},{1,0},{2,3},{3,2},{4,5},{5,4},{6,7},{7,6},{8,9},{9,8},{10,11... | collective-permute-start | bytes 1216520 | tf_op jit(solution)/shard_map/ppermute | solution.py:404
  41.6 4.2 %collective-permute-start.16 = (bf16[16,4096]{1,0:T(8,128)(2,1)S(1)}, bf16[16,4096]{1,0:T(8,128)(2,1)S(1)}, u32[]{:S(2)}, u32[]{:S(2)}) collective-permute-start(bf16[16,4096]{1,0:T(8,128)(2,1)S(1)} %add_convert_fusion.5), channel_id=1, source_target_pairs={{0,4},{1,3},{2,0},{3,7},{4,8},{5,1},{6,2},{7,11},{8,12},{9,5},{10,... | collective-permute-start | bytes 393224 | tf_op jit(solution)/shard_map/ppermute | solution.py:401
  43.4 3.9 %collective-permute-start.22 = (bf16[16,4224]{1,0:T(8,128)(2,1)S(1)}, bf16[16,4224]{1,0:T(8,128)(2,1)S(1)}, u32[]{:S(2)}, u32[]{:S(2)}) collective-permute-start(bf16[16,4224]{1,0:T(8,128)(2,1)S(1)} %add_convert_fusion.2), channel_id=1, source_target_pairs={{0,4},{1,3},{2,0},{3,7},{4,8},{5,1},{6,2},{7,11},{8,12},{9,5},{10,... | collective-permute-start | bytes 405512 | tf_op jit(solution)/shard_map/ppermute | solution.py:401
  45.8 3.9 %collective-permute-start.17 = (bf16[16,4096]{1,0:T(8,128)(2,1)S(1)}, bf16[16,4096]{1,0:T(8,128)(2,1)S(1)}, u32[]{:S(2)}, u32[]{:S(2)}) collective-permute-start(bf16[16,4096]{1,0:T(8,128)(2,1)S(1)} %add_convert_fusion.4), channel_id=1, source_target_pairs={{0,4},{1,3},{2,0},{3,7},{4,8},{5,1},{6,2},{7,11},{8,12},{9,5},{10,... | collective-permute-start | bytes 393224 | tf_op jit(solution)/shard_map/ppermute | solution.py:401
  47.3 4.2 %collective-permute-start.23 = (bf16[16,4224]{1,0:T(8,128)(2,1)S(1)}, bf16[16,4224]{1,0:T(8,128)(2,1)S(1)}, u32[]{:S(2)}, u32[]{:S(2)}) collective-permute-start(bf16[16,4224]{1,0:T(8,128)(2,1)S(1)} %add_convert_fusion.1), channel_id=1, source_target_pairs={{0,4},{1,3},{2,0},{3,7},{4,8},{5,1},{6,2},{7,11},{8,12},{9,5},{10,... | collective-permute-start | bytes 405512 | tf_op jit(solution)/shard_map/ppermute | solution.py:401
  49.8 4.2 %collective-permute-start.18 = (bf16[16,4096]{1,0:T(8,128)(2,1)S(1)}, bf16[16,4096]{1,0:T(8,128)(2,1)S(1)}, u32[]{:S(2)}, u32[]{:S(2)}) collective-permute-start(bf16[16,4096]{1,0:T(8,128)(2,1)S(1)} %add_convert_fusion.3), channel_id=1, source_target_pairs={{0,4},{1,3},{2,0},{3,7},{4,8},{5,1},{6,2},{7,11},{8,12},{9,5},{10,... | collective-permute-start | bytes 393224 | tf_op jit(solution)/shard_map/ppermute | solution.py:401
  51.6 7.5 %collective-permute-start.24 = (bf16[16,4224]{1,0:T(8,128)(2,1)S(1)}, bf16[16,4224]{1,0:T(8,128)(2,1)S(1)}, u32[]{:S(2)}, u32[]{:S(2)}) collective-permute-start(bf16[16,4224]{1,0:T(8,128)(2,1)S(1)} %add_convert_fusion), channel_id=1, source_target_pairs={{0,4},{1,3},{2,0},{3,7},{4,8},{5,1},{6,2},{7,11},{8,12},{9,5},{10,... | collective-permute-start | bytes 405512 | tf_op jit(solution)/shard_map/ppermute | solution.py:401
  54.0 6.5 %collective-permute-start.19 = (f32[16,4096]{1,0:T(8,128)S(1)}, f32[16,4096]{1,0:T(8,128)S(1)}, u32[]{:S(2)}, u32[]{:S(2)}) collective-permute-start(f32[16,4096]{1,0:T(8,128)S(1)} %convert_add_fusion.1.mine_ref), channel_id=1, source_target_pairs={{0,1},{1,0},{2,3},{3,2},{4,5},{5,4},{6,7},{7,6},{8,9},{9,8},{10,11... | collective-permute-start | bytes 786440 | tf_op jit(solution)/shard_map/ppermute | solution.py:404
  59.1 3.3 %collective-permute-start.25 = (f32[16,4224]{1,0:T(8,128)S(1)}, f32[16,4224]{1,0:T(8,128)S(1)}, u32[]{:S(2)}, u32[]{:S(2)}) collective-permute-start(f32[16,4224]{1,0:T(8,128)S(1)} %convert_add_fusion.mine_ref), channel_id=1, source_target_pairs={{0,1},{1,0},{2,3},{3,2},{4,5},{5,4},{6,7},{7,6},{8,9},{9,8},{10,11... | collective-permute-start | bytes 811016 | tf_op jit(solution)/shard_map/ppermute | solution.py:404
  (4 other events, 26.4 us)

commit v6 on v5

--- a/solution.py
+++ b/solution.py
@@ -494,7 +494,7 @@
             limit=n,
         )
         own, sent, scaled, rows, tables, middle, coeffs, pulled, stats = call(
-            functools.partial(hidden_kernel, n, 1024),
+            functools.partial(hidden_kernel, n, 2048),
             [
                 ((SEG, width), F32),
                 ((rows_total - SEG, width), BF),

time: 63.3 us -> 63 us (level)
  no operation moved by 1% of the time
where the time goes in v6:
time: 63 us; the launch traced here: 62.8 us
  starting transfers between devices  33.8 us (54%)
  Pallas kernels  18.1 us (29%)
  waiting for transfers between devices  9.45 us (15%)
  between operations  0.94 us (1%)
    pallas_call x11, Pallas kernels, call(): pl.pallas_call(kernel, out_shape=tuple((jax.ShapeDtypeStruct(s, d) for s,...  18.1 us
    ppermute x16, starting transfers between devices, hop(): return lax.ppermute(x, ('dp', 'tensor'), pairs)  17.5 us
    ppermute x10, starting transfers between devices, swap(): return lax.ppermute(x, 'tensor', [(0, 1), (1, 0)])  16.3 us
    ppermute x16, waiting for transfers between devices, hop(): return lax.ppermute(x, ('dp', 'tensor'), pairs)  9.42 us
  transfers between devices with their start and end apart: 26, of which 10 were waited for; matrix products, arithmetic and copies ran while one was open for 1% of the time, Pallas kernels for 14%

profile of v6, /device:TPU:1, one launch (start us, length us, event | category | flops | bytes accessed | tf_op | source)
XLA Modules:
  0.0 62.8 jit_solution(2177097026214464326)
XLA Ops:
  0.7 1.1 %shard_map.148.refs_0_ = bf16[16,6272]{1,0:T(8,128)(2,1)S(1)} custom-call(bf16[16,4096]{1,0:T(8,128)(2,1)} %upstream_hbm.1, bf16[1,8,4096]{2,1,0:T(8,128)(2,1)} %basis_hbm.3, bf16[1,8,4096]{2,1,0:T(8,128)(2,1)} %learned_hbm.3, bf16[1,8]{1,0:T(2,128)(2,1)} %bias_hbm.1), custom_call_target="tpu_custom_call" | custom-call | bytes 540672 | tf_op jit(solution)/shard_map/pallas_call | solution.py:363
  1.8 2.1 %collective-permute-start.7 = (bf16[16,6272]{1,0:T(8,128)(2,1)S(1)}, bf16[16,6272]{1,0:T(8,128)(2,1)S(1)}, u32[]{:S(2)}, u32[]{:S(2)}) collective-permute-start(bf16[16,6272]{1,0:T(8,128)(2,1)S(1)} %shard_map.148.refs_0_), channel_id=1, source_target_pairs={{0,4},{1,3},{2,0},{3,7},{4,8},{5,1},{6,2},{7,11},{8,12},{9,5},{10,... | collective-permute-start | bytes 602120 | tf_op jit(solution)/shard_map/ppermute | solution.py:401
  3.9 1.0 %shard_map.147.after.refs_0_ = bf16[16,6272]{1,0:T(8,128)(2,1)S(1)} custom-call(bf16[16,4096]{1,0:T(8,128)(2,1)} %hidden_hbm.1, bf16[1,8,4096]{2,1,0:T(8,128)(2,1)} %basis_hbm.3, bf16[1,8,4096]{2,1,0:T(8,128)(2,1)} %learned_hbm.3), custom_call_target="tpu_custom_call" | custom-call | bytes 540672 | tf_op jit(solution)/shard_map/pallas_call | solution.py:363
  4.9 1.3 %collective-permute-start = (bf16[16,6272]{1,0:T(8,128)(2,1)S(1)}, bf16[16,6272]{1,0:T(8,128)(2,1)S(1)}, u32[]{:S(2)}, u32[]{:S(2)}) collective-permute-start(bf16[16,6272]{1,0:T(8,128)(2,1)S(1)} %shard_map.147.after.refs_0_), channel_id=1, source_target_pairs={{0,4},{1,3},{2,0},{3,7},{4,8},{5,1},{6,2},{7,11},{8,12},{9,5},{10,... | collective-permute-start | bytes 602120 | tf_op jit(solution)/shard_map/ppermute | solution.py:401
  6.2 1.1 %collective-permute-done.7.after.refs_1_ = bf16[16,6272]{1,0:T(8,128)(2,1)S(1)} collective-permute-done((bf16[16,6272]{1,0:T(8,128)(2,1)S(1)}, bf16[16,6272]{1,0:T(8,128)(2,1)S(1)}, u32[]{:S(2)}, u32[]{:S(2)}) %collective-permute-start.7) | collective-permute-done | bytes 200736 | tf_op jit(solution)/shard_map/ppermute | solution.py:401
  7.4 1.4 %collective-permute-start.8 = (bf16[16,6272]{1,0:T(8,128)(2,1)S(1)}, bf16[16,6272]{1,0:T(8,128)(2,1)S(1)}, u32[]{:S(2)}, u32[]{:S(2)}) collective-permute-start(bf16[16,6272]{1,0:T(8,128)(2,1)S(1)} %collective-permute-done.7.after.refs_1_), channel_id=1, source_target_pairs={{0,4},{1,3},{2,0},{3,7},{4,8},{5,1},{6,2},{7,11},{8,12},{9,5},{10,... | collective-permute-start | bytes 602120 | tf_op jit(solution)/shard_map/ppermute | solution.py:401
  8.8 1.9 %collective-permute-start.10 = (bf16[16,6272]{1,0:T(8,128)(2,1)S(1)}, bf16[16,6272]{1,0:T(8,128)(2,1)S(1)}, u32[]{:S(2)}, u32[]{:S(2)}) collective-permute-start(bf16[16,6272]{1,0:T(8,128)(2,1)S(1)} %collective-permute-done.7.after.refs_1_), channel_id=1, source_target_pairs={{0,1},{1,0},{2,3},{3,2},{4,5},{5,4},{6,7},{7,6},{8,9},{9,8},{10,11... | collective-permute-start | bytes 602120 | tf_op jit(solution)/shard_map/ppermute | solution.py:404
  11.1 1.1 %collective-permute-done.8.after.refs_2_ = bf16[16,6272]{1,0:T(8,128)(2,1)S(1)} collective-permute-done((bf16[16,6272]{1,0:T(8,128)(2,1)S(1)}, bf16[16,6272]{1,0:T(8,128)(2,1)S(1)}, u32[]{:S(2)}, u32[]{:S(2)}) %collective-permute-start.8) | collective-permute-done | bytes 200736 | tf_op jit(solution)/shard_map/ppermute | solution.py:401
  12.2 1.4 %collective-permute-start.9 = (bf16[16,6272]{1,0:T(8,128)(2,1)S(1)}, bf16[16,6272]{1,0:T(8,128)(2,1)S(1)}, u32[]{:S(2)}, u32[]{:S(2)}) collective-permute-start(bf16[16,6272]{1,0:T(8,128)(2,1)S(1)} %collective-permute-done.8.after.refs_2_), channel_id=1, source_target_pairs={{0,4},{1,3},{2,0},{3,7},{4,8},{5,1},{6,2},{7,11},{8,12},{9,5},{10,... | collective-permute-start | bytes 602120 | tf_op jit(solution)/shard_map/ppermute | solution.py:401
  13.6 0.7 %shard_map.149.refs_8_.mask_ref = f32[128,128]{1,0:T(8,128)S(1)} custom-call(s32[2]{0:T(128)S(1)} %pad_add_fusion.where_ref, s32[8]{0:T(128)S(1)} %copy-done.1, s32[8]{0:T(128)S(1)} %copy-done.2, s32[8]{0:T(128)S(1)} %copy-done.3, bf16[16,6272]{1,0:T(8,128)(2,1)S(1)} %collective-permute-done.7.after.refs_1_), custom_call_target="tpu_custom_call" | custom-call | flops 4000000000 | tf_op jit(solution)/shard_map/pallas_call | solution.py:363
  14.4 2.8 %collective-permute-start.11 = (bf16[16,6272]{1,0:T(8,128)(2,1)S(1)}, bf16[16,6272]{1,0:T(8,128)(2,1)S(1)}, u32[]{:S(2)}, u32[]{:S(2)}) collective-permute-start(bf16[16,6272]{1,0:T(8,128)(2,1)S(1)} %collective-permute-done.8.after.refs_2_), channel_id=1, source_target_pairs={{0,1},{1,0},{2,3},{3,2},{4,5},{5,4},{6,7},{7,6},{8,9},{9,8},{10,11... | collective-permute-start | bytes 602120 | tf_op jit(solution)/shard_map/ppermute | solution.py:404
  17.7 0.9 %collective-permute-start.13 = (bf16[16,6272]{1,0:T(8,128)(2,1)S(1)}, bf16[16,6272]{1,0:T(8,128)(2,1)S(1)}, u32[]{:S(2)}, u32[]{:S(2)}) collective-permute-start(bf16[16,6272]{1,0:T(8,128)(2,1)S(1)} %collective-permute-done.9.refs_3_), channel_id=1, source_target_pairs={{0,4},{1,3},{2,0},{3,7},{4,8},{5,1},{6,2},{7,11},{8,12},{9,5},{10,... | collective-permute-start | bytes 602120 | tf_op jit(solution)/shard_map/ppermute | solution.py:401
  18.6 3.4 %collective-permute-start.12 = (bf16[16,6272]{1,0:T(8,128)(2,1)S(1)}, bf16[16,6272]{1,0:T(8,128)(2,1)S(1)}, u32[]{:S(2)}, u32[]{:S(2)}) collective-permute-start(bf16[16,6272]{1,0:T(8,128)(2,1)S(1)} %collective-permute-done.9.refs_3_), channel_id=1, source_target_pairs={{0,1},{1,0},{2,3},{3,2},{4,5},{5,4},{6,7},{7,6},{8,9},{9,8},{10,11... | collective-permute-start | bytes 602120 | tf_op jit(solution)/shard_map/ppermute | solution.py:404
  22.7 1.5 %collective-permute-done.13.refs_7_ = bf16[16,6272]{1,0:T(8,128)(2,1)S(1)} collective-permute-done((bf16[16,6272]{1,0:T(8,128)(2,1)S(1)}, bf16[16,6272]{1,0:T(8,128)(2,1)S(1)}, u32[]{:S(2)}, u32[]{:S(2)}) %collective-permute-start.13) | collective-permute-done | bytes 200736 | tf_op jit(solution)/shard_map/ppermute | solution.py:401
  24.2 1.5 %collective-permute-start.5 = (bf16[16,6272]{1,0:T(8,128)(2,1)S(1)}, bf16[16,6272]{1,0:T(8,128)(2,1)S(1)}, u32[]{:S(2)}, u32[]{:S(2)}) collective-permute-start(bf16[16,6272]{1,0:T(8,128)(2,1)S(1)} %collective-permute-done.2.refs_3_), channel_id=1, source_target_pairs={{0,1},{1,0},{2,3},{3,2},{4,5},{5,4},{6,7},{7,6},{8,9},{9,8},{10,11... | collective-permute-start | bytes 602120 | tf_op jit(solution)/shard_map/ppermute | solution.py:404
  25.7 2.9 %shard_map.152 = (bf16[128,4096]{1,0:T(8,128)(2,1)S(1)}, bf16[128,2176]{1,0:T(8,128)(2,1)S(1)}, f32[128,1024]{1,0:T(8,128)S(1)}) custom-call(bf16[16,6272]{1,0:T(8,128)(2,1)S(1)} %shard_map.148.refs_0_, bf16[16,6272]{1,0:T(8,128)(2,1)S(1)} %collective-permute-done.7.after.refs_1_, bf16[16,6272]{1,0:T(8,128)(2,1)S(1)} %collective-permute-done.8.after.refs_2_, ...), custom_call_target="tpu_custom_call" | custom-call | flops 40000000000 | bytes 8388608 | tf_op jit(solution)/shard_map/pallas_call | solution.py:363
  28.7 7.4 %shard_map.153 = (f32[16,4096]{1,0:T(8,128)S(1)}, bf16[112,4096]{1,0:T(8,128)(2,1)S(1)}, f32[128,4096]{1,0:T(8,128)S(1)}, bf16[128,4224]{1,0:T(8,128)(2,1)S(1)},...) custom-call(bf16[16,6272]{1,0:T(8,128)(2,1)S(1)} %shard_map.147.afte, ...), custom_call_target="tpu_custom_call" | custom-call | flops 4294967296 | bytes 16777216 | tf_op jit(solution)/shard_map/pallas_call | solution.py:363
  36.4 1.7 %collective-permute-start.14 = (bf16[16,4096]{1,0:T(8,128)(2,1)S(1)}, bf16[16,4096]{1,0:T(8,128)(2,1)S(1)}, u32[]{:S(2)}, u32[]{:S(2)}) collective-permute-start(bf16[16,4096]{1,0:T(8,128)(2,1)S(1)} %slice.48), channel_id=1, source_target_pairs={{0,4},{1,3},{2,0},{3,7},{4,8},{5,1},{6,2},{7,11},{8,12},{9,5},{10,... | collective-permute-start | bytes 393224 | tf_op jit(solution)/shard_map/ppermute | solution.py:401
  38.8 1.3 %collective-permute-start.20 = (bf16[16,4224]{1,0:T(8,128)(2,1)S(1)}, bf16[16,4224]{1,0:T(8,128)(2,1)S(1)}, u32[]{:S(2)}, u32[]{:S(2)}) collective-permute-start(bf16[16,4224]{1,0:T(8,128)(2,1)S(1)} %slice.56), channel_id=1, source_target_pairs={{0,4},{1,3},{2,0},{3,7},{4,8},{5,1},{6,2},{7,11},{8,12},{9,5},{10,... | collective-permute-start | bytes 405512 | tf_op jit(solution)/shard_map/ppermute | solution.py:401
  40.1 1.1 %collective-permute-start.21 = (bf16[48,4224]{1,0:T(8,128)(2,1)S(1)}, bf16[48,4224]{1,0:T(8,128)(2,1)S(1)}, u32[]{:S(2)}, u32[]{:S(2)}) collective-permute-start(bf16[48,4224]{1,0:T(8,128)(2,1)S(1)} %slice.58), channel_id=1, source_target_pairs={{0,1},{1,0},{2,3},{3,2},{4,5},{5,4},{6,7},{7,6},{8,9},{9,8},{10,11... | collective-permute-start | bytes 1216520 | tf_op jit(solution)/shard_map/ppermute | solution.py:404
  41.3 1.0 %collective-permute-start.16 = (bf16[16,4096]{1,0:T(8,128)(2,1)S(1)}, bf16[16,4096]{1,0:T(8,128)(2,1)S(1)}, u32[]{:S(2)}, u32[]{:S(2)}) collective-permute-start(bf16[16,4096]{1,0:T(8,128)(2,1)S(1)} %add_convert_fusion.5), channel_id=1, source_target_pairs={{0,4},{1,3},{2,0},{3,7},{4,8},{5,1},{6,2},{7,11},{8,12},{9,5},{10,... | collective-permute-start | bytes 393224 | tf_op jit(solution)/shard_map/ppermute | solution.py:401
  43.1 1.3 %collective-permute-start.22 = (bf16[16,4224]{1,0:T(8,128)(2,1)S(1)}, bf16[16,4224]{1,0:T(8,128)(2,1)S(1)}, u32[]{:S(2)}, u32[]{:S(2)}) collective-permute-start(bf16[16,4224]{1,0:T(8,128)(2,1)S(1)} %add_convert_fusion.2), channel_id=1, source_target_pairs={{0,4},{1,3},{2,0},{3,7},{4,8},{5,1},{6,2},{7,11},{8,12},{9,5},{10,... | collective-permute-start | bytes 405512 | tf_op jit(solution)/shard_map/ppermute | solution.py:401
  44.4 1.1 %collective-permute-done.16 = bf16[16,4096]{1,0:T(8,128)(2,1)S(1)} collective-permute-done((bf16[16,4096]{1,0:T(8,128)(2,1)S(1)}, bf16[16,4096]{1,0:T(8,128)(2,1)S(1)}, u32[]{:S(2)}, u32[]{:S(2)}) %collective-permute-start.16) | collective-permute-done | bytes 131104 | tf_op jit(solution)/shard_map/ppermute | solution.py:401
  46.2 0.8 %collective-permute-done.22 = bf16[16,4224]{1,0:T(8,128)(2,1)S(1)} collective-permute-done((bf16[16,4224]{1,0:T(8,128)(2,1)S(1)}, bf16[16,4224]{1,0:T(8,128)(2,1)S(1)}, u32[]{:S(2)}, u32[]{:S(2)}) %collective-permute-start.22) | collective-permute-done | bytes 135200 | tf_op jit(solution)/shard_map/ppermute | solution.py:401
  47.0 1.6 %collective-permute-start.23 = (bf16[16,4224]{1,0:T(8,128)(2,1)S(1)}, bf16[16,4224]{1,0:T(8,128)(2,1)S(1)}, u32[]{:S(2)}, u32[]{:S(2)}) collective-permute-start(bf16[16,4224]{1,0:T(8,128)(2,1)S(1)} %add_convert_fusion.1), channel_id=1, source_target_pairs={{0,4},{1,3},{2,0},{3,7},{4,8},{5,1},{6,2},{7,11},{8,12},{9,5},{10,... | collective-permute-start | bytes 405512 | tf_op jit(solution)/shard_map/ppermute | solution.py:401
  48.7 0.7 %collective-permute-done.17 = bf16[16,4096]{1,0:T(8,128)(2,1)S(1)} collective-permute-done((bf16[16,4096]{1,0:T(8,128)(2,1)S(1)}, bf16[16,4096]{1,0:T(8,128)(2,1)S(1)}, u32[]{:S(2)}, u32[]{:S(2)}) %collective-permute-start.17) | collective-permute-done | bytes 131104 | tf_op jit(solution)/shard_map/ppermute | solution.py:401
  50.1 1.1 %collective-permute-done.23 = bf16[16,4224]{1,0:T(8,128)(2,1)S(1)} collective-permute-done((bf16[16,4224]{1,0:T(8,128)(2,1)S(1)}, bf16[16,4224]{1,0:T(8,128)(2,1)S(1)}, u32[]{:S(2)}, u32[]{:S(2)}) %collective-permute-start.23) | collective-permute-done | bytes 135200 | tf_op jit(solution)/shard_map/ppermute | solution.py:401
  51.3 1.6 %collective-permute-start.24 = (bf16[16,4224]{1,0:T(8,128)(2,1)S(1)}, bf16[16,4224]{1,0:T(8,128)(2,1)S(1)}, u32[]{:S(2)}, u32[]{:S(2)}) collective-permute-start(bf16[16,4224]{1,0:T(8,128)(2,1)S(1)} %add_convert_fusion), channel_id=1, source_target_pairs={{0,4},{1,3},{2,0},{3,7},{4,8},{5,1},{6,2},{7,11},{8,12},{9,5},{10,... | collective-permute-start | bytes 405512 | tf_op jit(solution)/shard_map/ppermute | solution.py:401
  53.7 3.4 %collective-permute-start.19 = (f32[16,4096]{1,0:T(8,128)S(1)}, f32[16,4096]{1,0:T(8,128)S(1)}, u32[]{:S(2)}, u32[]{:S(2)}) collective-permute-start(f32[16,4096]{1,0:T(8,128)S(1)} %convert_add_fusion.1.mine_ref), channel_id=1, source_target_pairs={{0,1},{1,0},{2,3},{3,2},{4,5},{5,4},{6,7},{7,6},{8,9},{9,8},{10,11... | collective-permute-start | bytes 786440 | tf_op jit(solution)/shard_map/ppermute | solution.py:404
  57.1 1.7 %shard_map.156.local_ref = f32[16,4224]{1,0:T(8,128)S(1)} custom-call(f32[128,128]{1,0:T(8,128)S(1)} %shard_map.149.refs_8_.mask_ref, bf16[128,4224]{1,0:T(8,128)(2,1)S(1)} %get-tuple-element.33.rows_ref, bf16[128,4224]{1,0:T(8,128)(2,1)S(1)} %get-tuple-element.30.tables_ref, bf16[128,4096]{1,0:T(8,128)(2,1)S(1)} %get-tuple-element.27.upstream_ref, ...), custom_call_target="tpu_custom_call" | custom-call | flops 1073741824 | bytes 5242880 | tf_op jit(solution)/shard_map/pallas_call | solution.py:363
  58.8 1.4 %collective-permute-start.25 = (f32[16,4224]{1,0:T(8,128)S(1)}, f32[16,4224]{1,0:T(8,128)S(1)}, u32[]{:S(2)}, u32[]{:S(2)}) collective-permute-start(f32[16,4224]{1,0:T(8,128)S(1)} %convert_add_fusion.mine_ref), channel_id=1, source_target_pairs={{0,1},{1,0},{2,3},{3,2},{4,5},{5,4},{6,7},{7,6},{8,9},{9,8},{10,11... | collective-permute-start | bytes 811016 | tf_op jit(solution)/shard_map/ppermute | solution.py:404
  60.2 1.9 %shard_map.154 = (bf16[16,4096]{1,0:T(8,128)(2,1)}, f32[8,128]{1,0:T(8,128)S(1)}) custom-call(s32[2]{0:T(128)S(1)} %pad_add_fusion.where_ref, s32[8]{0:T(128)S(1)} %copy-done.1, s32[8]{0:T(128)S(1)} %copy-done.2, s32[8]{0:T(128)S(1)} %copy-done.3, f32[16,4096]{1,0:T(8,128)S(1)} %convert_add_fusion.1.mine_ref, ...), custom_call_target="tpu_custom_call" | custom-call | flops 40000000000 | bytes 917504 | tf_op jit(solution)/shard_map/pallas_call | solution.py:363
  (67 shorter events, 6.4 us)
Async XLA Ops:
  0.6 13.0 %copy-start.3 = (s32[8]{0:T(128)S(1)}, s32[8]{0:T(128)}, u32[]{:S(2)}) copy-start(s32[8]{0:T(128)} %slots_ref.3) | copy-start | bytes 100
  0.6 13.0 %copy-start.2 = (s32[8]{0:T(128)S(1)}, s32[8]{0:T(128)}, u32[]{:S(2)}) copy-start(s32[8]{0:T(128)} %starts_ref.3) | copy-start | bytes 100
  0.7 13.0 %copy-start.1 = (s32[8]{0:T(128)S(1)}, s32[8]{0:T(128)}, u32[]{:S(2)}) copy-start(s32[8]{0:T(128)} %counts_ref.3) | copy-start | bytes 100
  1.8 5.6 %collective-permute-start.7 = (bf16[16,6272]{1,0:T(8,128)(2,1)S(1)}, bf16[16,6272]{1,0:T(8,128)(2,1)S(1)}, u32[]{:S(2)}, u32[]{:S(2)}) collective-permute-start(bf16[16,6272]{1,0:T(8,128)(2,1)S(1)} %shard_map.148.refs_0_), channel_id=1, source_target_pairs={{0,4},{1,3},{2,0},{3,7},{4,8},{5,1},{6,2},{7,11},{8,12},{9,5},{10,... | collective-permute-start | bytes 602120 | tf_op jit(solution)/shard_map/ppermute | solution.py:401
  4.9 5.8 %collective-permute-start = (bf16[16,6272]{1,0:T(8,128)(2,1)S(1)}, bf16[16,6272]{1,0:T(8,128)(2,1)S(1)}, u32[]{:S(2)}, u32[]{:S(2)}) collective-permute-start(bf16[16,6272]{1,0:T(8,128)(2,1)S(1)} %shard_map.147.after.refs_0_), channel_id=1, source_target_pairs={{0,4},{1,3},{2,0},{3,7},{4,8},{5,1},{6,2},{7,11},{8,12},{9,5},{10,... | collective-permute-start | bytes 602120 | tf_op jit(solution)/shard_map/ppermute | solution.py:401
  7.4 4.9 %collective-permute-start.8 = (bf16[16,6272]{1,0:T(8,128)(2,1)S(1)}, bf16[16,6272]{1,0:T(8,128)(2,1)S(1)}, u32[]{:S(2)}, u32[]{:S(2)}) collective-permute-start(bf16[16,6272]{1,0:T(8,128)(2,1)S(1)} %collective-permute-done.7.after.refs_1_), channel_id=1, source_target_pairs={{0,4},{1,3},{2,0},{3,7},{4,8},{5,1},{6,2},{7,11},{8,12},{9,5},{10,... | collective-permute-start | bytes 602120 | tf_op jit(solution)/shard_map/ppermute | solution.py:401
  8.8 13.3 %collective-permute-start.10 = (bf16[16,6272]{1,0:T(8,128)(2,1)S(1)}, bf16[16,6272]{1,0:T(8,128)(2,1)S(1)}, u32[]{:S(2)}, u32[]{:S(2)}) collective-permute-start(bf16[16,6272]{1,0:T(8,128)(2,1)S(1)} %collective-permute-done.7.after.refs_1_), channel_id=1, source_target_pairs={{0,1},{1,0},{2,3},{3,2},{4,5},{5,4},{6,7},{7,6},{8,9},{9,8},{10,11... | collective-permute-start | bytes 602120 | tf_op jit(solution)/shard_map/ppermute | solution.py:404
  10.7 6.5 %collective-permute-start.1 = (bf16[16,6272]{1,0:T(8,128)(2,1)S(1)}, bf16[16,6272]{1,0:T(8,128)(2,1)S(1)}, u32[]{:S(2)}, u32[]{:S(2)}) collective-permute-start(bf16[16,6272]{1,0:T(8,128)(2,1)S(1)} %collective-permute-done.refs_1_), channel_id=1, source_target_pairs={{0,4},{1,3},{2,0},{3,7},{4,8},{5,1},{6,2},{7,11},{8,12},{9,5},{10,... | collective-permute-start | bytes 602120 | tf_op jit(solution)/shard_map/ppermute | solution.py:401
  12.2 5.5 %collective-permute-start.9 = (bf16[16,6272]{1,0:T(8,128)(2,1)S(1)}, bf16[16,6272]{1,0:T(8,128)(2,1)S(1)}, u32[]{:S(2)}, u32[]{:S(2)}) collective-permute-start(bf16[16,6272]{1,0:T(8,128)(2,1)S(1)} %collective-permute-done.8.after.refs_2_), channel_id=1, source_target_pairs={{0,4},{1,3},{2,0},{3,7},{4,8},{5,1},{6,2},{7,11},{8,12},{9,5},{10,... | collective-permute-start | bytes 602120 | tf_op jit(solution)/shard_map/ppermute | solution.py:401
  13.6 12.1 %slice-start.4 = ((s8[8388608]{0:T(1024)(128)(4,1)}), s8[4194304]{0:T(1024)(128)(4,1)S(1)}, s32[]{:S(2)}) async-start(s8[8388608]{0:T(1024)(128)(4,1)} %bitcast.8), calls=%async_computation.4 | async-start | bytes 8388608
  14.4 11.3 %slice-start.5 = ((s8[8388608]{0:T(1024)(128)(4,1)}), s8[4194304]{0:T(1024)(128)(4,1)S(1)}, s32[]{:S(2)}) async-start(s8[8388608]{0:T(1024)(128)(4,1)} %bitcast.8), calls=%async_computation.5 | async-start | bytes 8388608
  14.4 7.8 %collective-permute-start.11 = (bf16[16,6272]{1,0:T(8,128)(2,1)S(1)}, bf16[16,6272]{1,0:T(8,128)(2,1)S(1)}, u32[]{:S(2)}, u32[]{:S(2)}) collective-permute-start(bf16[16,6272]{1,0:T(8,128)(2,1)S(1)} %collective-permute-done.8.after.refs_2_), channel_id=1, source_target_pairs={{0,1},{1,0},{2,3},{3,2},{4,5},{5,4},{6,7},{7,6},{8,9},{9,8},{10,11... | collective-permute-start | bytes 602120 | tf_op jit(solution)/shard_map/ppermute | solution.py:404
  17.2 5.5 %collective-permute-start.2 = (bf16[16,6272]{1,0:T(8,128)(2,1)S(1)}, bf16[16,6272]{1,0:T(8,128)(2,1)S(1)}, u32[]{:S(2)}, u32[]{:S(2)}) collective-permute-start(bf16[16,6272]{1,0:T(8,128)(2,1)S(1)} %collective-permute-done.1.refs_2_), channel_id=1, source_target_pairs={{0,4},{1,3},{2,0},{3,7},{4,8},{5,1},{6,2},{7,11},{8,12},{9,5},{10,... | collective-permute-start | bytes 602120 | tf_op jit(solution)/shard_map/ppermute | solution.py:401
  17.7 6.5 %collective-permute-start.13 = (bf16[16,6272]{1,0:T(8,128)(2,1)S(1)}, bf16[16,6272]{1,0:T(8,128)(2,1)S(1)}, u32[]{:S(2)}, u32[]{:S(2)}) collective-permute-start(bf16[16,6272]{1,0:T(8,128)(2,1)S(1)} %collective-permute-done.9.refs_3_), channel_id=1, source_target_pairs={{0,4},{1,3},{2,0},{3,7},{4,8},{5,1},{6,2},{7,11},{8,12},{9,5},{10,... | collective-permute-start | bytes 602120 | tf_op jit(solution)/shard_map/ppermute | solution.py:401
  18.6 7.1 %collective-permute-start.12 = (bf16[16,6272]{1,0:T(8,128)(2,1)S(1)}, bf16[16,6272]{1,0:T(8,128)(2,1)S(1)}, u32[]{:S(2)}, u32[]{:S(2)}) collective-permute-start(bf16[16,6272]{1,0:T(8,128)(2,1)S(1)} %collective-permute-done.9.refs_3_), channel_id=1, source_target_pairs={{0,1},{1,0},{2,3},{3,2},{4,5},{5,4},{6,7},{7,6},{8,9},{9,8},{10,11... | collective-permute-start | bytes 602120 | tf_op jit(solution)/shard_map/ppermute | solution.py:404
  22.1 6.6 %slice-start.3 = ((s8[8388608]{0:T(1024)(128)(4,1)}), s8[4194304]{0:T(1024)(128)(4,1)S(1)}, s32[]{:S(2)}) async-start(s8[8388608]{0:T(1024)(128)(4,1)} %bitcast.5), calls=%async_computation.3 | async-start | bytes 8388608
  22.1 6.5 %collective-permute-start.3 = (bf16[16,6272]{1,0:T(8,128)(2,1)S(1)}, bf16[16,6272]{1,0:T(8,128)(2,1)S(1)}, u32[]{:S(2)}, u32[]{:S(2)}) collective-permute-start(bf16[16,6272]{1,0:T(8,128)(2,1)S(1)} %collective-permute-done.refs_1_), channel_id=1, source_target_pairs={{0,1},{1,0},{2,3},{3,2},{4,5},{5,4},{6,7},{7,6},{8,9},{9,8},{10,11... | collective-permute-start | bytes 602120 | tf_op jit(solution)/shard_map/ppermute | solution.py:404
  22.2 6.4 %collective-permute-start.4 = (bf16[16,6272]{1,0:T(8,128)(2,1)S(1)}, bf16[16,6272]{1,0:T(8,128)(2,1)S(1)}, u32[]{:S(2)}, u32[]{:S(2)}) collective-permute-start(bf16[16,6272]{1,0:T(8,128)(2,1)S(1)} %collective-permute-done.1.refs_2_), channel_id=1, source_target_pairs={{0,1},{1,0},{2,3},{3,2},{4,5},{5,4},{6,7},{7,6},{8,9},{9,8},{10,11... | collective-permute-start | bytes 602120 | tf_op jit(solution)/shard_map/ppermute | solution.py:404
  22.7 5.9 %collective-permute-start.6 = (bf16[16,6272]{1,0:T(8,128)(2,1)S(1)}, bf16[16,6272]{1,0:T(8,128)(2,1)S(1)}, u32[]{:S(2)}, u32[]{:S(2)}) collective-permute-start(bf16[16,6272]{1,0:T(8,128)(2,1)S(1)} %collective-permute-done.2.refs_3_), channel_id=1, source_target_pairs={{0,4},{1,3},{2,0},{3,7},{4,8},{5,1},{6,2},{7,11},{8,12},{9,5},{10,... | collective-permute-start | bytes 602120 | tf_op jit(solution)/shard_map/ppermute | solution.py:401
  24.2 4.4 %collective-permute-start.5 = (bf16[16,6272]{1,0:T(8,128)(2,1)S(1)}, bf16[16,6272]{1,0:T(8,128)(2,1)S(1)}, u32[]{:S(2)}, u32[]{:S(2)}) collective-permute-start(bf16[16,6272]{1,0:T(8,128)(2,1)S(1)} %collective-permute-done.2.refs_3_), channel_id=1, source_target_pairs={{0,1},{1,0},{2,3},{3,2},{4,5},{5,4},{6,7},{7,6},{8,9},{9,8},{10,11... | collective-permute-start | bytes 602120 | tf_op jit(solution)/shard_map/ppermute | solution.py:404
  36.2 5.1 %collective-permute-start.15 = (bf16[48,4096]{1,0:T(8,128)(2,1)S(1)}, bf16[48,4096]{1,0:T(8,128)(2,1)S(1)}, u32[]{:S(2)}, u32[]{:S(2)}) collective-permute-start(bf16[48,4096]{1,0:T(8,128)(2,1)S(1)} %slice.50), channel_id=1, source_target_pairs={{0,1},{1,0},{2,3},{3,2},{4,5},{5,4},{6,7},{7,6},{8,9},{9,8},{10,11... | collective-permute-start | bytes 1179656 | tf_op jit(solution)/shard_map/ppermute | solution.py:404
  36.4 4.9 %collective-permute-start.14 = (bf16[16,4096]{1,0:T(8,128)(2,1)S(1)}, bf16[16,4096]{1,0:T(8,128)(2,1)S(1)}, u32[]{:S(2)}, u32[]{:S(2)}) collective-permute-start(bf16[16,4096]{1,0:T(8,128)(2,1)S(1)} %slice.48), channel_id=1, source_target_pairs={{0,4},{1,3},{2,0},{3,7},{4,8},{5,1},{6,2},{7,11},{8,12},{9,5},{10,... | collective-permute-start | bytes 393224 | tf_op jit(solution)/shard_map/ppermute | solution.py:401
  38.8 4.2 %collective-permute-start.20 = (bf16[16,4224]{1,0:T(8,128)(2,1)S(1)}, bf16[16,4224]{1,0:T(8,128)(2,1)S(1)}, u32[]{:S(2)}, u32[]{:S(2)}) collective-permute-start(bf16[16,4224]{1,0:T(8,128)(2,1)S(1)} %slice.56), channel_id=1, source_target_pairs={{0,4},{1,3},{2,0},{3,7},{4,8},{5,1},{6,2},{7,11},{8,12},{9,5},{10,... | collective-permute-start | bytes 405512 | tf_op jit(solution)/shard_map/ppermute | solution.py:401
  40.1 2.9 %collective-permute-start.21 = (bf16[48,4224]{1,0:T(8,128)(2,1)S(1)}, bf16[48,4224]{1,0:T(8,128)(2,1)S(1)}, u32[]{:S(2)}, u32[]{:S(2)}) collective-permute-start(bf16[48,4224]{1,0:T(8,128)(2,1)S(1)} %slice.58), channel_id=1, source_target_pairs={{0,1},{1,0},{2,3},{3,2},{4,5},{5,4},{6,7},{7,6},{8,9},{9,8},{10,11... | collective-permute-start | bytes 1216520 | tf_op jit(solution)/shard_map/ppermute | solution.py:404
  41.3 4.2 %collective-permute-start.16 = (bf16[16,4096]{1,0:T(8,128)(2,1)S(1)}, bf16[16,4096]{1,0:T(8,128)(2,1)S(1)}, u32[]{:S(2)}, u32[]{:S(2)}) collective-permute-start(bf16[16,4096]{1,0:T(8,128)(2,1)S(1)} %add_convert_fusion.5), channel_id=1, source_target_pairs={{0,4},{1,3},{2,0},{3,7},{4,8},{5,1},{6,2},{7,11},{8,12},{9,5},{10,... | collective-permute-start | bytes 393224 | tf_op jit(solution)/shard_map/ppermute | solution.py:401
  43.1 3.9 %collective-permute-start.22 = (bf16[16,4224]{1,0:T(8,128)(2,1)S(1)}, bf16[16,4224]{1,0:T(8,128)(2,1)S(1)}, u32[]{:S(2)}, u32[]{:S(2)}) collective-permute-start(bf16[16,4224]{1,0:T(8,128)(2,1)S(1)} %add_convert_fusion.2), channel_id=1, source_target_pairs={{0,4},{1,3},{2,0},{3,7},{4,8},{5,1},{6,2},{7,11},{8,12},{9,5},{10,... | collective-permute-start | bytes 405512 | tf_op jit(solution)/shard_map/ppermute | solution.py:401
  45.5 3.9 %collective-permute-start.17 = (bf16[16,4096]{1,0:T(8,128)(2,1)S(1)}, bf16[16,4096]{1,0:T(8,128)(2,1)S(1)}, u32[]{:S(2)}, u32[]{:S(2)}) collective-permute-start(bf16[16,4096]{1,0:T(8,128)(2,1)S(1)} %add_convert_fusion.4), channel_id=1, source_target_pairs={{0,4},{1,3},{2,0},{3,7},{4,8},{5,1},{6,2},{7,11},{8,12},{9,5},{10,... | collective-permute-start | bytes 393224 | tf_op jit(solution)/shard_map/ppermute | solution.py:401
  47.0 4.2 %collective-permute-start.23 = (bf16[16,4224]{1,0:T(8,128)(2,1)S(1)}, bf16[16,4224]{1,0:T(8,128)(2,1)S(1)}, u32[]{:S(2)}, u32[]{:S(2)}) collective-permute-start(bf16[16,4224]{1,0:T(8,128)(2,1)S(1)} %add_convert_fusion.1), channel_id=1, source_target_pairs={{0,4},{1,3},{2,0},{3,7},{4,8},{5,1},{6,2},{7,11},{8,12},{9,5},{10,... | collective-permute-start | bytes 405512 | tf_op jit(solution)/shard_map/ppermute | solution.py:401
  49.5 4.2 %collective-permute-start.18 = (bf16[16,4096]{1,0:T(8,128)(2,1)S(1)}, bf16[16,4096]{1,0:T(8,128)(2,1)S(1)}, u32[]{:S(2)}, u32[]{:S(2)}) collective-permute-start(bf16[16,4096]{1,0:T(8,128)(2,1)S(1)} %add_convert_fusion.3), channel_id=1, source_target_pairs={{0,4},{1,3},{2,0},{3,7},{4,8},{5,1},{6,2},{7,11},{8,12},{9,5},{10,... | collective-permute-start | bytes 393224 | tf_op jit(solution)/shard_map/ppermute | solution.py:401
  51.3 7.5 %collective-permute-start.24 = (bf16[16,4224]{1,0:T(8,128)(2,1)S(1)}, bf16[16,4224]{1,0:T(8,128)(2,1)S(1)}, u32[]{:S(2)}, u32[]{:S(2)}) collective-permute-start(bf16[16,4224]{1,0:T(8,128)(2,1)S(1)} %add_convert_fusion), channel_id=1, source_target_pairs={{0,4},{1,3},{2,0},{3,7},{4,8},{5,1},{6,2},{7,11},{8,12},{9,5},{10,... | collective-permute-start | bytes 405512 | tf_op jit(solution)/shard_map/ppermute | solution.py:401
  53.7 6.5 %collective-permute-start.19 = (f32[16,4096]{1,0:T(8,128)S(1)}, f32[16,4096]{1,0:T(8,128)S(1)}, u32[]{:S(2)}, u32[]{:S(2)}) collective-permute-start(f32[16,4096]{1,0:T(8,128)S(1)} %convert_add_fusion.1.mine_ref), channel_id=1, source_target_pairs={{0,1},{1,0},{2,3},{3,2},{4,5},{5,4},{6,7},{7,6},{8,9},{9,8},{10,11... | collective-permute-start | bytes 786440 | tf_op jit(solution)/shard_map/ppermute | solution.py:404
  58.8 3.3 %collective-permute-start.25 = (f32[16,4224]{1,0:T(8,128)S(1)}, f32[16,4224]{1,0:T(8,128)S(1)}, u32[]{:S(2)}, u32[]{:S(2)}) collective-permute-start(f32[16,4224]{1,0:T(8,128)S(1)} %convert_add_fusion.mine_ref), channel_id=1, source_target_pairs={{0,1},{1,0},{2,3},{3,2},{4,5},{5,4},{6,7},{7,6},{8,9},{9,8},{10,11... | collective-permute-start | bytes 811016 | tf_op jit(solution)/shard_map/ppermute | solution.py:404
  (4 other events, 26.4 us)
